TPU v7x, 256 devices: a whole 4x4x8 slice. The times are simulated.
256 devices in a mesh: seq: 32 (over y_lo, z, core), ulysses: 8 (over y_hi, x).
Axes of the slice: x: 4, y: 4 (y_hi: 2, y_lo: 2; y = y_hi * 2 + y_lo), z: 8, core: 2. Of those that a mesh axis runs over, the one named last changes fastest.
Arguments:
- queries: bfloat16 [8192, 3072], P(('seq', 'ulysses')), may hold values from -90 to 90
- keys_edit: bfloat16 [8192, 3072], P(('seq', 'ulysses')), may hold values from -6 to 6
- values_edit: bfloat16 [8192, 3072], P(('seq', 'ulysses')), may hold values from -6 to 6
- keys_source: bfloat16 [8192, 3072], P(('seq', 'ulysses')), may hold values from -6 to 6
- values_source: bfloat16 [8192, 3072], P(('seq', 'ulysses')), may hold values from -6 to 6
- edit_mask: int32 [8192], P('seq'), may hold values 0 or 1
- inject_gate: float32 [50, 24], replicated, may hold values from 0 to 0.9
- step_index: int32 [1], replicated, may hold values from 0 to 49
Outputs:
- attended: bfloat16 [8192, 3072], P(('seq', 'ulysses'))
All inputs are finite; a program needn't handle non-finite values. No bound on the sum of `edit_mask` on one device may be relied on, other than what follows from the above.
Results may differ from a plain program's by a relative error of at most 0.008.
Values may be sent and summed in bfloat16 or wider, within the bound.
No kernel may reach another device: no remote copies, remote signals or barrier semaphores. Data moves between devices by JAX's collectives and lax.ppermute only.
A program may use at most 128 MiB of HBM per device.

v0:
```python
import jax
import jax.numpy as jnp
from jax import lax
from jax.sharding import PartitionSpec as P


def mix_pair(edit, source, flags, strength):
    edit_f = edit.astype(jnp.float32)
    source_f = source.astype(jnp.float32)
    mixed = jnp.where(
        flags[:, None] == 1, edit_f, source_f + strength[None, :] * (edit_f - source_f)
    )
    return mixed.astype(jnp.bfloat16)


def fold_step(carry, piece, query_heads, head_count):
    run_max, run_sum, run_acc = carry
    key_piece, value_piece = piece
    rows = key_piece.shape[0]
    head_size = key_piece.shape[1] // head_count
    key_heads = key_piece.reshape(rows, head_count, head_size)
    value_heads = value_piece.reshape(rows, head_count, head_size)
    scores = jnp.einsum(
        "qhd,khd->hqk", query_heads, key_heads, preferred_element_type=jnp.float32
    ) * head_size ** (-0.5)
    new_max = jnp.maximum(run_max, jnp.max(scores, axis=-1))
    expo = jnp.exp(scores - new_max[:, :, None])
    run_sum = jnp.sum(expo, axis=-1)
    added = jnp.einsum(
        "hqk,khd->hqd", expo.astype(jnp.bfloat16), value_heads, preferred_element_type=jnp.float32
    )
    run_acc = added
    return (new_max, run_sum, run_acc)


def start_state(query_rows, head_count, head_size):
    run_max = jnp.full((head_count, query_rows), -1e30, jnp.float32)
    run_sum = jnp.zeros((head_count, query_rows), jnp.float32)
    run_acc = jnp.zeros((head_count, query_rows, head_size), jnp.float32)
    return (run_max, run_sum, run_acc)


def finish(state):
    run_max, run_sum, run_acc = state
    normed = run_acc / run_sum[:, :, None]
    head_count, query_rows, head_size = normed.shape
    return (
        normed.transpose(1, 0, 2).reshape(query_rows, head_count * head_size).astype(jnp.bfloat16)
    )


def attend_gathered(query_group, key_group, value_group, head_count):
    query_rows = query_group.shape[0]
    head_size = query_group.shape[1] // head_count
    query_heads = query_group.reshape(query_rows, head_count, head_size)
    state = fold_step(
        start_state(query_rows, head_count, head_size),
        (
            lax.all_gather(key_group, "seq", axis=0, tiled=True),
            lax.all_gather(value_group, "seq", axis=0, tiled=True),
        ),
        query_heads,
        head_count,
    )
    return finish(state)


def on_device(
    queries, keys_edit, values_edit, keys_source, values_source, edit_mask, inject_gate, step_index
):
    head_total = inject_gate.shape[1]
    head_size = queries.shape[1] // head_total
    group_count = lax.axis_size("ulysses")
    group_slot = lax.axis_index("ulysses")
    local_heads = head_total // group_count
    picked = (lax.iota(jnp.int32, inject_gate.shape[0]) == step_index[0]).astype(jnp.float32)
    head_gate = jnp.dot(picked, inject_gate, precision=lax.Precision.HIGHEST)
    query_group, kedit_group, vedit_group, ksource_group, vsource_group = (
        lax.all_to_all(queries, "ulysses", split_axis=1, concat_axis=0, tiled=True),
        lax.all_to_all(keys_edit, "ulysses", split_axis=1, concat_axis=0, tiled=True),
        lax.all_to_all(values_edit, "ulysses", split_axis=1, concat_axis=0, tiled=True),
        lax.all_to_all(keys_source, "ulysses", split_axis=1, concat_axis=0, tiled=True),
        lax.all_to_all(values_source, "ulysses", split_axis=1, concat_axis=0, tiled=True),
    )
    local_gate = lax.dynamic_slice_in_dim(head_gate, group_slot * local_heads, local_heads)
    strength = jnp.repeat(local_gate, head_size)
    key_group = mix_pair(kedit_group, ksource_group, edit_mask, strength)
    value_group = mix_pair(vedit_group, vsource_group, edit_mask, strength)
    result = attend_gathered(query_group, key_group, value_group, local_heads)
    return lax.all_to_all(result, "ulysses", split_axis=0, concat_axis=1, tiled=True)


def solution(mesh):
    in_specs = (
        P(("seq", "ulysses"), None),
        P(("seq", "ulysses"), None),
        P(("seq", "ulysses"), None),
        P(("seq", "ulysses"), None),
        P(("seq", "ulysses"), None),
        P("seq"),
        P(),
        P(),
    )
    out_specs = P(("seq", "ulysses"), None)
    return jax.shard_map(
        on_device, mesh=mesh, in_specs=in_specs, out_specs=out_specs, check_vma=False
    )
```

profile of v0, /device:TPU:1, one launch (start us, length us, event | category | flops | bytes accessed | tf_op | source)
XLA Modules:
  0.0 245.4 jit_solution(6490964626813764448)
XLA Ops:
  6.5 0.0 copy-start
  6.5 1.6 copy.66
  8.2 7.5 %all-to-all-start = ((bf16[32,8,384]{2,0,1:T(8,128)(2,1)}), bf16[32,8,384]{2,0,1:T(8,128)(2,1)S(1)}, u32[]{:S(2)}, u32[]{:S(2)}) async-start(bf16[32,8,384]{2,0,1:T(8,128)(2,1)} %bitcast.93), calls=%async_computation | async-start | bytes 393216 | tf_op jit(solution)/shard_map/all_to_all | solution.py:80
  15.7 1.6 copy.65
  17.3 5.7 %all-to-all-done = bf16[32,8,384]{2,0,1:T(8,128)(2,1)S(1)} async-done(((bf16[32,8,384]{2,0,1:T(8,128)(2,1)}), bf16[32,8,384]{2,0,1:T(8,128)(2,1)S(1)}, u32[]{:S(2)}, u32[]{:S(2)}) %all-to-all-start) | async-done | bytes 196640 | tf_op jit(solution)/shard_map/all_to_all | solution.py:80
  23.0 3.4 %all-to-all-start.1 = ((bf16[32,8,384]{2,0,1:T(8,128)(2,1)}), bf16[32,8,384]{2,0,1:T(8,128)(2,1)S(1)}, u32[]{:S(2)}, u32[]{:S(2)}) async-start(bf16[32,8,384]{2,0,1:T(8,128)(2,1)} %bitcast.92), calls=%async_computation.1 | async-start | bytes 393216 | tf_op jit(solution)/shard_map/all_to_all | solution.py:82
  27.1 1.6 copy.63
  28.7 1.6 copy.62
  30.3 0.0 copy-done
  30.3 0.1 convolution_bitcast_fusion
  30.4 0.1 dynamic_slice.3
  30.5 3.1 %all-to-all-done.1 = bf16[32,8,384]{2,0,1:T(8,128)(2,1)S(1)} async-done(((bf16[32,8,384]{2,0,1:T(8,128)(2,1)}), bf16[32,8,384]{2,0,1:T(8,128)(2,1)S(1)}, u32[]{:S(2)}, u32[]{:S(2)}) %all-to-all-start.1) | async-done | bytes 196640 | tf_op jit(solution)/shard_map/all_to_all | solution.py:82
  33.6 3.5 %all-to-all-start.3 = ((bf16[32,8,384]{2,0,1:T(8,128)(2,1)}), bf16[32,8,384]{2,0,1:T(8,128)(2,1)S(1)}, u32[]{:S(2)}, u32[]{:S(2)}) async-start(bf16[32,8,384]{2,0,1:T(8,128)(2,1)} %bitcast.90), calls=%async_computation.3 | async-start | bytes 393216 | tf_op jit(solution)/shard_map/all_to_all | solution.py:81
  37.1 0.1 broadcast_bitcast_fusion
  37.2 7.2 %all-to-all-done.3 = bf16[32,8,384]{2,0,1:T(8,128)(2,1)S(1)} async-done(((bf16[32,8,384]{2,0,1:T(8,128)(2,1)}), bf16[32,8,384]{2,0,1:T(8,128)(2,1)S(1)}, u32[]{:S(2)}, u32[]{:S(2)}) %all-to-all-start.3) | async-done | bytes 196640 | tf_op jit(solution)/shard_map/all_to_all | solution.py:81
  44.4 3.4 %all-to-all-start.4 = ((bf16[32,8,384]{2,0,1:T(8,128)(2,1)}), bf16[32,8,384]{2,0,1:T(8,128)(2,1)S(1)}, u32[]{:S(2)}, u32[]{:S(2)}) async-start(bf16[32,8,384]{2,0,1:T(8,128)(2,1)} %bitcast.89), calls=%async_computation.4 | async-start | bytes 393216 | tf_op jit(solution)/shard_map/all_to_all | solution.py:83
  47.8 0.0 all-gather.3.cloned.1.call-start
  47.8 0.7 broadcast_compare_fusion
  48.5 6.5 %all-to-all-done.4 = bf16[32,8,384]{2,0,1:T(8,128)(2,1)S(1)} async-done(((bf16[32,8,384]{2,0,1:T(8,128)(2,1)}), bf16[32,8,384]{2,0,1:T(8,128)(2,1)S(1)}, u32[]{:S(2)}, u32[]{:S(2)}) %all-to-all-start.4) | async-done | bytes 196640 | tf_op jit(solution)/shard_map/all_to_all | solution.py:83
  55.0 1.0 fusion.21
  56.0 0.0 all-gather.3.cloned.1.call-update
  56.0 0.0 all-gather.5.cloned.1.call-start
  56.1 0.7 all-gather.5.cloned.1.call-update
  56.8 0.9 copy.64
  57.7 9.7 %all_to_all.84 = bf16[32,8,384]{2,0,1:T(8,128)(2,1)S(1)} all-to-all(bf16[32,8,384]{2,0,1:T(8,128)(2,1)S(1)} %bitcast.99), channel_id=1, replica_groups=mesh['seq'=32,'ulysses'=8] {'ulysses'}, dimensions={1} | all-to-all | bytes 393216 | tf_op jit(solution)/shard_map/all_to_all | solution.py:79
  67.4 0.1 reshape.47
  67.5 62.8 %all-gather.3.cloned.1.call-done = bf16[8192,384]{1,0:T(8,128)(2,1)} async-done(((bf16[256,384]{1,0:T(8,128)(2,1)}), bf16[8192,384]{1,0:T(8,128)(2,1)}) %all-gather.3.cloned.1.call-update) | async-done | bytes 6291472 | tf_op jit(solution)/shard_map/all_gather | solution.py:59
  130.2 8.6 %copy.33 = bf16[8192,384]{0,1:T(8,128)(2,1)} copy(bf16[8192,384]{1,0:T(8,128)(2,1)} %all-gather.3.cloned.1.call-done) | data formatting | bytes 12582912 | tf_op jit(solution)/shard_map/all_gather | solution.py:59
  138.9 14.9 %bitcast_reduce_fusion = (f32[3,256]{1,0:T(4,128)S(1)}, f32[3,8192,256]{2,1,0:T(8,128)}) fusion(bf16[8192,3,128]{0,2,1:T(8,128)(2,1)} %bitcast.95, bf16[256,3,128]{2,1,0:T(4,128)(2,1)S(1)} %reshape.47), kind=kOutput, calls=%fused_computation.1 | convolution fusion | flops 1623194880 | bytes 31656960 | tf_op jit(solution)/shard_map/qhd,khd->hqk/dot_general | solution.py:23
  153.8 11.8 %fusion.1 = f32[3,256]{1,0:T(4,128)S(1)} fusion(f32[3,8192,256]{2,1,0:T(8,128)} %get-tuple-element.8, f32[3,256]{1,0:T(4,128)S(1)} %broadcast_maximum_fusion), kind=kLoop, calls=%fused_computation.3 | loop fusion | flops 18873600 | bytes 25171968 | tf_op jit(solution)/shard_map/reduce_sum | solution.py:28
  165.6 36.6 %all-gather.5.cloned.1.call-done = bf16[8192,384]{1,0:T(8,128)(2,1)} async-done(((bf16[256,384]{1,0:T(8,128)(2,1)}), bf16[8192,384]{1,0:T(8,128)(2,1)}) %all-gather.5.cloned.1.call-update) | async-done | bytes 6291472 | tf_op jit(solution)/shard_map/all_gather | solution.py:60
  202.1 8.6 %copy.39 = bf16[8192,384]{0,1:T(8,128)(2,1)} copy(bf16[8192,384]{1,0:T(8,128)(2,1)} %all-gather.5.cloned.1.call-done) | data formatting | bytes 12582912 | tf_op jit(solution)/shard_map/all_gather | solution.py:60
  210.7 13.2 %fusion.13 = bf16[256,3,128]{2,0,1:T(8,128)(2,1)S(1)} fusion(bf16[8192,3,128]{0,2,1:T(8,128)(2,1)} %bitcast.96, f32[3,8192,256]{2,1,0:T(8,128)} %get-tuple-element.8, f32[3,256]{1,0:T(4,128)S(1)} %broadcast_maximum_fusion, f32[256,3]{0,1:T(4,128)S(1)} %bitcast.105), kind=kOutput, calls=%fused_computation.11 | convolution fusion | flops 1629683712 | bytes 31660032 | tf_op jit(solution)/shard_map/hqk,khd->hqd/dot_general | solution.py:29
  223.9 0.2 copy.42
  224.1 0.2 convert_element_type.69
  224.3 13.6 %all_to_all.85 = bf16[8,32,384]{2,1,0:T(8,128)(2,1)S(1)} all-to-all(bf16[8,32,384]{2,1,0:T(8,128)(2,1)S(1)} %convert_element_type.69), channel_id=1, replica_groups=mesh['seq'=32,'ulysses'=8] {'ulysses'}, dimensions={0} | all-to-all | bytes 393216 | tf_op jit(solution)/shard_map/all_to_all | solution.py:90
  237.8 0.7 copy.52
  (1 shorter events, 0.0 us)
Async XLA Ops:
  6.5 23.8 %copy-start = (f32[50,24]{0,1:T(8,128)S(1)}, f32[50,24]{0,1:T(8,128)}, u32[]{:S(2)}) copy-start(f32[50,24]{0,1:T(8,128)} %param.14) | copy-start | bytes 14404
  8.2 14.8 %all-to-all-start = ((bf16[32,8,384]{2,0,1:T(8,128)(2,1)}), bf16[32,8,384]{2,0,1:T(8,128)(2,1)S(1)}, u32[]{:S(2)}, u32[]{:S(2)}) async-start(bf16[32,8,384]{2,0,1:T(8,128)(2,1)} %bitcast.93), calls=%async_computation | async-start | bytes 393216 | tf_op jit(solution)/shard_map/all_to_all | solution.py:80
  23.0 10.6 %all-to-all-start.1 = ((bf16[32,8,384]{2,0,1:T(8,128)(2,1)}), bf16[32,8,384]{2,0,1:T(8,128)(2,1)S(1)}, u32[]{:S(2)}, u32[]{:S(2)}) async-start(bf16[32,8,384]{2,0,1:T(8,128)(2,1)} %bitcast.92), calls=%async_computation.1 | async-start | bytes 393216 | tf_op jit(solution)/shard_map/all_to_all | solution.py:82
  33.6 10.8 %all-to-all-start.3 = ((bf16[32,8,384]{2,0,1:T(8,128)(2,1)}), bf16[32,8,384]{2,0,1:T(8,128)(2,1)S(1)}, u32[]{:S(2)}, u32[]{:S(2)}) async-start(bf16[32,8,384]{2,0,1:T(8,128)(2,1)} %bitcast.90), calls=%async_computation.3 | async-start | bytes 393216 | tf_op jit(solution)/shard_map/all_to_all | solution.py:81
  44.4 10.6 %all-to-all-start.4 = ((bf16[32,8,384]{2,0,1:T(8,128)(2,1)}), bf16[32,8,384]{2,0,1:T(8,128)(2,1)S(1)}, u32[]{:S(2)}, u32[]{:S(2)}) async-start(bf16[32,8,384]{2,0,1:T(8,128)(2,1)} %bitcast.89), calls=%async_computation.4 | async-start | bytes 393216 | tf_op jit(solution)/shard_map/all_to_all | solution.py:83
  47.8 82.4 %all-gather.3.cloned.1.call-start = ((), (), s32[]{:S(2)}) async-start(), calls=%async_computation.6 | async-start | bytes 6488064 | tf_op jit(solution)/shard_map/all_gather | solution.py:59
  56.0 146.1 %all-gather.5.cloned.1.call-start = ((), (), s32[]{:S(2)}) async-start(), calls=%async_computation.7 | async-start | bytes 6488064 | tf_op jit(solution)/shard_map/all_gather | solution.py:60
Sparse Core Ops, SparseCore 0:
  56.1 74.0 all-gather.2
  132.1 69.9 all-gather.4
where the time goes:
time: 247 us; the launch traced here: 245 us
  waiting for transfers between devices  123 us (50%)
  matrix products  28.2 us (11%)
  local copies, waits for them, and re-layouts  25.9 us (10%)
  blocking collectives  23.2 us (9%)
  starting transfers between devices  17.8 us (7%)
  between operations  14.1 us (6%)
  other arithmetic  13.4 us (5%)
    all_gather x1, waiting for transfers between devices, attend_gathered(): lax.all_gather(key_group, 'seq', axis=0, tiled=True)  62.8 us
    all_gather x1, waiting for transfers between devices, attend_gathered(): lax.all_gather(value_group, 'seq', axis=0, tiled=True)  36.6 us
    dot_general x1, matrix products, fold_step(): jnp.einsum('qhd,khd->hqk', query_heads, key_heads, preferred_element_type...  14.9 us
    all_to_all x1, blocking collectives, on_device(): lax.all_to_all(result, 'ulysses', split_axis=0, concat_axis=1, tiled=True)  13.6 us
    dot_general x1, matrix products, fold_step(): jnp.einsum('hqk,khd->hqd', expo.astype(jnp.bfloat16), value_heads, prefer...  13.2 us
    reduce_sum x1, other arithmetic, fold_step(): run_sum = jnp.sum(expo, axis=-1)  11.8 us
    all_to_all x1, blocking collectives, on_device(): lax.all_to_all(queries, 'ulysses', split_axis=1, concat_axis=0, tiled=True)  9.69 us
    all_gather x1, local copies, waits for them, and re-layouts, attend_gathered(): lax.all_gather(key_group, 'seq', axis=0, tiled=True)  8.62 us
  transfers between devices with their start and end apart: 6, of which 6 were waited for; matrix products, arithmetic and copies ran while one was open for 17% of the time, Pallas kernels for 0%

commit v1 on v0

v1 whole, which is shorter than its diff:
```python
import functools

import jax
import jax.numpy as jnp
from jax import lax
from jax.experimental import pallas as pl
from jax.experimental.pallas import tpu as pltpu
from jax.sharding import PartitionSpec as P

NX, NY, NZ = 4, 4, 8
HEAD = 128
TOK = 32
GROUP_HEADS = 6
CHUNKS = 1
WIDTH = GROUP_HEADS * HEAD // CHUNKS
CH_HEADS = GROUP_HEADS // CHUNKS
LOG2E = 1.4426950408889634
SCALE2 = HEAD**-0.5 * LOG2E
VMEM = 48 * 1024 * 1024


def coords(index):
    seq, uly = divmod(index, 8)
    core = seq % 2
    z = (seq // 2) % NZ
    y = 2 * (uly // NX) + seq // (2 * NZ)
    return uly % NX, y, z, core


def index_of(x, y, z, core):
    return (((y % 2) * NZ + z) * 2 + core) * 8 + (y // 2) * NX + x


def permute(value, move):
    pairs = [(i, index_of(*move(*coords(i)))) for i in range(2 * NX * NY * NZ)]
    return lax.ppermute(value, ("seq", "ulysses"), pairs)


def shift_x(value, d):
    return permute(value, lambda x, y, z, c: ((x + d) % NX, y, z, c))


def shift_y(value, d):
    return permute(value, lambda x, y, z, c: (x, (y + d) % NY, z, c))


def ring_z(value):
    return permute(value, lambda x, y, z, c: (x, y, (z + 1 - 2 * c) % NZ, c))


def swap_core(value):
    return permute(value, lambda x, y, z, c: (x, y, z, 1 - c))


def cost(flops, nbytes, trans=0):
    return pl.CostEstimate(flops=int(flops), bytes_accessed=int(nbytes), transcendentals=int(trans))


def params():
    return pltpu.CompilerParams(vmem_limit_bytes=VMEM)


def mix_kernel(where_ref, step_ref, q_ref, ke_ref, ve_ref, ks_ref, vs_ref, mask_ref, gate_ref, *outs):
    y, u = where_ref[0], where_ref[1]
    lane = lax.broadcasted_iota(jnp.int32, (TOK, 256), 1)
    row = lax.broadcasted_iota(jnp.int32, (TOK, 256), 0)
    picked = jnp.where(lane == u * TOK + row, jnp.broadcast_to(mask_ref[...], (TOK, 256)), 0)
    inside = jnp.sum(picked, axis=1, keepdims=True) == 1
    gates = gate_ref[pl.ds(step_ref[0], 1), :]
    head_lane = lax.broadcasted_iota(jnp.int32, gates.shape, 1)
    for d in range(NY):
        group = lax.rem(y + d, NY)
        for c in range(CHUNKS):
            out = outs[c * NY + d]
            for h in range(CH_HEADS):
                head = group * GROUP_HEADS + c * CH_HEADS + h
                strength = jnp.sum(jnp.where(head_lane == head, gates, 0.0), axis=1, keepdims=True)
                cols = pl.ds(pl.multiple_of(head * HEAD, HEAD), HEAD)
                to = slice(h * HEAD, (h + 1) * HEAD)
                for n, (edit, source) in enumerate(((ke_ref, ks_ref), (ve_ref, vs_ref))):
                    e = edit[:, cols].astype(jnp.float32)
                    s = source[:, cols].astype(jnp.float32)
                    mixed = jnp.where(inside, e, s + strength * (e - s))
                    out[n * TOK : (n + 1) * TOK, to] = mixed.astype(jnp.bfloat16)
                out[2 * TOK : 3 * TOK, to] = q_ref[:, cols]


def mix(where, step_index, queries, ke, ve, ks, vs, edit_mask, gate):
    vmem = pl.BlockSpec(memory_space=pltpu.VMEM)
    smem = pl.BlockSpec(memory_space=pltpu.SMEM)
    return pl.pallas_call(
        mix_kernel,
        out_shape=[jax.ShapeDtypeStruct((3 * TOK, WIDTH), jnp.bfloat16)] * (NY * CHUNKS),
        in_specs=[smem, smem] + [vmem] * 7,
        out_specs=[vmem] * (NY * CHUNKS),
        compiler_params=params(),
        cost_estimate=cost(1e6, 2e6),
        name="mix",
    )(where, step_index, queries, ke, ve, ks, vs, edit_mask.reshape(1, -1), gate)


def flash_kernel(first, last, blocks, *refs):
    refs = list(refs)
    q_refs, refs = refs[:NX], refs[NX:]
    kv_refs, refs = refs[:blocks], refs[blocks:]
    if not first:
        acc_in, ml_in, refs = refs[0], refs[1], refs[2:]
    rows = q_refs[0].shape[0]
    half = kv_refs[0].shape[0] // 2
    keys = jnp.concatenate([r[:half, :] for r in kv_refs], axis=0)
    values = jnp.concatenate([r[half:, :] for r in kv_refs], axis=0)
    span = 2 * rows
    for part in range(NX // 2):
        at = slice(part * span, (part + 1) * span)
        q = jnp.concatenate([q_refs[2 * part][...], q_refs[2 * part + 1][...]], axis=0)
        s = lax.dot_general(keys, q, (((1,), (1,)), ((), ())), preferred_element_type=jnp.float32)
        top = jnp.max(s, axis=0, keepdims=True)
        if not first:
            old = ml_in[0:1, at]
            top = jnp.maximum(top, old)
        p = jnp.exp2((s - top) * SCALE2)
        total = jnp.sum(p, axis=0, keepdims=True)
        o = lax.dot_general(
            values, p.astype(jnp.bfloat16), (((0,), (0,)), ((), ())), preferred_element_type=jnp.float32
        )
        if not first:
            alpha = jnp.exp2((old - top) * SCALE2)
            total = total + alpha * ml_in[1:2, at]
            o = o + alpha * acc_in[:, at]
        if last:
            o = o / total
            lse = top * SCALE2 + jnp.log2(total)
            hi = lse.astype(jnp.bfloat16).astype(jnp.float32)
            mid = (lse - hi).astype(jnp.bfloat16).astype(jnp.float32)
            low = lse - hi - mid
            r = lax.broadcasted_iota(jnp.int32, (16, span), 0)
            tail = jnp.where(r == 0, hi, jnp.where(r == 1, mid, jnp.where(r == 2, low, 0.0)))
            for i in range(2):
                out = refs[2 * part + i]
                cut = slice(i * rows, (i + 1) * rows)
                out[:HEAD, :] = o[:, cut].astype(jnp.bfloat16)
                out[HEAD:, :] = tail[:, cut].astype(jnp.bfloat16)
        else:
            refs[0][:, at] = o
            refs[1][0:1, at] = top
            refs[1][1:2, at] = total


def flash(q_parts, kv_blocks, state, last):
    rows = q_parts[0].shape[0]
    width = q_parts[0].shape[1]
    heads = width // HEAD
    queries = NX * rows
    first = state is None
    col = lambda n: pl.BlockSpec((n, HEAD), lambda h: (0, h))
    state_specs = [
        pl.BlockSpec((HEAD, queries), lambda h: (h, 0)),
        pl.BlockSpec((8, queries), lambda h: (h, 0)),
    ]
    in_specs = [col(rows)] * NX + [col(b.shape[0]) for b in kv_blocks]
    if last:
        out_shape = [jax.ShapeDtypeStruct((HEAD + 16, heads * rows), jnp.bfloat16)] * NX
        out_specs = [pl.BlockSpec((HEAD + 16, rows), lambda h: (0, h))] * NX
    else:
        out_shape = [
            jax.ShapeDtypeStruct((heads * HEAD, queries), jnp.float32),
            jax.ShapeDtypeStruct((heads * 8, queries), jnp.float32),
        ]
        out_specs = state_specs
    n = sum(b.shape[0] // 2 for b in kv_blocks)
    return pl.pallas_call(
        functools.partial(flash_kernel, first, last, len(kv_blocks)),
        grid=(heads,),
        out_shape=out_shape,
        in_specs=in_specs + ([] if first else state_specs),
        out_specs=out_specs,
        compiler_params=params(),
        cost_estimate=cost(4 * heads * queries * n * HEAD * 2, 4e6, heads * queries * n),
        name="flash",
    )(*q_parts, *kv_blocks, *(state or ()))


def merge_kernel(*refs):
    msgs, outs = refs[:NX], refs[NX:]
    lse = [jnp.sum(m[HEAD : HEAD + 16, :].astype(jnp.float32), axis=0, keepdims=True) for m in msgs]
    top = functools.reduce(jnp.maximum, lse)
    weight = [jnp.exp2(v - top) for v in lse]
    scale = 1.0 / functools.reduce(jnp.add, weight)
    o = functools.reduce(
        jnp.add, [(w * scale) * m[:HEAD, :].astype(jnp.float32) for w, m in zip(weight, msgs)]
    )
    o = o.T.astype(jnp.bfloat16)
    for i, out in enumerate(outs):
        out[...] = o[i * TOK : (i + 1) * TOK, :]


def merge(msgs):
    heads = msgs[0].shape[1] // HEAD
    return pl.pallas_call(
        merge_kernel,
        grid=(heads,),
        out_shape=[jax.ShapeDtypeStruct((TOK, heads * HEAD), jnp.bfloat16)] * NY,
        in_specs=[pl.BlockSpec((HEAD + 16, HEAD), lambda h: (0, h))] * NX,
        out_specs=[pl.BlockSpec((TOK, HEAD), lambda h: (0, h))] * NY,
        compiler_params=params(),
        cost_estimate=cost(1e6, 1e6),
        name="merge",
    )(*msgs)


def assemble_kernel(where_ref, *refs):
    out = refs[-1]
    for d in range(NY):
        group = lax.rem(where_ref[0] + d, NY)
        for c in range(CHUNKS):
            at = group * (GROUP_HEADS * HEAD) + c * WIDTH
            out[:, pl.ds(pl.multiple_of(at, HEAD), WIDTH)] = refs[c * NY + d][...]


def assemble(where, pieces):
    vmem = pl.BlockSpec(memory_space=pltpu.VMEM)
    return pl.pallas_call(
        assemble_kernel,
        out_shape=jax.ShapeDtypeStruct((TOK, NY * GROUP_HEADS * HEAD), jnp.bfloat16),
        in_specs=[pl.BlockSpec(memory_space=pltpu.SMEM)] + [vmem] * len(pieces),
        out_specs=vmem,
        compiler_params=params(),
        cost_estimate=cost(1e5, 4e5),
        name="assemble",
    )(where, *pieces)


def on_device(
    queries, keys_edit, values_edit, keys_source, values_source, edit_mask, inject_gate, step_index
):
    seq, uly = lax.axis_index("seq"), lax.axis_index("ulysses")
    y = 2 * (uly // NX) + seq // (2 * NZ)
    where = jnp.stack([y, uly]).astype(jnp.int32)
    sent = mix(
        where, step_index, queries, keys_edit, values_edit, keys_source, values_source, edit_mask, inject_gate
    )
    pieces = [None] * (CHUNKS * NY)
    for c in range(CHUNKS):
        mine = sent[c * NY : (c + 1) * NY]
        got = [mine[0]] + [shift_y(mine[d], d) for d in range(1, NY)]
        own = jnp.concatenate([g[:TOK] for g in got] + [g[TOK : 2 * TOK] for g in got], axis=0)
        query = jnp.concatenate([g[2 * TOK :] for g in got], axis=0)
        one, two = own, swap_core(own)
        q_parts = [query] + [shift_x(query, d) for d in range(1, NX)]
        state = flash(q_parts, [one, two], None, False)
        for step in range(3):
            one, two = ring_z(one), ring_z(two)
            state = flash(q_parts, [one, two, swap_core(one), swap_core(two)], state, False)
        one = ring_z(one)
        msgs = flash(q_parts, [one, swap_core(one)], state, True)
        back = [msgs[0]] + [shift_x(msgs[d], -d) for d in range(1, NX)]
        merged = merge(back)
        for d in range(NY):
            pieces[c * NY + d] = merged[0] if d == 0 else shift_y(merged[d], -d)
    return assemble(where, pieces)


def solution(mesh):
    in_specs = (
        P(("seq", "ulysses"), None),
        P(("seq", "ulysses"), None),
        P(("seq", "ulysses"), None),
        P(("seq", "ulysses"), None),
        P(("seq", "ulysses"), None),
        P("seq"),
        P(),
        P(),
    )
    out_specs = P(("seq", "ulysses"), None)
    return jax.shard_map(
        on_device, mesh=mesh, in_specs=in_specs, out_specs=out_specs, check_vma=False
    )
```

time: 247 us -> 117 us (0.47)
  waiting for transfers between devices: 123 us -> 39.3 us
  Pallas kernels: 0 us -> 32.5 us
  matrix products: 28.2 us -> 0 us
  blocking collectives: 23.2 us -> 0 us
  local copies, waits for them, and re-layouts: 25.9 us -> 6.16 us
  starting transfers between devices: 17.8 us -> 37.5 us
  other arithmetic: 13.4 us -> 0.09 us
  between operations: 14.1 us -> 0.86 us
    all_gather x2 -> x0, waiting for transfers between devices: 99.3 us -> none  [the longest x1 62.8 us: attend_gathered(): lax.all_gather(key_group, 'seq', axis=0, tiled=True)]
    ppermute x0 -> x27, waiting for transfers between devices: none -> 39.3 us  [permute(): return lax.ppermute(value, ('seq', 'ulysses'), pairs)]
    ppermute x0 -> x27, starting transfers between devices: none -> 37.5 us  [permute(): return lax.ppermute(value, ('seq', 'ulysses'), pairs)]
    pallas_call x0 -> x8, Pallas kernels: none -> 32.5 us  [the longest x5 29.2 us: flash(): pl.pallas_call(functools.partial(flash_kernel, first, last, len(kv_blocks...]
    dot_general x3 -> x0, matrix products: 28.2 us -> none  [the longest x1 14.9 us: fold_step(): jnp.einsum('qhd,khd->hqk', query_heads, key_heads, preferred_element_type...]
    all_to_all x2 -> x0, blocking collectives: 23.2 us -> none  [the longest x1 13.6 us: on_device(): lax.all_to_all(result, 'ulysses', split_axis=0, concat_axis=1, tiled=True)]
    all_to_all x4 -> x0, waiting for transfers between devices: 22.6 us -> none  [the longest x1 7.22 us: on_device(): lax.all_to_all(values_edit, 'ulysses', split_axis=1, concat_axis=0, tiled...]
    all_to_all x4 -> x0, starting transfers between devices: 17.7 us -> none  [the longest x1 7.48 us: on_device(): lax.all_to_all(keys_edit, 'ulysses', split_axis=1, concat_axis=0, tiled=T...]
  transfers between devices with their start and end apart: 6 -> 27, of which waited for: 6 -> 13; matrix products, arithmetic and copies ran while one was open for 17% -> 0% of each run, Pallas kernels for 0% -> 21%
where the time goes in v1:
time: 117 us; the launch traced here: 116 us
  waiting for transfers between devices  39.3 us (34%)
  starting transfers between devices  37.5 us (32%)
  Pallas kernels  32.5 us (28%)
  local copies, waits for them, and re-layouts  6.16 us (5%)
    ppermute x27, waiting for transfers between devices, permute(): return lax.ppermute(value, ('seq', 'ulysses'), pairs)  39.3 us
    ppermute x27, starting transfers between devices, permute(): return lax.ppermute(value, ('seq', 'ulysses'), pairs)  37.5 us
    pallas_call x5, Pallas kernels, flash(): pl.pallas_call(functools.partial(flash_kernel, first, last, len(kv_blocks...  29.2 us
    unnamed x20, local copies, waits for them, and re-layouts  6.15 us
  transfers between devices with their start and end apart: 27, of which 13 were waited for; matrix products, arithmetic and copies ran while one was open for 0% of the time, Pallas kernels for 21%

profile of v1, /device:TPU:1, one launch (start us, length us, event | category | flops | bytes accessed | tf_op | source)
XLA Modules:
  0.0 116.4 jit_solution(13088328439003342321)
XLA Ops:
  0.0 0.8 copy.9.gate_ref
  1.5 0.1 pad_add_fusion.where_ref
  1.5 0.9 copy-done
  2.5 0.9 copy-done.1
  3.4 0.9 copy-done.2
  4.3 0.9 copy-done.3
  5.3 0.9 copy-done.4
  6.2 0.7 copy-done.5
  6.9 0.9 mix.1
  7.8 2.2 %collective-permute-start = (bf16[96,768]{1,0:T(8,128)(2,1)S(1)}, bf16[96,768]{1,0:T(8,128)(2,1)S(1)}, u32[]{:S(2)}, u32[]{:S(2)}) collective-permute-start(bf16[96,768]{1,0:T(8,128)(2,1)S(1)} %get-tuple-element.26), channel_id=1, source_target_pairs={{0,128},{1,129},{2,130},{3,131},{4,132},{5,133},{6,134},{7,135},{8... | collective-permute-start | bytes 442376 | tf_op jit(solution)/shard_map/ppermute | solution.py:36
  10.0 2.6 %collective-permute-start.1 = (bf16[96,768]{1,0:T(8,128)(2,1)S(1)}, bf16[96,768]{1,0:T(8,128)(2,1)S(1)}, u32[]{:S(2)}, u32[]{:S(2)}) collective-permute-start(bf16[96,768]{1,0:T(8,128)(2,1)S(1)} %get-tuple-element.27), channel_id=1, source_target_pairs={{0,4},{1,5},{2,6},{3,7},{4,0},{5,1},{6,2},{7,3},{8,12},{9,13},{10,... | collective-permute-start | bytes 442376 | tf_op jit(solution)/shard_map/ppermute | solution.py:36
  12.6 1.1 collective-permute-start.2
  13.7 0.3 collective-permute-done
  14.0 5.1 %collective-permute-done.1 = bf16[96,768]{1,0:T(8,128)(2,1)S(1)} collective-permute-done((bf16[96,768]{1,0:T(8,128)(2,1)S(1)}, bf16[96,768]{1,0:T(8,128)(2,1)S(1)}, u32[]{:S(2)}, u32[]{:S(2)}) %collective-permute-start.1) | collective-permute-done | bytes 147488 | tf_op jit(solution)/shard_map/ppermute | solution.py:36
  19.0 0.0 collective-permute-done.2
  19.1 1.7 %collective-permute-start.11 = (bf16[256,768]{1,0:T(8,128)(2,1)S(1)}, bf16[256,768]{1,0:T(8,128)(2,1)S(1)}, u32[]{:S(2)}, u32[]{:S(2)}) collective-permute-start(bf16[256,768]{1,0:T(8,128)(2,1)S(1)} %get-tuple-element.45.refs_4_), channel_id=1, source_target_pairs={{0,8},{1,9},{2,10},{3,11},{4,12},{5,13},{6,14},{7,15},{8,0},{9,1},... | collective-permute-start | bytes 1179656 | tf_op jit(solution)/shard_map/ppermute | solution.py:36
  20.8 5.5 %collective-permute-start.6 = (bf16[256,768]{1,0:T(8,128)(2,1)S(1)}, bf16[256,768]{1,0:T(8,128)(2,1)S(1)}, u32[]{:S(2)}, u32[]{:S(2)}) collective-permute-start(bf16[256,768]{1,0:T(8,128)(2,1)S(1)} %get-tuple-element.45.refs_4_), channel_id=1, source_target_pairs={{0,16},{1,17},{2,18},{3,19},{4,20},{5,21},{6,22},{7,23},{8,120},{9... | collective-permute-start | bytes 1179656 | tf_op jit(solution)/shard_map/ppermute | solution.py:36
  26.3 0.0 collective-permute-done.11.refs_5_
  26.3 1.3 %collective-permute-start.12 = (bf16[256,768]{1,0:T(8,128)(2,1)S(1)}, bf16[256,768]{1,0:T(8,128)(2,1)S(1)}, u32[]{:S(2)}, u32[]{:S(2)}) collective-permute-start(bf16[256,768]{1,0:T(8,128)(2,1)S(1)} %collective-permute-done.11.refs_5_), channel_id=1, source_target_pairs={{0,16},{1,17},{2,18},{3,19},{4,20},{5,21},{6,22},{7,23},{8,120},{9... | collective-permute-start | bytes 1179656 | tf_op jit(solution)/shard_map/ppermute | solution.py:36
  27.7 3.4 %collective-permute-done.6.refs_4_ = bf16[256,768]{1,0:T(8,128)(2,1)S(1)} collective-permute-done((bf16[256,768]{1,0:T(8,128)(2,1)S(1)}, bf16[256,768]{1,0:T(8,128)(2,1)S(1)}, u32[]{:S(2)}, u32[]{:S(2)}) %collective-permute-start.6) | collective-permute-done | bytes 393248 | tf_op jit(solution)/shard_map/ppermute | solution.py:36
  31.1 3.1 %collective-permute-start.7 = (bf16[256,768]{1,0:T(8,128)(2,1)S(1)}, bf16[256,768]{1,0:T(8,128)(2,1)S(1)}, u32[]{:S(2)}, u32[]{:S(2)}) collective-permute-start(bf16[256,768]{1,0:T(8,128)(2,1)S(1)} %collective-permute-done.6.refs_4_), channel_id=1, source_target_pairs={{0,16},{1,17},{2,18},{3,19},{4,20},{5,21},{6,22},{7,23},{8,120},{9... | collective-permute-start | bytes 1179656 | tf_op jit(solution)/shard_map/ppermute | solution.py:36
  34.2 1.1 collective-permute-done.12.refs_5_
  35.3 3.1 %collective-permute-start.13 = (bf16[256,768]{1,0:T(8,128)(2,1)S(1)}, bf16[256,768]{1,0:T(8,128)(2,1)S(1)}, u32[]{:S(2)}, u32[]{:S(2)}) collective-permute-start(bf16[256,768]{1,0:T(8,128)(2,1)S(1)} %collective-permute-done.12.refs_5_), channel_id=1, source_target_pairs={{0,16},{1,17},{2,18},{3,19},{4,20},{5,21},{6,22},{7,23},{8,120},{9... | collective-permute-start | bytes 1179656 | tf_op jit(solution)/shard_map/ppermute | solution.py:36
  38.4 1.1 collective-permute-done.7.refs_4_
  39.5 3.1 %collective-permute-start.8 = (bf16[256,768]{1,0:T(8,128)(2,1)S(1)}, bf16[256,768]{1,0:T(8,128)(2,1)S(1)}, u32[]{:S(2)}, u32[]{:S(2)}) collective-permute-start(bf16[256,768]{1,0:T(8,128)(2,1)S(1)} %collective-permute-done.7.refs_4_), channel_id=1, source_target_pairs={{0,16},{1,17},{2,18},{3,19},{4,20},{5,21},{6,22},{7,23},{8,120},{9... | collective-permute-start | bytes 1179656 | tf_op jit(solution)/shard_map/ppermute | solution.py:36
  42.6 1.3 %collective-permute-start.3 = (bf16[128,768]{1,0:T(8,128)(2,1)S(1)}, bf16[128,768]{1,0:T(8,128)(2,1)S(1)}, u32[]{:S(2)}, u32[]{:S(2)}) collective-permute-start(bf16[128,768]{1,0:T(8,128)(2,1)S(1)} %pad_maximum_fusion.refs_0_), channel_id=1, source_target_pairs={{0,1},{1,2},{2,3},{3,0},{4,5},{5,6},{6,7},{7,4},{8,9},{9,10},{10,1... | collective-permute-start | bytes 589832 | tf_op jit(solution)/shard_map/ppermute | solution.py:36
  43.9 2.5 %collective-permute-start.4 = (bf16[128,768]{1,0:T(8,128)(2,1)S(1)}, bf16[128,768]{1,0:T(8,128)(2,1)S(1)}, u32[]{:S(2)}, u32[]{:S(2)}) collective-permute-start(bf16[128,768]{1,0:T(8,128)(2,1)S(1)} %pad_maximum_fusion.refs_0_), channel_id=1, source_target_pairs={{0,2},{1,3},{2,0},{3,1},{4,6},{5,7},{6,4},{7,5},{8,10},{9,11},{10,... | collective-permute-start | bytes 589832 | tf_op jit(solution)/shard_map/ppermute | solution.py:36
  46.4 0.0 collective-permute-start.19
  46.4 3.7 %collective-permute-done.3.refs_1_ = bf16[128,768]{1,0:T(8,128)(2,1)S(1)} collective-permute-done((bf16[128,768]{1,0:T(8,128)(2,1)S(1)}, bf16[128,768]{1,0:T(8,128)(2,1)S(1)}, u32[]{:S(2)}, u32[]{:S(2)}) %collective-permute-start.3) | collective-permute-done | bytes 196640 | tf_op jit(solution)/shard_map/ppermute | solution.py:36
  50.0 0.0 collective-permute-start.20
  50.0 0.0 collective-permute-done.13.refs_5_
  50.0 2.8 %collective-permute-start.14 = (bf16[256,768]{1,0:T(8,128)(2,1)S(1)}, bf16[256,768]{1,0:T(8,128)(2,1)S(1)}, u32[]{:S(2)}, u32[]{:S(2)}) collective-permute-start(bf16[256,768]{1,0:T(8,128)(2,1)S(1)} %collective-permute-done.13.refs_5_), channel_id=1, source_target_pairs={{0,16},{1,17},{2,18},{3,19},{4,20},{5,21},{6,22},{7,23},{8,120},{9... | collective-permute-start | bytes 1179656 | tf_op jit(solution)/shard_map/ppermute | solution.py:36
  52.9 2.2 %collective-permute-done.4.refs_2_ = bf16[128,768]{1,0:T(8,128)(2,1)S(1)} collective-permute-done((bf16[128,768]{1,0:T(8,128)(2,1)S(1)}, bf16[128,768]{1,0:T(8,128)(2,1)S(1)}, u32[]{:S(2)}, u32[]{:S(2)}) %collective-permute-start.4) | collective-permute-done | bytes 196640 | tf_op jit(solution)/shard_map/ppermute | solution.py:36
  55.0 0.0 collective-permute-start.5
  55.0 0.0 collective-permute-done.8.refs_4_
  55.0 0.0 collective-permute-start.9
  55.1 6.5 %collective-permute-done.5.refs_3_ = bf16[128,768]{1,0:T(8,128)(2,1)S(1)} collective-permute-done((bf16[128,768]{1,0:T(8,128)(2,1)S(1)}, bf16[128,768]{1,0:T(8,128)(2,1)S(1)}, u32[]{:S(2)}, u32[]{:S(2)}) %collective-permute-start.5) | collective-permute-done | bytes 196640 | tf_op jit(solution)/shard_map/ppermute | solution.py:36
  61.5 0.8 collective-permute-start.17
  62.4 0.0 collective-permute-start.18
  62.4 0.0 collective-permute-done.20.refs_7_
  62.4 0.5 collective-permute-start.15
  62.9 0.1 collective-permute-start.16
  63.0 4.7 %flash.5 = (f32[768,512]{1,0:T(8,128)S(1)}, f32[48,512]{1,0:T(8,128)S(1)}) custom-call(bf16[128,768]{1,0:T(8,128)(2,1)S(1)} %pad_maximum_fusion.refs_0_, bf16[128,768]{1,0:T(8,128)(2,1)S(1)} %collective-permute-done.3.refs_1_, bf16[128,768]{1,0:T(8,128)(2,1)S(1)} %collective-permute-done.4.refs_2_, bf16[128,768]{1,0:T(8,128)(2,1)S(1)} %collective-permute-done.5.refs_3_, ...), custom_call_target="tpu_custom_call" | custom-call | flops 805306368 | bytes 4000000 | tf_op jit(solution)/shard_map/flash/pallas_call | solution.py:171
  67.7 0.5 collective-permute-start.10
  68.2 6.5 %flash.6 = (f32[768,512]{1,0:T(8,128)S(1)}, f32[48,512]{1,0:T(8,128)S(1)}) custom-call(bf16[128,768]{1,0:T(8,128)(2,1)S(1)} %pad_maximum_fusion.refs_0_, bf16[128,768]{1,0:T(8,128)(2,1)S(1)} %collective-permute-done.3.refs_1_, bf16[128,768]{1,0:T(8,128)(2,1)S(1)} %collective-permute-done.4.refs_2_, bf16[128,768]{1,0:T(8,128)(2,1)S(1)} %collective-permute-done.5.refs_3_, ...), custom_call_target="tpu_custom_call" | custom-call | flops 1610612736 | bytes 4000000 | tf_op jit(solution)/shard_map/flash/pallas_call | solution.py:171
  74.7 0.0 collective-permute-done.17.refs_6_
  74.7 6.5 %flash.7 = (f32[768,512]{1,0:T(8,128)S(1)}, f32[48,512]{1,0:T(8,128)S(1)}) custom-call(bf16[128,768]{1,0:T(8,128)(2,1)S(1)} %pad_maximum_fusion.refs_0_, bf16[128,768]{1,0:T(8,128)(2,1)S(1)} %collective-permute-done.3.refs_1_, bf16[128,768]{1,0:T(8,128)(2,1)S(1)} %collective-permute-done.4.refs_2_, bf16[128,768]{1,0:T(8,128)(2,1)S(1)} %collective-permute-done.5.refs_3_, ...), custom_call_target="tpu_custom_call" | custom-call | flops 1610612736 | bytes 4000000 | tf_op jit(solution)/shard_map/flash/pallas_call | solution.py:171
  81.2 0.0 collective-permute-done.15.refs_6_
  81.3 0.0 collective-permute-done.16.refs_7_
  81.3 6.5 %flash.8 = (f32[768,512]{1,0:T(8,128)S(1)}, f32[48,512]{1,0:T(8,128)S(1)}) custom-call(bf16[128,768]{1,0:T(8,128)(2,1)S(1)} %pad_maximum_fusion.refs_0_, bf16[128,768]{1,0:T(8,128)(2,1)S(1)} %collective-permute-done.3.refs_1_, bf16[128,768]{1,0:T(8,128)(2,1)S(1)} %collective-permute-done.4.refs_2_, bf16[128,768]{1,0:T(8,128)(2,1)S(1)} %collective-permute-done.5.refs_3_, ...), custom_call_target="tpu_custom_call" | custom-call | flops 1610612736 | bytes 4000000 | tf_op jit(solution)/shard_map/flash/pallas_call | solution.py:171
  87.8 0.0 collective-permute-done.10.refs_5_
  87.8 5.0 %flash.9 = (bf16[144,768]{1,0:T(8,128)(2,1)S(1)}, bf16[144,768]{1,0:T(8,128)(2,1)S(1)}, bf16[144,768]{1,0:T(8,128)(2,1)S(1)}, bf16[144,768]{1,0:T(8,128)(2,1)S(1)}) custom-call(bf16[128,768]{1,0:T(8,128)(2,1)S(1)} %pad_maximum_fusion.refs_0_, bf16[128,768]{1,0:T(8,128)(2,1)S(1)} %collective-permute-done.3.refs_1_, ...), custom_call_target="tpu_custom_call" | custom-call | flops 805306368 | bytes 4000000 | tf_op jit(solution)/shard_map/flash/pallas_call | solution.py:171
  92.8 1.3 %collective-permute-start.21 = (bf16[144,768]{1,0:T(8,128)(2,1)S(1)}, bf16[144,768]{1,0:T(8,128)(2,1)S(1)}, u32[]{:S(2)}, u32[]{:S(2)}) collective-permute-start(bf16[144,768]{1,0:T(8,128)(2,1)S(1)} %get-tuple-element.38), channel_id=1, source_target_pairs={{0,3},{1,0},{2,1},{3,2},{4,7},{5,4},{6,5},{7,6},{8,11},{9,8},{10,9... | collective-permute-start | bytes 663560 | tf_op jit(solution)/shard_map/ppermute | solution.py:36
  94.1 0.7 collective-permute-start.23
  94.8 5.1 %collective-permute-done.21.refs_1_ = bf16[144,768]{1,0:T(8,128)(2,1)S(1)} collective-permute-done((bf16[144,768]{1,0:T(8,128)(2,1)S(1)}, bf16[144,768]{1,0:T(8,128)(2,1)S(1)}, u32[]{:S(2)}, u32[]{:S(2)}) %collective-permute-start.21) | collective-permute-done | bytes 221216 | tf_op jit(solution)/shard_map/ppermute | solution.py:36
  99.8 2.4 %collective-permute-done.22.refs_2_ = bf16[144,768]{1,0:T(8,128)(2,1)S(1)} collective-permute-done((bf16[144,768]{1,0:T(8,128)(2,1)S(1)}, bf16[144,768]{1,0:T(8,128)(2,1)S(1)}, u32[]{:S(2)}, u32[]{:S(2)}) %collective-permute-start.22) | collective-permute-done | bytes 221216 | tf_op jit(solution)/shard_map/ppermute | solution.py:36
  102.3 4.8 %collective-permute-done.23.refs_3_ = bf16[144,768]{1,0:T(8,128)(2,1)S(1)} collective-permute-done((bf16[144,768]{1,0:T(8,128)(2,1)S(1)}, bf16[144,768]{1,0:T(8,128)(2,1)S(1)}, u32[]{:S(2)}, u32[]{:S(2)}) %collective-permute-start.23) | collective-permute-done | bytes 221216 | tf_op jit(solution)/shard_map/ppermute | solution.py:36
  107.1 1.1 merge.1
  108.3 1.9 %collective-permute-start.24 = (bf16[32,768]{1,0:T(8,128)(2,1)S(1)}, bf16[32,768]{1,0:T(8,128)(2,1)S(1)}, u32[]{:S(2)}, u32[]{:S(2)}) collective-permute-start(bf16[32,768]{1,0:T(8,128)(2,1)S(1)} %get-tuple-element.42), channel_id=1, source_target_pairs={{0,132},{1,133},{2,134},{3,135},{4,128},{5,129},{6,130},{7,131},{8... | collective-permute-start | bytes 147464 | tf_op jit(solution)/shard_map/ppermute | solution.py:36
  110.2 0.9 collective-permute-start.25
  111.1 0.4 collective-permute-start.26
  111.5 3.2 %collective-permute-done.25.refs_2_ = bf16[32,768]{1,0:T(8,128)(2,1)S(1)} collective-permute-done((bf16[32,768]{1,0:T(8,128)(2,1)S(1)}, bf16[32,768]{1,0:T(8,128)(2,1)S(1)}, u32[]{:S(2)}, u32[]{:S(2)}) %collective-permute-start.25) | collective-permute-done | bytes 49184 | tf_op jit(solution)/shard_map/ppermute | solution.py:36
  114.6 0.6 collective-permute-done.26.refs_3_
  115.2 1.2 %assemble.1 = bf16[32,3072]{1,0:T(8,128)(2,1)} custom-call(s32[2]{0:T(128)S(1)} %pad_add_fusion.where_ref, bf16[32,768]{1,0:T(8,128)(2,1)S(1)} %get-tuple-element.41.refs_0_, bf16[32,768]{1,0:T(8,128)(2,1)S(1)} %collective-permute-done.24.refs_1_, bf16[32,768]{1,0:T(8,128)(2,1)S(1)} %collective-permute-done.25.refs_2_, ...), custom_call_target="tpu_custom_call" | custom-call | flops 100000 | bytes 400000 | tf_op jit(solution)/shard_map/assemble/pallas_call | solution.py:222
  (21 shorter events, 0.1 us)
Async XLA Ops:
  1.5 0.9 copy-start
  2.5 0.9 copy-start.1
  3.4 0.9 copy-start.2
  4.3 0.9 copy-start.3
  5.3 0.9 copy-start.4
  6.2 0.7 copy-start.5
  7.8 6.2 %collective-permute-start = (bf16[96,768]{1,0:T(8,128)(2,1)S(1)}, bf16[96,768]{1,0:T(8,128)(2,1)S(1)}, u32[]{:S(2)}, u32[]{:S(2)}) collective-permute-start(bf16[96,768]{1,0:T(8,128)(2,1)S(1)} %get-tuple-element.26), channel_id=1, source_target_pairs={{0,128},{1,129},{2,130},{3,131},{4,132},{5,133},{6,134},{7,135},{8... | collective-permute-start | bytes 442376 | tf_op jit(solution)/shard_map/ppermute | solution.py:36
  10.0 9.0 %collective-permute-start.1 = (bf16[96,768]{1,0:T(8,128)(2,1)S(1)}, bf16[96,768]{1,0:T(8,128)(2,1)S(1)}, u32[]{:S(2)}, u32[]{:S(2)}) collective-permute-start(bf16[96,768]{1,0:T(8,128)(2,1)S(1)} %get-tuple-element.27), channel_id=1, source_target_pairs={{0,4},{1,5},{2,6},{3,7},{4,0},{5,1},{6,2},{7,3},{8,12},{9,13},{10,... | collective-permute-start | bytes 442376 | tf_op jit(solution)/shard_map/ppermute | solution.py:36
  12.6 6.4 %collective-permute-start.2 = (bf16[96,768]{1,0:T(8,128)(2,1)S(1)}, bf16[96,768]{1,0:T(8,128)(2,1)S(1)}, u32[]{:S(2)}, u32[]{:S(2)}) collective-permute-start(bf16[96,768]{1,0:T(8,128)(2,1)S(1)} %get-tuple-element.28), channel_id=1, source_target_pairs={{0,132},{1,133},{2,134},{3,135},{4,128},{5,129},{6,130},{7,131},{8... | collective-permute-start | bytes 442376 | tf_op jit(solution)/shard_map/ppermute | solution.py:36
  19.1 7.2 %collective-permute-start.11 = (bf16[256,768]{1,0:T(8,128)(2,1)S(1)}, bf16[256,768]{1,0:T(8,128)(2,1)S(1)}, u32[]{:S(2)}, u32[]{:S(2)}) collective-permute-start(bf16[256,768]{1,0:T(8,128)(2,1)S(1)} %get-tuple-element.45.refs_4_), channel_id=1, source_target_pairs={{0,8},{1,9},{2,10},{3,11},{4,12},{5,13},{6,14},{7,15},{8,0},{9,1},... | collective-permute-start | bytes 1179656 | tf_op jit(solution)/shard_map/ppermute | solution.py:36
  20.8 10.2 %collective-permute-start.6 = (bf16[256,768]{1,0:T(8,128)(2,1)S(1)}, bf16[256,768]{1,0:T(8,128)(2,1)S(1)}, u32[]{:S(2)}, u32[]{:S(2)}) collective-permute-start(bf16[256,768]{1,0:T(8,128)(2,1)S(1)} %get-tuple-element.45.refs_4_), channel_id=1, source_target_pairs={{0,16},{1,17},{2,18},{3,19},{4,20},{5,21},{6,22},{7,23},{8,120},{9... | collective-permute-start | bytes 1179656 | tf_op jit(solution)/shard_map/ppermute | solution.py:36
  26.3 8.9 %collective-permute-start.12 = (bf16[256,768]{1,0:T(8,128)(2,1)S(1)}, bf16[256,768]{1,0:T(8,128)(2,1)S(1)}, u32[]{:S(2)}, u32[]{:S(2)}) collective-permute-start(bf16[256,768]{1,0:T(8,128)(2,1)S(1)} %collective-permute-done.11.refs_5_), channel_id=1, source_target_pairs={{0,16},{1,17},{2,18},{3,19},{4,20},{5,21},{6,22},{7,23},{8,120},{9... | collective-permute-start | bytes 1179656 | tf_op jit(solution)/shard_map/ppermute | solution.py:36
  31.1 8.4 %collective-permute-start.7 = (bf16[256,768]{1,0:T(8,128)(2,1)S(1)}, bf16[256,768]{1,0:T(8,128)(2,1)S(1)}, u32[]{:S(2)}, u32[]{:S(2)}) collective-permute-start(bf16[256,768]{1,0:T(8,128)(2,1)S(1)} %collective-permute-done.6.refs_4_), channel_id=1, source_target_pairs={{0,16},{1,17},{2,18},{3,19},{4,20},{5,21},{6,22},{7,23},{8,120},{9... | collective-permute-start | bytes 1179656 | tf_op jit(solution)/shard_map/ppermute | solution.py:36
  35.3 14.8 %collective-permute-start.13 = (bf16[256,768]{1,0:T(8,128)(2,1)S(1)}, bf16[256,768]{1,0:T(8,128)(2,1)S(1)}, u32[]{:S(2)}, u32[]{:S(2)}) collective-permute-start(bf16[256,768]{1,0:T(8,128)(2,1)S(1)} %collective-permute-done.12.refs_5_), channel_id=1, source_target_pairs={{0,16},{1,17},{2,18},{3,19},{4,20},{5,21},{6,22},{7,23},{8,120},{9... | collective-permute-start | bytes 1179656 | tf_op jit(solution)/shard_map/ppermute | solution.py:36
  39.5 15.6 %collective-permute-start.8 = (bf16[256,768]{1,0:T(8,128)(2,1)S(1)}, bf16[256,768]{1,0:T(8,128)(2,1)S(1)}, u32[]{:S(2)}, u32[]{:S(2)}) collective-permute-start(bf16[256,768]{1,0:T(8,128)(2,1)S(1)} %collective-permute-done.7.refs_4_), channel_id=1, source_target_pairs={{0,16},{1,17},{2,18},{3,19},{4,20},{5,21},{6,22},{7,23},{8,120},{9... | collective-permute-start | bytes 1179656 | tf_op jit(solution)/shard_map/ppermute | solution.py:36
  42.6 7.4 %collective-permute-start.3 = (bf16[128,768]{1,0:T(8,128)(2,1)S(1)}, bf16[128,768]{1,0:T(8,128)(2,1)S(1)}, u32[]{:S(2)}, u32[]{:S(2)}) collective-permute-start(bf16[128,768]{1,0:T(8,128)(2,1)S(1)} %pad_maximum_fusion.refs_0_), channel_id=1, source_target_pairs={{0,1},{1,2},{2,3},{3,0},{4,5},{5,6},{6,7},{7,4},{8,9},{9,10},{10,1... | collective-permute-start | bytes 589832 | tf_op jit(solution)/shard_map/ppermute | solution.py:36
  43.9 11.1 %collective-permute-start.4 = (bf16[128,768]{1,0:T(8,128)(2,1)S(1)}, bf16[128,768]{1,0:T(8,128)(2,1)S(1)}, u32[]{:S(2)}, u32[]{:S(2)}) collective-permute-start(bf16[128,768]{1,0:T(8,128)(2,1)S(1)} %pad_maximum_fusion.refs_0_), channel_id=1, source_target_pairs={{0,2},{1,3},{2,0},{3,1},{4,6},{5,7},{6,4},{7,5},{8,10},{9,11},{10,... | collective-permute-start | bytes 589832 | tf_op jit(solution)/shard_map/ppermute | solution.py:36
  46.4 16.0 %collective-permute-start.19 = (bf16[256,768]{1,0:T(8,128)(2,1)S(1)}, bf16[256,768]{1,0:T(8,128)(2,1)S(1)}, u32[]{:S(2)}, u32[]{:S(2)}) collective-permute-start(bf16[256,768]{1,0:T(8,128)(2,1)S(1)} %collective-permute-done.6.refs_4_), channel_id=1, source_target_pairs={{0,8},{1,9},{2,10},{3,11},{4,12},{5,13},{6,14},{7,15},{8,0},{9,1},... | collective-permute-start | bytes 1179656 | tf_op jit(solution)/shard_map/ppermute | solution.py:36
  50.0 12.3 %collective-permute-start.20 = (bf16[256,768]{1,0:T(8,128)(2,1)S(1)}, bf16[256,768]{1,0:T(8,128)(2,1)S(1)}, u32[]{:S(2)}, u32[]{:S(2)}) collective-permute-start(bf16[256,768]{1,0:T(8,128)(2,1)S(1)} %collective-permute-done.12.refs_5_), channel_id=1, source_target_pairs={{0,8},{1,9},{2,10},{3,11},{4,12},{5,13},{6,14},{7,15},{8,0},{9,1},... | collective-permute-start | bytes 1179656 | tf_op jit(solution)/shard_map/ppermute | solution.py:36
  50.0 12.8 %collective-permute-start.14 = (bf16[256,768]{1,0:T(8,128)(2,1)S(1)}, bf16[256,768]{1,0:T(8,128)(2,1)S(1)}, u32[]{:S(2)}, u32[]{:S(2)}) collective-permute-start(bf16[256,768]{1,0:T(8,128)(2,1)S(1)} %collective-permute-done.13.refs_5_), channel_id=1, source_target_pairs={{0,16},{1,17},{2,18},{3,19},{4,20},{5,21},{6,22},{7,23},{8,120},{9... | collective-permute-start | bytes 1179656 | tf_op jit(solution)/shard_map/ppermute | solution.py:36
  55.0 6.5 %collective-permute-start.5 = (bf16[128,768]{1,0:T(8,128)(2,1)S(1)}, bf16[128,768]{1,0:T(8,128)(2,1)S(1)}, u32[]{:S(2)}, u32[]{:S(2)}) collective-permute-start(bf16[128,768]{1,0:T(8,128)(2,1)S(1)} %pad_maximum_fusion.refs_0_), channel_id=1, source_target_pairs={{0,3},{1,0},{2,1},{3,2},{4,7},{5,4},{6,5},{7,6},{8,11},{9,8},{10,9... | collective-permute-start | bytes 589832 | tf_op jit(solution)/shard_map/ppermute | solution.py:36
  55.0 12.6 %collective-permute-start.9 = (bf16[256,768]{1,0:T(8,128)(2,1)S(1)}, bf16[256,768]{1,0:T(8,128)(2,1)S(1)}, u32[]{:S(2)}, u32[]{:S(2)}) collective-permute-start(bf16[256,768]{1,0:T(8,128)(2,1)S(1)} %collective-permute-done.8.refs_4_), channel_id=1, source_target_pairs={{0,16},{1,17},{2,18},{3,19},{4,20},{5,21},{6,22},{7,23},{8,120},{9... | collective-permute-start | bytes 1179656 | tf_op jit(solution)/shard_map/ppermute | solution.py:36
  61.5 13.2 %collective-permute-start.17 = (bf16[256,768]{1,0:T(8,128)(2,1)S(1)}, bf16[256,768]{1,0:T(8,128)(2,1)S(1)}, u32[]{:S(2)}, u32[]{:S(2)}) collective-permute-start(bf16[256,768]{1,0:T(8,128)(2,1)S(1)} %collective-permute-done.7.refs_4_), channel_id=1, source_target_pairs={{0,8},{1,9},{2,10},{3,11},{4,12},{5,13},{6,14},{7,15},{8,0},{9,1},... | collective-permute-start | bytes 1179656 | tf_op jit(solution)/shard_map/ppermute | solution.py:36
  62.4 12.4 %collective-permute-start.18 = (bf16[256,768]{1,0:T(8,128)(2,1)S(1)}, bf16[256,768]{1,0:T(8,128)(2,1)S(1)}, u32[]{:S(2)}, u32[]{:S(2)}) collective-permute-start(bf16[256,768]{1,0:T(8,128)(2,1)S(1)} %collective-permute-done.13.refs_5_), channel_id=1, source_target_pairs={{0,8},{1,9},{2,10},{3,11},{4,12},{5,13},{6,14},{7,15},{8,0},{9,1},... | collective-permute-start | bytes 1179656 | tf_op jit(solution)/shard_map/ppermute | solution.py:36
  62.4 18.9 %collective-permute-start.15 = (bf16[256,768]{1,0:T(8,128)(2,1)S(1)}, bf16[256,768]{1,0:T(8,128)(2,1)S(1)}, u32[]{:S(2)}, u32[]{:S(2)}) collective-permute-start(bf16[256,768]{1,0:T(8,128)(2,1)S(1)} %collective-permute-done.8.refs_4_), channel_id=1, source_target_pairs={{0,8},{1,9},{2,10},{3,11},{4,12},{5,13},{6,14},{7,15},{8,0},{9,1},... | collective-permute-start | bytes 1179656 | tf_op jit(solution)/shard_map/ppermute | solution.py:36
  62.9 18.4 %collective-permute-start.16 = (bf16[256,768]{1,0:T(8,128)(2,1)S(1)}, bf16[256,768]{1,0:T(8,128)(2,1)S(1)}, u32[]{:S(2)}, u32[]{:S(2)}) collective-permute-start(bf16[256,768]{1,0:T(8,128)(2,1)S(1)} %collective-permute-done.14.refs_5_), channel_id=1, source_target_pairs={{0,8},{1,9},{2,10},{3,11},{4,12},{5,13},{6,14},{7,15},{8,0},{9,1},... | collective-permute-start | bytes 1179656 | tf_op jit(solution)/shard_map/ppermute | solution.py:36
  67.7 20.1 %collective-permute-start.10 = (bf16[256,768]{1,0:T(8,128)(2,1)S(1)}, bf16[256,768]{1,0:T(8,128)(2,1)S(1)}, u32[]{:S(2)}, u32[]{:S(2)}) collective-permute-start(bf16[256,768]{1,0:T(8,128)(2,1)S(1)} %collective-permute-done.9.refs_4_), channel_id=1, source_target_pairs={{0,8},{1,9},{2,10},{3,11},{4,12},{5,13},{6,14},{7,15},{8,0},{9,1},... | collective-permute-start | bytes 1179656 | tf_op jit(solution)/shard_map/ppermute | solution.py:36
  92.8 7.1 %collective-permute-start.21 = (bf16[144,768]{1,0:T(8,128)(2,1)S(1)}, bf16[144,768]{1,0:T(8,128)(2,1)S(1)}, u32[]{:S(2)}, u32[]{:S(2)}) collective-permute-start(bf16[144,768]{1,0:T(8,128)(2,1)S(1)} %get-tuple-element.38), channel_id=1, source_target_pairs={{0,3},{1,0},{2,1},{3,2},{4,7},{5,4},{6,5},{7,6},{8,11},{9,8},{10,9... | collective-permute-start | bytes 663560 | tf_op jit(solution)/shard_map/ppermute | solution.py:36
  94.1 8.2 %collective-permute-start.22 = (bf16[144,768]{1,0:T(8,128)(2,1)S(1)}, bf16[144,768]{1,0:T(8,128)(2,1)S(1)}, u32[]{:S(2)}, u32[]{:S(2)}) collective-permute-start(bf16[144,768]{1,0:T(8,128)(2,1)S(1)} %get-tuple-element.39), channel_id=1, source_target_pairs={{0,2},{1,3},{2,0},{3,1},{4,6},{5,7},{6,4},{7,5},{8,10},{9,11},{10,... | collective-permute-start | bytes 663560 | tf_op jit(solution)/shard_map/ppermute | solution.py:36
  94.1 13.0 %collective-permute-start.23 = (bf16[144,768]{1,0:T(8,128)(2,1)S(1)}, bf16[144,768]{1,0:T(8,128)(2,1)S(1)}, u32[]{:S(2)}, u32[]{:S(2)}) collective-permute-start(bf16[144,768]{1,0:T(8,128)(2,1)S(1)} %get-tuple-element.40), channel_id=1, source_target_pairs={{0,1},{1,2},{2,3},{3,0},{4,5},{5,6},{6,7},{7,4},{8,9},{9,10},{10,1... | collective-permute-start | bytes 663560 | tf_op jit(solution)/shard_map/ppermute | solution.py:36
  108.3 3.2 %collective-permute-start.24 = (bf16[32,768]{1,0:T(8,128)(2,1)S(1)}, bf16[32,768]{1,0:T(8,128)(2,1)S(1)}, u32[]{:S(2)}, u32[]{:S(2)}) collective-permute-start(bf16[32,768]{1,0:T(8,128)(2,1)S(1)} %get-tuple-element.42), channel_id=1, source_target_pairs={{0,132},{1,133},{2,134},{3,135},{4,128},{5,129},{6,130},{7,131},{8... | collective-permute-start | bytes 147464 | tf_op jit(solution)/shard_map/ppermute | solution.py:36
  110.2 4.4 %collective-permute-start.25 = (bf16[32,768]{1,0:T(8,128)(2,1)S(1)}, bf16[32,768]{1,0:T(8,128)(2,1)S(1)}, u32[]{:S(2)}, u32[]{:S(2)}) collective-permute-start(bf16[32,768]{1,0:T(8,128)(2,1)S(1)} %get-tuple-element.43), channel_id=1, source_target_pairs={{0,4},{1,5},{2,6},{3,7},{4,0},{5,1},{6,2},{7,3},{8,12},{9,13},{10,... | collective-permute-start | bytes 147464 | tf_op jit(solution)/shard_map/ppermute | solution.py:36
  111.1 4.2 %collective-permute-start.26 = (bf16[32,768]{1,0:T(8,128)(2,1)S(1)}, bf16[32,768]{1,0:T(8,128)(2,1)S(1)}, u32[]{:S(2)}, u32[]{:S(2)}) collective-permute-start(bf16[32,768]{1,0:T(8,128)(2,1)S(1)} %get-tuple-element.44), channel_id=1, source_target_pairs={{0,128},{1,129},{2,130},{3,131},{4,132},{5,133},{6,134},{7,135},{8... | collective-permute-start | bytes 147464 | tf_op jit(solution)/shard_map/ppermute | solution.py:36

commit v2 on v0

v2 whole, which is shorter than its diff:
```python
import functools

import jax
import jax.numpy as jnp
from jax import lax
from jax.experimental import pallas as pl
from jax.experimental.pallas import tpu as pltpu
from jax.sharding import Mesh
from jax.sharding import PartitionSpec as P

AXES = ("yl", "z", "core", "yh", "x")
SIZES = (2, 8, 2, 2, 4)
NX, NY, NZ = 4, 4, 8
HEAD = 128
TOK = 32
HEADS = 6
WIDTH = HEADS * HEAD
TAIL = 128
LOG2E = 1.4426950408889634
SCALE2 = HEAD**-0.5 * LOG2E
VMEM_LIMIT = 32 * 1024 * 1024
BF16, F32 = jnp.bfloat16, jnp.float32
IN_VMEM = pl.BlockSpec(memory_space=pltpu.VMEM)
IN_SMEM = pl.BlockSpec(memory_space=pltpu.SMEM)


def permute(value, move):
    pairs = []
    for index in range(2 * NX * NY * NZ):
        rest, x = divmod(index, NX)
        rest, yh = divmod(rest, 2)
        rest, core = divmod(rest, 2)
        yl, z = divmod(rest, NZ)
        x, y, z, core = move(x, 2 * yh + yl, z, core)
        pairs.append((index, ((((y % 2) * NZ + z) * 2 + core) * 2 + y // 2) * NX + x))
    return lax.ppermute(value, AXES, pairs)


def shift_x(value, d):
    return permute(value, lambda x, y, z, c: ((x + d) % NX, y, z, c))


def shift_y(value, d):
    return permute(value, lambda x, y, z, c: (x, (y + d) % NY, z, c))


def ring_z(value):
    return permute(value, lambda x, y, z, c: (x, y, (z + 1 - 2 * c) % NZ, c))


def swap_core(value):
    return permute(value, lambda x, y, z, c: (x, y, z, 1 - c))


def options(us, limit=VMEM_LIMIT):
    return dict(
        compiler_params=pltpu.CompilerParams(vmem_limit_bytes=limit),
        cost_estimate=pl.CostEstimate(flops=int(us * 1.0e9), bytes_accessed=int(us * 3.0e6), transcendentals=0),
    )


def mix_kernel(where_ref, step_ref, q_hbm, ke_hbm, ve_hbm, ks_hbm, vs_hbm, mask_hbm, gate_hbm, *refs):
    sources = (mask_hbm, gate_hbm, ke_hbm, ks_hbm, ve_hbm, vs_hbm, q_hbm)
    outs, scratch, gates, sem = refs[: NY + 1], refs[NY + 1 : -2], refs[-2], refs[-1]
    copies = [pltpu.make_async_copy(a, b, sem.at[i]) for i, (a, b) in enumerate(zip(sources, scratch))]
    for copy in copies:
        copy.start()
    for copy in copies:
        copy.wait()
    mask_ref, gate_ref, ke_ref, ks_ref, ve_ref, vs_ref, q_ref = scratch
    y, u = where_ref[0], where_ref[2]
    span = mask_ref.shape[1]
    lane = lax.broadcasted_iota(jnp.int32, (TOK, span), 1)
    row = lax.broadcasted_iota(jnp.int32, (TOK, span), 0)
    picked = jnp.where(lane == u * TOK + row, jnp.broadcast_to(mask_ref[...], (TOK, span)), 0)
    inside = jnp.sum(picked, axis=1, keepdims=True) == 1
    step_lane = lax.broadcasted_iota(jnp.int32, gate_ref.shape, 1)
    at_step = jnp.sum(jnp.where(step_lane == step_ref[0], gate_ref[...], 0.0), axis=1, keepdims=True)
    gates[...] = jnp.broadcast_to(at_step, gates.shape)
    for d in range(NY):
        group = lax.rem(y + d, NY)
        for h in range(HEADS):
            head = group * HEADS + h
            strength = gates[pl.ds(head, 1), :]
            cols = pl.ds(pl.multiple_of(head * HEAD, HEAD), HEAD)
            to = slice(h * HEAD, (h + 1) * HEAD)
            for n, (edit, source) in enumerate(((ke_ref, ks_ref), (ve_ref, vs_ref))):
                e = edit[:, cols].astype(F32)
                s = source[:, cols].astype(F32)
                mixed = jnp.where(inside, e, s + strength * (e - s))
                outs[d][n * TOK : (n + 1) * TOK, to] = mixed.astype(BF16)
            if d == 0:
                outs[NY][:, to] = q_ref[:, cols]
            else:
                outs[d][2 * TOK :, to] = q_ref[:, cols]


def mix(where, step_index, queries, ke, ve, ks, vs, edit_mask, gate):
    edit_mask = edit_mask.reshape(1, -1)
    gate = gate.T
    big = pltpu.VMEM(queries.shape, BF16)
    return pl.pallas_call(
        mix_kernel,
        out_shape=[jax.ShapeDtypeStruct((n * TOK, WIDTH), BF16) for n in (2, 3, 3, 3, 1)],
        in_specs=[IN_SMEM, IN_SMEM] + [pl.BlockSpec(memory_space=pltpu.HBM)] * 7,
        out_specs=[IN_VMEM] * (NY + 1),
        scratch_shapes=[pltpu.VMEM(edit_mask.shape, jnp.int32), pltpu.VMEM(gate.shape, F32)]
        + [big] * 5
        + [pltpu.VMEM((gate.shape[0], HEAD), F32)]
        + [pltpu.SemaphoreType.DMA((7,))],
        name="mix",
        **options(2, 60 * 1024 * 1024),
    )(where, step_index, queries, ke, ve, ks, vs, edit_mask, gate)


def flash_kernel(first, last, blocks, *refs):
    refs = list(refs)
    if last:
        where_ref, refs = refs[0], refs[1:]
    q_refs, refs = refs[:NX], refs[NX:]
    kv_refs, refs = refs[:blocks], refs[blocks:]
    if not first:
        acc_in, ml_in, refs = refs[0], refs[1], refs[2:]
    rows = NY * TOK
    logs = [[] for _ in range(NX)]
    for h in range(HEADS):
        cols = slice(h * HEAD, (h + 1) * HEAD)
        pieces = [(r, at) for r in kv_refs for at in range(0, r.shape[0], 2 * TOK)]
        keys = jnp.concatenate([r[at : at + TOK, cols] for r, at in pieces], axis=0)
        values = jnp.concatenate([r[at + TOK : at + 2 * TOK, cols] for r, at in pieces], axis=0)
        for part in range(NX):
            at = slice(part * rows, (part + 1) * rows)
            q = q_refs[part][:, cols]
            s = lax.dot_general(keys, q, (((1,), (1,)), ((), ())), preferred_element_type=F32)
            top = jnp.max(s, axis=0, keepdims=True)
            if not first:
                old = ml_in[8 * h : 8 * h + 1, at]
                top = jnp.maximum(top, old)
            p = jnp.exp2((s - top) * SCALE2)
            total = jnp.sum(p, axis=0, keepdims=True)
            o = lax.dot_general(values, p.astype(BF16), (((0,), (0,)), ((), ())), preferred_element_type=F32)
            if not first:
                alpha = jnp.exp2((old - top) * SCALE2)
                total = total + alpha * ml_in[8 * h + 1 : 8 * h + 2, at]
                o = o + alpha * acc_in[cols, at]
            if last:
                o = (o * (1.0 / total)).T.astype(BF16)
                for e in range(NY):
                    out_at = pl.ds(target(where_ref, part, e) * TOK, TOK)
                    refs[0][out_at, cols] = o[e * TOK : (e + 1) * TOK, :]
                lse = top * SCALE2 + jnp.log2(total)
                hi = lse.astype(BF16).astype(F32)
                mid = (lse - hi).astype(BF16).astype(F32)
                logs[part].append((hi, mid, lse - hi - mid))
            else:
                refs[0][cols, at] = o
                refs[1][8 * h : 8 * h + 1, at] = top
                refs[1][8 * h + 1 : 8 * h + 2, at] = total
    if last:
        for part in range(NX):
            pad = jnp.zeros((TAIL - 3 * HEADS, rows), F32)
            columns = [log[i] for i in range(3) for log in logs[part]]
            packed = jnp.concatenate(columns + [pad], axis=0).T.astype(BF16)
            for e in range(NY):
                out_at = pl.ds(target(where_ref, part, e) * TOK, TOK)
                refs[0][out_at, WIDTH:] = packed[e * TOK : (e + 1) * TOK, :]


def target(where_ref, d, e):
    y = lax.rem(where_ref[0] + (NY - e), NY)
    x = lax.rem(where_ref[1] + (NX - d), NX)
    return (lax.rem(y, 2) * 2 + y // 2) * NX + x


def flash(q_parts, kv_blocks, state, where):
    queries = NX * NY * TOK
    first, last = state is None, where is not None
    if last:
        out_shape = jax.ShapeDtypeStruct((queries, WIDTH + TAIL), BF16)
    else:
        out_shape = [
            jax.ShapeDtypeStruct((WIDTH, queries), F32),
            jax.ShapeDtypeStruct((8 * HEADS, queries), F32),
        ]
    n = sum(b.shape[0] // 2 for b in kv_blocks)
    args = ([where] if last else []) + list(q_parts) + list(kv_blocks) + list(state or ())
    return pl.pallas_call(
        functools.partial(flash_kernel, first, last, len(kv_blocks)),
        out_shape=out_shape,
        in_specs=[IN_SMEM] * last + [IN_VMEM] * (len(args) - last),
        out_specs=IN_VMEM if last else [IN_VMEM, IN_VMEM],
        name="flash",
        **options(1.5 + n * 0.0045),
    )(*args)


def merge_kernel(in_ref, out_ref):
    lse = in_ref[:, WIDTH:].astype(F32)
    lse = lse[:, :HEADS] + lse[:, HEADS : 2 * HEADS] + lse[:, 2 * HEADS : 3 * HEADS]
    for y in range(NY):
        first = ((y % 2) * 2 + y // 2) * NX
        rows = [slice((first + x) * TOK, (first + x + 1) * TOK) for x in range(NX)]
        top = functools.reduce(jnp.maximum, [lse[r] for r in rows])
        weight = [jnp.exp2(lse[r] - top) for r in rows]
        scale = 1.0 / functools.reduce(jnp.add, weight)
        weight = [w * scale for w in weight]
        for h in range(HEADS):
            cols = slice(h * HEAD, (h + 1) * HEAD)
            total = functools.reduce(
                jnp.add, [w[:, h : h + 1] * in_ref[r, cols].astype(F32) for w, r in zip(weight, rows)]
            )
            at = y * WIDTH + h * HEAD
            out_ref[:, at : at + HEAD] = total.astype(BF16)


def merge(parts):
    return pl.pallas_call(
        merge_kernel,
        out_shape=jax.ShapeDtypeStruct((TOK, NY * WIDTH), BF16),
        in_specs=[IN_VMEM],
        out_specs=IN_VMEM,
        name="merge",
        **options(2),
    )(parts)


def on_device(
    queries, keys_edit, values_edit, keys_source, values_source, edit_mask, inject_gate, step_index
):
    x, y = lax.axis_index("x"), 2 * lax.axis_index("yh") + lax.axis_index("yl")
    where = jnp.stack([y, x, lax.axis_index("yh") * NX + x]).astype(jnp.int32)
    mixed = mix(
        where, step_index, queries, keys_edit, values_edit, keys_source, values_source, edit_mask, inject_gate
    )
    got = [shift_y(mixed[d], d) for d in (1, 3, 2)]
    near = jnp.concatenate([mixed[0]] + [v[: 2 * TOK] for v in got], axis=0)
    query = jnp.concatenate([mixed[NY], got[0][2 * TOK :], got[2][2 * TOK :], got[1][2 * TOK :]], axis=0)
    far = swap_core(near)
    q_parts = [query] + [shift_x(query, d) for d in range(1, NX)]
    near0, far0 = near, far
    for step in range(NZ // 2 - 1):
        near, far = ring_z(near), ring_z(far)
        if step == 0:
            near, *q_parts = lax.optimization_barrier([near, *q_parts])
            state = flash(q_parts, [near0, far0], None, None)
        state = flash(q_parts, [near, swap_core(near)], state, None)
        state = flash(q_parts, [far, swap_core(far)], state, None)
    near = ring_z(near)
    parts = flash(q_parts, [near, swap_core(near)], state, where)
    parts = lax.all_to_all(parts, ("yl", "yh", "x"), 0, 0, tiled=True)
    return merge(parts)


def solution(mesh):
    mesh = Mesh(mesh.devices.reshape(SIZES), AXES)
    tokens = P(AXES, None)
    in_specs = (tokens,) * 5 + (P(("yl", "z", "core")), P(), P())
    return jax.shard_map(on_device, mesh=mesh, in_specs=in_specs, out_specs=tokens, check_vma=False)
```

time: 247 us -> 91.6 us (0.37)
  waiting for transfers between devices: 123 us -> 16.6 us
  matrix products: 28.2 us -> 0 us
  local copies, waits for them, and re-layouts: 25.9 us -> 0.04 us
  starting transfers between devices: 17.8 us -> 34.9 us
  Pallas kernels: 0 us -> 16.8 us
  between operations: 14.1 us -> 0.85 us
  other arithmetic: 13.4 us -> 1.59 us
  blocking collectives: 23.2 us -> 20.6 us
    all_gather x2 -> x0, waiting for transfers between devices: 99.3 us -> none  [the longest x1 62.8 us: attend_gathered(): lax.all_gather(key_group, 'seq', axis=0, tiled=True)]
    ppermute x0 -> x21, starting transfers between devices: none -> 34.9 us  [permute(): return lax.ppermute(value, AXES, pairs)]
    dot_general x3 -> x0, matrix products: 28.2 us -> none  [the longest x1 14.9 us: fold_step(): jnp.einsum('qhd,khd->hqk', query_heads, key_heads, preferred_element_type...]
    all_to_all x4 -> x0, waiting for transfers between devices: 22.6 us -> none  [the longest x1 7.22 us: on_device(): lax.all_to_all(values_edit, 'ulysses', split_axis=1, concat_axis=0, tiled...]
    all_to_all x4 -> x0, starting transfers between devices: 17.7 us -> none  [the longest x1 7.48 us: on_device(): lax.all_to_all(keys_edit, 'ulysses', split_axis=1, concat_axis=0, tiled=T...]
    all_gather x2 -> x0, local copies, waits for them, and re-layouts: 17.2 us -> none  [the longest x1 8.62 us: attend_gathered(): lax.all_gather(key_group, 'seq', axis=0, tiled=True)]
    pallas_call x0 -> x10, Pallas kernels: none -> 16.8 us  [the longest x8 12.5 us: flash(): pl.pallas_call(functools.partial(flash_kernel, first, last, len(kv_blocks...]
    ppermute x0 -> x21, waiting for transfers between devices: none -> 16.6 us  [permute(): return lax.ppermute(value, AXES, pairs)]
  transfers between devices with their start and end apart: 6 -> 21, of which waited for: 6 -> 8; matrix products, arithmetic and copies ran while one was open for 17% -> 0% of each run, Pallas kernels for 0% -> 11%
where the time goes in v2:
time: 91.6 us; the launch traced here: 91.4 us
  starting transfers between devices  34.9 us (38%)
  blocking collectives  20.6 us (22%)
  Pallas kernels  16.8 us (18%)
  waiting for transfers between devices  16.6 us (18%)
  other arithmetic  1.59 us (2%)
    ppermute x21, starting transfers between devices, permute(): return lax.ppermute(value, AXES, pairs)  34.9 us
    all_to_all x1, blocking collectives, on_device(): parts = lax.all_to_all(parts, ('yl', 'yh', 'x'), 0, 0, tiled=True)  20.6 us
    ppermute x21, waiting for transfers between devices, permute(): return lax.ppermute(value, AXES, pairs)  16.6 us
    pallas_call x8, Pallas kernels, flash(): pl.pallas_call(functools.partial(flash_kernel, first, last, len(kv_blocks...  12.5 us
    pallas_call x1, Pallas kernels, mix(): pl.pallas_call(mix_kernel, out_shape=[jax.ShapeDtypeStruct((n * TOK, WIDT...  3 us
  transfers between devices with their start and end apart: 21, of which 8 were waited for; matrix products, arithmetic and copies ran while one was open for 0% of the time, Pallas kernels for 11%

profile of v2, /device:TPU:1, one launch (start us, length us, event | category | flops | bytes accessed | tf_op | source)
XLA Modules:
  0.0 91.4 jit_solution(14553614793706901524)
XLA Ops:
  0.7 0.6 pad_add_fusion.where_ref.refs_0_
  1.3 3.0 %mix.1 = (bf16[64,768]{1,0:T(8,128)(2,1)}, bf16[96,768]{1,0:T(8,128)(2,1)}, bf16[96,768]{1,0:T(8,128)(2,1)}, bf16[96,768]{1,0:T(8,128)(2,1)}, bf16[32,768]{1,0:T(8,128)(2,1)}) custom-call(s32[3]{0:T(128)} %pad_add_fusion.where_ref.refs_0_, s32[1]{0:T(128)S(6)} %copy.9.step_ref, bf16[32,3072]{1,0:T(8,128)(2,1)} %q_hbm.1, bf16[32,3072]{1,0:T(8,128)(2,1)} %ke_hbm.1, ...), custom_call_target="tpu_custom_call" | custom-call | flops 2000000000 | bytes 6000000 | tf_op jit(solution)/shard_map/mix/pallas_call | solution.py:102
  4.3 0.0 copy-start.1
  4.3 2.2 %collective-permute-start = (bf16[96,768]{1,0:T(8,128)(2,1)}, bf16[96,768]{1,0:T(8,128)(2,1)S(1)}, u32[]{:S(2)}, u32[]{:S(2)}) collective-permute-start(bf16[96,768]{1,0:T(8,128)(2,1)} %get-tuple-element.30), channel_id=1, source_target_pairs={{0,128},{1,129},{2,130},{3,131},{4,132},{5,133},{6,134},{7,135},{8... | collective-permute-start | bytes 442376 | tf_op jit(solution)/shard_map/ppermute | solution.py:36
  6.5 1.5 %collective-permute-start.1 = (bf16[96,768]{1,0:T(8,128)(2,1)}, bf16[96,768]{1,0:T(8,128)(2,1)S(1)}, u32[]{:S(2)}, u32[]{:S(2)}) collective-permute-start(bf16[96,768]{1,0:T(8,128)(2,1)} %get-tuple-element.31), channel_id=1, source_target_pairs={{0,132},{1,133},{2,134},{3,135},{4,128},{5,129},{6,130},{7,131},{8... | collective-permute-start | bytes 442376 | tf_op jit(solution)/shard_map/ppermute | solution.py:36
  8.1 1.6 %collective-permute-start.2 = (bf16[96,768]{1,0:T(8,128)(2,1)}, bf16[96,768]{1,0:T(8,128)(2,1)S(1)}, u32[]{:S(2)}, u32[]{:S(2)}) collective-permute-start(bf16[96,768]{1,0:T(8,128)(2,1)} %get-tuple-element.32), channel_id=1, source_target_pairs={{0,4},{1,5},{2,6},{3,7},{4,0},{5,1},{6,2},{7,3},{8,12},{9,13},{10,... | collective-permute-start | bytes 442376 | tf_op jit(solution)/shard_map/ppermute | solution.py:36
  9.6 1.1 %collective-permute-done = bf16[96,768]{1,0:T(8,128)(2,1)S(1)} collective-permute-done((bf16[96,768]{1,0:T(8,128)(2,1)}, bf16[96,768]{1,0:T(8,128)(2,1)S(1)}, u32[]{:S(2)}, u32[]{:S(2)}) %collective-permute-start) | collective-permute-done | bytes 147488 | tf_op jit(solution)/shard_map/ppermute | solution.py:36
  10.7 0.0 collective-permute-done.1
  10.8 4.3 %collective-permute-done.2 = bf16[96,768]{1,0:T(8,128)(2,1)S(1)} collective-permute-done((bf16[96,768]{1,0:T(8,128)(2,1)}, bf16[96,768]{1,0:T(8,128)(2,1)S(1)}, u32[]{:S(2)}, u32[]{:S(2)}) %collective-permute-start.2) | collective-permute-done | bytes 147488 | tf_op jit(solution)/shard_map/ppermute | solution.py:36
  15.1 0.9 %pad_maximum_fusion.refs_4_ = bf16[256,768]{1,0:T(8,128)(2,1)S(1)} fusion(bf16[64,768]{1,0:T(8,128)(2,1)S(1)} %slice.26, bf16[64,768]{1,0:T(8,128)(2,1)S(1)} %slice.25, bf16[64,768]{1,0:T(8,128)(2,1)S(1)} %slice.24, bf16[64,768]{1,0:T(8,128)(2,1)} %get-tuple-element.29), kind=kLoop, calls=%fused_computation | loop fusion | flops 1572864 | bytes 786432 | tf_op jit(solution)/shard_map/concatenate | solution.py:236
  16.0 2.7 %collective-permute-start.11 = (bf16[256,768]{1,0:T(8,128)(2,1)S(1)}, bf16[256,768]{1,0:T(8,128)(2,1)S(1)}, u32[]{:S(2)}, u32[]{:S(2)}) collective-permute-start(bf16[256,768]{1,0:T(8,128)(2,1)S(1)} %pad_maximum_fusion.refs_4_), channel_id=1, source_target_pairs={{0,8},{1,9},{2,10},{3,11},{4,12},{5,13},{6,14},{7,15},{8,0},{9,1},... | collective-permute-start | bytes 1179656 | tf_op jit(solution)/shard_map/ppermute | solution.py:36
  18.8 5.2 %collective-permute-start.3 = (bf16[256,768]{1,0:T(8,128)(2,1)S(1)}, bf16[256,768]{1,0:T(8,128)(2,1)S(1)}, u32[]{:S(2)}, u32[]{:S(2)}) collective-permute-start(bf16[256,768]{1,0:T(8,128)(2,1)S(1)} %pad_maximum_fusion.refs_4_), channel_id=1, source_target_pairs={{0,16},{1,17},{2,18},{3,19},{4,20},{5,21},{6,22},{7,23},{8,120},{9... | collective-permute-start | bytes 1179656 | tf_op jit(solution)/shard_map/ppermute | solution.py:36
  23.9 0.0 copy-done.1
  24.0 1.3 %collective-permute-start.4 = (bf16[128,768]{1,0:T(8,128)(2,1)S(1)}, bf16[128,768]{1,0:T(8,128)(2,1)S(1)}, u32[]{:S(2)}, u32[]{:S(2)}) collective-permute-start(bf16[128,768]{1,0:T(8,128)(2,1)S(1)} %pad_maximum_fusion.1.refs_0_.refs_1_), channel_id=1, source_target_pairs={{0,1},{1,2},{2,3},{3,0},{4,5},{5,6},{6,7},{7,4},{8,9},{9,10},{10,1... | collective-permute-start | bytes 589832 | tf_op jit(solution)/shard_map/ppermute | solution.py:36
  25.3 2.5 %collective-permute-start.5 = (bf16[128,768]{1,0:T(8,128)(2,1)S(1)}, bf16[128,768]{1,0:T(8,128)(2,1)S(1)}, u32[]{:S(2)}, u32[]{:S(2)}) collective-permute-start(bf16[128,768]{1,0:T(8,128)(2,1)S(1)} %pad_maximum_fusion.1.refs_0_.refs_1_), channel_id=1, source_target_pairs={{0,2},{1,3},{2,0},{3,1},{4,6},{5,7},{6,4},{7,5},{8,10},{9,11},{10,... | collective-permute-start | bytes 589832 | tf_op jit(solution)/shard_map/ppermute | solution.py:36
  27.7 1.2 %collective-permute-start.6 = (bf16[128,768]{1,0:T(8,128)(2,1)S(1)}, bf16[128,768]{1,0:T(8,128)(2,1)S(1)}, u32[]{:S(2)}, u32[]{:S(2)}) collective-permute-start(bf16[128,768]{1,0:T(8,128)(2,1)S(1)} %pad_maximum_fusion.1.refs_0_.refs_1_), channel_id=1, source_target_pairs={{0,3},{1,0},{2,1},{3,2},{4,7},{5,4},{6,5},{7,6},{8,11},{9,8},{10,9... | collective-permute-start | bytes 589832 | tf_op jit(solution)/shard_map/ppermute | solution.py:36
  28.9 0.0 collective-permute-done.11.refs_5_
  28.9 0.7 collective-permute-start.12
  29.6 2.6 %collective-permute-done.4.refs_1_.refs_2_ = bf16[128,768]{1,0:T(8,128)(2,1)S(1)} collective-permute-done((bf16[128,768]{1,0:T(8,128)(2,1)S(1)}, bf16[128,768]{1,0:T(8,128)(2,1)S(1)}, u32[]{:S(2)}, u32[]{:S(2)}) %collective-permute-start.4) | collective-permute-done | bytes 196640 | tf_op jit(solution)/shard_map/ppermute | solution.py:36
  32.2 1.8 %collective-permute-done.5.refs_2_.refs_3_ = bf16[128,768]{1,0:T(8,128)(2,1)S(1)} collective-permute-done((bf16[128,768]{1,0:T(8,128)(2,1)S(1)}, bf16[128,768]{1,0:T(8,128)(2,1)S(1)}, u32[]{:S(2)}, u32[]{:S(2)}) %collective-permute-start.5) | collective-permute-done | bytes 196640 | tf_op jit(solution)/shard_map/ppermute | solution.py:36
  34.0 0.2 collective-permute-done.6.refs_3_.refs_4_
  34.2 0.0 collective-permute-done.3.refs_4_
  34.2 3.6 %collective-permute-start.7 = (bf16[256,768]{1,0:T(8,128)(2,1)S(1)}, bf16[256,768]{1,0:T(8,128)(2,1)S(1)}, u32[]{:S(2)}, u32[]{:S(2)}) collective-permute-start(bf16[256,768]{1,0:T(8,128)(2,1)S(1)} %collective-permute-done.3.refs_4_), channel_id=1, source_target_pairs={{0,16},{1,17},{2,18},{3,19},{4,20},{5,21},{6,22},{7,23},{8,120},{9... | collective-permute-start | bytes 1179656 | tf_op jit(solution)/shard_map/ppermute | solution.py:36
  37.8 0.0 collective-permute-start.20
  37.8 0.0 collective-permute-done.12.refs_4_
  37.8 0.5 collective-permute-start.19
  38.3 0.2 collective-permute-start.13
  38.5 4.0 %collective-permute-done.7.refs_4_ = bf16[256,768]{1,0:T(8,128)(2,1)S(1)} collective-permute-done((bf16[256,768]{1,0:T(8,128)(2,1)S(1)}, bf16[256,768]{1,0:T(8,128)(2,1)S(1)}, u32[]{:S(2)}, u32[]{:S(2)}) %collective-permute-start.7) | collective-permute-done | bytes 393248 | tf_op jit(solution)/shard_map/ppermute | solution.py:36
  42.5 3.1 %collective-permute-start.8 = (bf16[256,768]{1,0:T(8,128)(2,1)S(1)}, bf16[256,768]{1,0:T(8,128)(2,1)S(1)}, u32[]{:S(2)}, u32[]{:S(2)}) collective-permute-start(bf16[256,768]{1,0:T(8,128)(2,1)S(1)} %collective-permute-done.7.refs_4_), channel_id=1, source_target_pairs={{0,16},{1,17},{2,18},{3,19},{4,20},{5,21},{6,22},{7,23},{8,120},{9... | collective-permute-start | bytes 1179656 | tf_op jit(solution)/shard_map/ppermute | solution.py:36
  45.7 1.4 %flash.8 = (f32[768,512]{1,0:T(8,128)S(1)}, f32[48,512]{1,0:T(8,128)S(1)}) custom-call(bf16[128,768]{1,0:T(8,128)(2,1)S(1)} %pad_maximum_fusion.1.refs_0_.refs_1_, bf16[128,768]{1,0:T(8,128)(2,1)S(1)} %collective-permute-done.4.refs_1_.refs_2_, bf16[128,768]{1,0:T(8,128)(2,1)S(1)} %collective-permute-done.5.refs_2_.refs_3_, ...), custom_call_target="tpu_custom_call" | custom-call | flops 2652000000 | bytes 7956000 | tf_op jit(solution)/shard_map/flash/pallas_call | solution.py:187
  47.1 0.3 collective-permute-start.18
  47.3 0.0 collective-permute-done.20.refs_5_
  47.3 1.5 %flash.9 = (f32[768,512]{1,0:T(8,128)S(1)}, f32[48,512]{1,0:T(8,128)S(1)}) custom-call(bf16[128,768]{1,0:T(8,128)(2,1)S(1)} %pad_maximum_fusion.1.refs_0_.refs_1_, bf16[128,768]{1,0:T(8,128)(2,1)S(1)} %collective-permute-done.4.refs_1_.refs_2_, bf16[128,768]{1,0:T(8,128)(2,1)S(1)} %collective-permute-done.5.refs_2_.refs_3_, ...), custom_call_target="tpu_custom_call" | custom-call | flops 2652000000 | bytes 7956000 | tf_op jit(solution)/shard_map/flash/pallas_call | solution.py:187
  48.8 0.0 collective-permute-done.13.refs_4_
  48.8 0.6 collective-permute-start.17
  49.4 1.1 %collective-permute-start.14 = (bf16[256,768]{1,0:T(8,128)(2,1)S(1)}, bf16[256,768]{1,0:T(8,128)(2,1)S(1)}, u32[]{:S(2)}, u32[]{:S(2)}) collective-permute-start(bf16[256,768]{1,0:T(8,128)(2,1)S(1)} %collective-permute-done.13.refs_4_), channel_id=1, source_target_pairs={{0,16},{1,17},{2,18},{3,19},{4,20},{5,21},{6,22},{7,23},{8,120},{9... | collective-permute-start | bytes 1179656 | tf_op jit(solution)/shard_map/ppermute | solution.py:36
  50.5 0.4 collective-permute-done.8.refs_4_
  51.0 2.3 %collective-permute-start.16 = (bf16[256,768]{1,0:T(8,128)(2,1)S(1)}, bf16[256,768]{1,0:T(8,128)(2,1)S(1)}, u32[]{:S(2)}, u32[]{:S(2)}) collective-permute-start(bf16[256,768]{1,0:T(8,128)(2,1)S(1)} %collective-permute-done.8.refs_4_), channel_id=1, source_target_pairs={{0,8},{1,9},{2,10},{3,11},{4,12},{5,13},{6,14},{7,15},{8,0},{9,1},... | collective-permute-start | bytes 1179656 | tf_op jit(solution)/shard_map/ppermute | solution.py:36
  53.2 0.0 collective-permute-done.19.refs_5_
  53.2 1.2 %collective-permute-start.9 = (bf16[256,768]{1,0:T(8,128)(2,1)S(1)}, bf16[256,768]{1,0:T(8,128)(2,1)S(1)}, u32[]{:S(2)}, u32[]{:S(2)}) collective-permute-start(bf16[256,768]{1,0:T(8,128)(2,1)S(1)} %collective-permute-done.8.refs_4_), channel_id=1, source_target_pairs={{0,16},{1,17},{2,18},{3,19},{4,20},{5,21},{6,22},{7,23},{8,120},{9... | collective-permute-start | bytes 1179656 | tf_op jit(solution)/shard_map/ppermute | solution.py:36
  54.4 1.5 %flash.10 = (f32[768,512]{1,0:T(8,128)S(1)}, f32[48,512]{1,0:T(8,128)S(1)}) custom-call(bf16[128,768]{1,0:T(8,128)(2,1)S(1)} %pad_maximum_fusion.1.refs_0_.refs_1_, bf16[128,768]{1,0:T(8,128)(2,1)S(1)} %collective-permute-done.4.refs_1_.refs_2_, bf16[128,768]{1,0:T(8,128)(2,1)S(1)} %collective-permute-done.5.refs_2_.refs_3_, ...), custom_call_target="tpu_custom_call" | custom-call | flops 2652000000 | bytes 7956000 | tf_op jit(solution)/shard_map/flash/pallas_call | solution.py:187
  55.9 0.0 collective-permute-done.18.refs_5_
  55.9 1.5 %flash.11 = (f32[768,512]{1,0:T(8,128)S(1)}, f32[48,512]{1,0:T(8,128)S(1)}) custom-call(bf16[128,768]{1,0:T(8,128)(2,1)S(1)} %pad_maximum_fusion.1.refs_0_.refs_1_, bf16[128,768]{1,0:T(8,128)(2,1)S(1)} %collective-permute-done.4.refs_1_.refs_2_, bf16[128,768]{1,0:T(8,128)(2,1)S(1)} %collective-permute-done.5.refs_2_.refs_3_, ...), custom_call_target="tpu_custom_call" | custom-call | flops 2652000000 | bytes 7956000 | tf_op jit(solution)/shard_map/flash/pallas_call | solution.py:187
  57.4 0.0 collective-permute-done.14.refs_4_
  57.4 1.1 %collective-permute-start.15 = (bf16[256,768]{1,0:T(8,128)(2,1)S(1)}, bf16[256,768]{1,0:T(8,128)(2,1)S(1)}, u32[]{:S(2)}, u32[]{:S(2)}) collective-permute-start(bf16[256,768]{1,0:T(8,128)(2,1)S(1)} %collective-permute-done.14.refs_4_), channel_id=1, source_target_pairs={{0,8},{1,9},{2,10},{3,11},{4,12},{5,13},{6,14},{7,15},{8,0},{9,1},... | collective-permute-start | bytes 1179656 | tf_op jit(solution)/shard_map/ppermute | solution.py:36
  58.5 2.1 %collective-permute-done.9.refs_5_ = bf16[256,768]{1,0:T(8,128)(2,1)S(1)} collective-permute-done((bf16[256,768]{1,0:T(8,128)(2,1)S(1)}, bf16[256,768]{1,0:T(8,128)(2,1)S(1)}, u32[]{:S(2)}, u32[]{:S(2)}) %collective-permute-start.9) | collective-permute-done | bytes 393248 | tf_op jit(solution)/shard_map/ppermute | solution.py:36
  60.5 2.2 %collective-permute-start.10 = (bf16[256,768]{1,0:T(8,128)(2,1)S(1)}, bf16[256,768]{1,0:T(8,128)(2,1)S(1)}, u32[]{:S(2)}, u32[]{:S(2)}) collective-permute-start(bf16[256,768]{1,0:T(8,128)(2,1)S(1)} %collective-permute-done.9.refs_5_), channel_id=1, source_target_pairs={{0,8},{1,9},{2,10},{3,11},{4,12},{5,13},{6,14},{7,15},{8,0},{9,1},... | collective-permute-start | bytes 1179656 | tf_op jit(solution)/shard_map/ppermute | solution.py:36
  62.7 0.0 collective-permute-done.17.refs_5_
  62.7 1.5 %flash.12 = (f32[768,512]{1,0:T(8,128)S(1)}, f32[48,512]{1,0:T(8,128)S(1)}) custom-call(bf16[128,768]{1,0:T(8,128)(2,1)S(1)} %pad_maximum_fusion.1.refs_0_.refs_1_, bf16[128,768]{1,0:T(8,128)(2,1)S(1)} %collective-permute-done.4.refs_1_.refs_2_, bf16[128,768]{1,0:T(8,128)(2,1)S(1)} %collective-permute-done.5.refs_2_.refs_3_, ...), custom_call_target="tpu_custom_call" | custom-call | flops 2652000000 | bytes 7956000 | tf_op jit(solution)/shard_map/flash/pallas_call | solution.py:187
  64.2 0.0 collective-permute-done.16.refs_5_
  64.2 1.5 %flash.13 = (f32[768,512]{1,0:T(8,128)S(1)}, f32[48,512]{1,0:T(8,128)S(1)}) custom-call(bf16[128,768]{1,0:T(8,128)(2,1)S(1)} %pad_maximum_fusion.1.refs_0_.refs_1_, bf16[128,768]{1,0:T(8,128)(2,1)S(1)} %collective-permute-done.4.refs_1_.refs_2_, bf16[128,768]{1,0:T(8,128)(2,1)S(1)} %collective-permute-done.5.refs_2_.refs_3_, ...), custom_call_target="tpu_custom_call" | custom-call | flops 2652000000 | bytes 7956000 | tf_op jit(solution)/shard_map/flash/pallas_call | solution.py:187
  65.7 0.0 collective-permute-done.15.refs_5_
  65.7 0.0 copy-start
  65.7 1.5 %flash.14 = (f32[768,512]{1,0:T(8,128)S(1)}, f32[48,512]{1,0:T(8,128)S(1)}) custom-call(bf16[128,768]{1,0:T(8,128)(2,1)S(1)} %pad_maximum_fusion.1.refs_0_.refs_1_, bf16[128,768]{1,0:T(8,128)(2,1)S(1)} %collective-permute-done.4.refs_1_.refs_2_, bf16[128,768]{1,0:T(8,128)(2,1)S(1)} %collective-permute-done.5.refs_2_.refs_3_, ...), custom_call_target="tpu_custom_call" | custom-call | flops 2652000000 | bytes 7956000 | tf_op jit(solution)/shard_map/flash/pallas_call | solution.py:187
  67.1 0.0 collective-permute-done.10.refs_6_
  67.2 0.0 copy-done
  67.2 2.3 %flash.15 = bf16[512,896]{1,0:T(8,128)(2,1)S(1)} custom-call(s32[3]{0:T(128)S(1)} %copy-done, bf16[128,768]{1,0:T(8,128)(2,1)S(1)} %pad_maximum_fusion.1.refs_0_.refs_1_, bf16[128,768]{1,0:T(8,128)(2,1)S(1)} %collective-permute-done.4.refs_1_.refs_2_, bf16[128,768]{1,0:T(8,128)(2,1)S(1)} %collective-permute-done.5.refs_2_.refs_3_, ...), custom_call_target="tpu_custom_call" | custom-call | flops 2652000000 | bytes 7956000 | tf_op jit(solution)/shard_map/flash/pallas_call | solution.py:187
  69.4 20.6 %all_to_all.11 = bf16[16,32,896]{2,1,0:T(8,128)(2,1)S(1)} all-to-all(bf16[16,32,896]{2,1,0:T(8,128)(2,1)S(1)} %bitcast.7), channel_id=1, replica_groups=mesh['yl'=2,'z'=8,'core'=2,'yh'=2,'x'=4] {'yl','yh','x'}, dimensions={0} | all-to-all | bytes 1835008 | tf_op jit(solution)/shard_map/all_to_all | solution.py:250
  90.1 1.3 %merge.1 = bf16[32,3072]{1,0:T(8,128)(2,1)} custom-call(bf16[512,896]{1,0:T(8,128)(2,1)S(1)} %bitcast.8), custom_call_target="tpu_custom_call" | custom-call | flops 2000000000 | bytes 6000000 | tf_op jit(solution)/shard_map/merge/pallas_call | solution.py:217
  (7 shorter events, 0.1 us)
Async XLA Ops:
  4.3 19.6 %copy-start.1 = (bf16[32,768]{1,0:T(8,128)(2,1)S(1)}, bf16[32,768]{1,0:T(8,128)(2,1)}, u32[]{:S(2)}) copy-start(bf16[32,768]{1,0:T(8,128)(2,1)} %get-tuple-element.33) | copy-start | bytes 147460
  4.3 6.4 %collective-permute-start = (bf16[96,768]{1,0:T(8,128)(2,1)}, bf16[96,768]{1,0:T(8,128)(2,1)S(1)}, u32[]{:S(2)}, u32[]{:S(2)}) collective-permute-start(bf16[96,768]{1,0:T(8,128)(2,1)} %get-tuple-element.30), channel_id=1, source_target_pairs={{0,128},{1,129},{2,130},{3,131},{4,132},{5,133},{6,134},{7,135},{8... | collective-permute-start | bytes 442376 | tf_op jit(solution)/shard_map/ppermute | solution.py:36
  6.5 4.2 %collective-permute-start.1 = (bf16[96,768]{1,0:T(8,128)(2,1)}, bf16[96,768]{1,0:T(8,128)(2,1)S(1)}, u32[]{:S(2)}, u32[]{:S(2)}) collective-permute-start(bf16[96,768]{1,0:T(8,128)(2,1)} %get-tuple-element.31), channel_id=1, source_target_pairs={{0,132},{1,133},{2,134},{3,135},{4,128},{5,129},{6,130},{7,131},{8... | collective-permute-start | bytes 442376 | tf_op jit(solution)/shard_map/ppermute | solution.py:36
  8.1 7.0 %collective-permute-start.2 = (bf16[96,768]{1,0:T(8,128)(2,1)}, bf16[96,768]{1,0:T(8,128)(2,1)S(1)}, u32[]{:S(2)}, u32[]{:S(2)}) collective-permute-start(bf16[96,768]{1,0:T(8,128)(2,1)} %get-tuple-element.32), channel_id=1, source_target_pairs={{0,4},{1,5},{2,6},{3,7},{4,0},{5,1},{6,2},{7,3},{8,12},{9,13},{10,... | collective-permute-start | bytes 442376 | tf_op jit(solution)/shard_map/ppermute | solution.py:36
  16.0 12.8 %collective-permute-start.11 = (bf16[256,768]{1,0:T(8,128)(2,1)S(1)}, bf16[256,768]{1,0:T(8,128)(2,1)S(1)}, u32[]{:S(2)}, u32[]{:S(2)}) collective-permute-start(bf16[256,768]{1,0:T(8,128)(2,1)S(1)} %pad_maximum_fusion.refs_4_), channel_id=1, source_target_pairs={{0,8},{1,9},{2,10},{3,11},{4,12},{5,13},{6,14},{7,15},{8,0},{9,1},... | collective-permute-start | bytes 1179656 | tf_op jit(solution)/shard_map/ppermute | solution.py:36
  18.8 15.4 %collective-permute-start.3 = (bf16[256,768]{1,0:T(8,128)(2,1)S(1)}, bf16[256,768]{1,0:T(8,128)(2,1)S(1)}, u32[]{:S(2)}, u32[]{:S(2)}) collective-permute-start(bf16[256,768]{1,0:T(8,128)(2,1)S(1)} %pad_maximum_fusion.refs_4_), channel_id=1, source_target_pairs={{0,16},{1,17},{2,18},{3,19},{4,20},{5,21},{6,22},{7,23},{8,120},{9... | collective-permute-start | bytes 1179656 | tf_op jit(solution)/shard_map/ppermute | solution.py:36
  24.0 8.2 %collective-permute-start.4 = (bf16[128,768]{1,0:T(8,128)(2,1)S(1)}, bf16[128,768]{1,0:T(8,128)(2,1)S(1)}, u32[]{:S(2)}, u32[]{:S(2)}) collective-permute-start(bf16[128,768]{1,0:T(8,128)(2,1)S(1)} %pad_maximum_fusion.1.refs_0_.refs_1_), channel_id=1, source_target_pairs={{0,1},{1,2},{2,3},{3,0},{4,5},{5,6},{6,7},{7,4},{8,9},{9,10},{10,1... | collective-permute-start | bytes 589832 | tf_op jit(solution)/shard_map/ppermute | solution.py:36
  25.3 8.7 %collective-permute-start.5 = (bf16[128,768]{1,0:T(8,128)(2,1)S(1)}, bf16[128,768]{1,0:T(8,128)(2,1)S(1)}, u32[]{:S(2)}, u32[]{:S(2)}) collective-permute-start(bf16[128,768]{1,0:T(8,128)(2,1)S(1)} %pad_maximum_fusion.1.refs_0_.refs_1_), channel_id=1, source_target_pairs={{0,2},{1,3},{2,0},{3,1},{4,6},{5,7},{6,4},{7,5},{8,10},{9,11},{10,... | collective-permute-start | bytes 589832 | tf_op jit(solution)/shard_map/ppermute | solution.py:36
  27.7 6.5 %collective-permute-start.6 = (bf16[128,768]{1,0:T(8,128)(2,1)S(1)}, bf16[128,768]{1,0:T(8,128)(2,1)S(1)}, u32[]{:S(2)}, u32[]{:S(2)}) collective-permute-start(bf16[128,768]{1,0:T(8,128)(2,1)S(1)} %pad_maximum_fusion.1.refs_0_.refs_1_), channel_id=1, source_target_pairs={{0,3},{1,0},{2,1},{3,2},{4,7},{5,4},{6,5},{7,6},{8,11},{9,8},{10,9... | collective-permute-start | bytes 589832 | tf_op jit(solution)/shard_map/ppermute | solution.py:36
  28.9 8.9 %collective-permute-start.12 = (bf16[256,768]{1,0:T(8,128)(2,1)S(1)}, bf16[256,768]{1,0:T(8,128)(2,1)S(1)}, u32[]{:S(2)}, u32[]{:S(2)}) collective-permute-start(bf16[256,768]{1,0:T(8,128)(2,1)S(1)} %collective-permute-done.11.refs_5_), channel_id=1, source_target_pairs={{0,16},{1,17},{2,18},{3,19},{4,20},{5,21},{6,22},{7,23},{8,120},{9... | collective-permute-start | bytes 1179656 | tf_op jit(solution)/shard_map/ppermute | solution.py:36
  34.2 8.3 %collective-permute-start.7 = (bf16[256,768]{1,0:T(8,128)(2,1)S(1)}, bf16[256,768]{1,0:T(8,128)(2,1)S(1)}, u32[]{:S(2)}, u32[]{:S(2)}) collective-permute-start(bf16[256,768]{1,0:T(8,128)(2,1)S(1)} %collective-permute-done.3.refs_4_), channel_id=1, source_target_pairs={{0,16},{1,17},{2,18},{3,19},{4,20},{5,21},{6,22},{7,23},{8,120},{9... | collective-permute-start | bytes 1179656 | tf_op jit(solution)/shard_map/ppermute | solution.py:36
  37.8 9.5 %collective-permute-start.20 = (bf16[256,768]{1,0:T(8,128)(2,1)S(1)}, bf16[256,768]{1,0:T(8,128)(2,1)S(1)}, u32[]{:S(2)}, u32[]{:S(2)}) collective-permute-start(bf16[256,768]{1,0:T(8,128)(2,1)S(1)} %collective-permute-done.3.refs_4_), channel_id=1, source_target_pairs={{0,8},{1,9},{2,10},{3,11},{4,12},{5,13},{6,14},{7,15},{8,0},{9,1},... | collective-permute-start | bytes 1179656 | tf_op jit(solution)/shard_map/ppermute | solution.py:36
  37.8 15.4 %collective-permute-start.19 = (bf16[256,768]{1,0:T(8,128)(2,1)S(1)}, bf16[256,768]{1,0:T(8,128)(2,1)S(1)}, u32[]{:S(2)}, u32[]{:S(2)}) collective-permute-start(bf16[256,768]{1,0:T(8,128)(2,1)S(1)} %collective-permute-done.12.refs_4_), channel_id=1, source_target_pairs={{0,8},{1,9},{2,10},{3,11},{4,12},{5,13},{6,14},{7,15},{8,0},{9,1},... | collective-permute-start | bytes 1179656 | tf_op jit(solution)/shard_map/ppermute | solution.py:36
  38.3 10.5 %collective-permute-start.13 = (bf16[256,768]{1,0:T(8,128)(2,1)S(1)}, bf16[256,768]{1,0:T(8,128)(2,1)S(1)}, u32[]{:S(2)}, u32[]{:S(2)}) collective-permute-start(bf16[256,768]{1,0:T(8,128)(2,1)S(1)} %collective-permute-done.12.refs_4_), channel_id=1, source_target_pairs={{0,16},{1,17},{2,18},{3,19},{4,20},{5,21},{6,22},{7,23},{8,120},{9... | collective-permute-start | bytes 1179656 | tf_op jit(solution)/shard_map/ppermute | solution.py:36
  42.5 8.4 %collective-permute-start.8 = (bf16[256,768]{1,0:T(8,128)(2,1)S(1)}, bf16[256,768]{1,0:T(8,128)(2,1)S(1)}, u32[]{:S(2)}, u32[]{:S(2)}) collective-permute-start(bf16[256,768]{1,0:T(8,128)(2,1)S(1)} %collective-permute-done.7.refs_4_), channel_id=1, source_target_pairs={{0,16},{1,17},{2,18},{3,19},{4,20},{5,21},{6,22},{7,23},{8,120},{9... | collective-permute-start | bytes 1179656 | tf_op jit(solution)/shard_map/ppermute | solution.py:36
  47.1 8.8 %collective-permute-start.18 = (bf16[256,768]{1,0:T(8,128)(2,1)S(1)}, bf16[256,768]{1,0:T(8,128)(2,1)S(1)}, u32[]{:S(2)}, u32[]{:S(2)}) collective-permute-start(bf16[256,768]{1,0:T(8,128)(2,1)S(1)} %collective-permute-done.7.refs_4_), channel_id=1, source_target_pairs={{0,8},{1,9},{2,10},{3,11},{4,12},{5,13},{6,14},{7,15},{8,0},{9,1},... | collective-permute-start | bytes 1179656 | tf_op jit(solution)/shard_map/ppermute | solution.py:36
  48.8 13.9 %collective-permute-start.17 = (bf16[256,768]{1,0:T(8,128)(2,1)S(1)}, bf16[256,768]{1,0:T(8,128)(2,1)S(1)}, u32[]{:S(2)}, u32[]{:S(2)}) collective-permute-start(bf16[256,768]{1,0:T(8,128)(2,1)S(1)} %collective-permute-done.13.refs_4_), channel_id=1, source_target_pairs={{0,8},{1,9},{2,10},{3,11},{4,12},{5,13},{6,14},{7,15},{8,0},{9,1},... | collective-permute-start | bytes 1179656 | tf_op jit(solution)/shard_map/ppermute | solution.py:36
  49.4 8.0 %collective-permute-start.14 = (bf16[256,768]{1,0:T(8,128)(2,1)S(1)}, bf16[256,768]{1,0:T(8,128)(2,1)S(1)}, u32[]{:S(2)}, u32[]{:S(2)}) collective-permute-start(bf16[256,768]{1,0:T(8,128)(2,1)S(1)} %collective-permute-done.13.refs_4_), channel_id=1, source_target_pairs={{0,16},{1,17},{2,18},{3,19},{4,20},{5,21},{6,22},{7,23},{8,120},{9... | collective-permute-start | bytes 1179656 | tf_op jit(solution)/shard_map/ppermute | solution.py:36
  51.0 13.2 %collective-permute-start.16 = (bf16[256,768]{1,0:T(8,128)(2,1)S(1)}, bf16[256,768]{1,0:T(8,128)(2,1)S(1)}, u32[]{:S(2)}, u32[]{:S(2)}) collective-permute-start(bf16[256,768]{1,0:T(8,128)(2,1)S(1)} %collective-permute-done.8.refs_4_), channel_id=1, source_target_pairs={{0,8},{1,9},{2,10},{3,11},{4,12},{5,13},{6,14},{7,15},{8,0},{9,1},... | collective-permute-start | bytes 1179656 | tf_op jit(solution)/shard_map/ppermute | solution.py:36
  53.2 7.3 %collective-permute-start.9 = (bf16[256,768]{1,0:T(8,128)(2,1)S(1)}, bf16[256,768]{1,0:T(8,128)(2,1)S(1)}, u32[]{:S(2)}, u32[]{:S(2)}) collective-permute-start(bf16[256,768]{1,0:T(8,128)(2,1)S(1)} %collective-permute-done.8.refs_4_), channel_id=1, source_target_pairs={{0,16},{1,17},{2,18},{3,19},{4,20},{5,21},{6,22},{7,23},{8,120},{9... | collective-permute-start | bytes 1179656 | tf_op jit(solution)/shard_map/ppermute | solution.py:36
  57.4 8.3 %collective-permute-start.15 = (bf16[256,768]{1,0:T(8,128)(2,1)S(1)}, bf16[256,768]{1,0:T(8,128)(2,1)S(1)}, u32[]{:S(2)}, u32[]{:S(2)}) collective-permute-start(bf16[256,768]{1,0:T(8,128)(2,1)S(1)} %collective-permute-done.14.refs_4_), channel_id=1, source_target_pairs={{0,8},{1,9},{2,10},{3,11},{4,12},{5,13},{6,14},{7,15},{8,0},{9,1},... | collective-permute-start | bytes 1179656 | tf_op jit(solution)/shard_map/ppermute | solution.py:36
  60.5 6.6 %collective-permute-start.10 = (bf16[256,768]{1,0:T(8,128)(2,1)S(1)}, bf16[256,768]{1,0:T(8,128)(2,1)S(1)}, u32[]{:S(2)}, u32[]{:S(2)}) collective-permute-start(bf16[256,768]{1,0:T(8,128)(2,1)S(1)} %collective-permute-done.9.refs_5_), channel_id=1, source_target_pairs={{0,8},{1,9},{2,10},{3,11},{4,12},{5,13},{6,14},{7,15},{8,0},{9,1},... | collective-permute-start | bytes 1179656 | tf_op jit(solution)/shard_map/ppermute | solution.py:36
  65.7 1.5 %copy-start = (s32[3]{0:T(128)S(1)}, s32[3]{0:T(128)}, u32[]{:S(2)}) copy-start(s32[3]{0:T(128)} %pad_add_fusion.where_ref.refs_0_) | copy-start | bytes 40

commit v3 on v2

v3 whole, which is shorter than its diff:
```python
import functools

import jax
import jax.numpy as jnp
from jax import lax
from jax.experimental import pallas as pl
from jax.experimental.pallas import tpu as pltpu
from jax.sharding import Mesh
from jax.sharding import PartitionSpec as P

AXES = ("yl", "z", "core", "yh", "xh", "xl")
SIZES = (2, 8, 2, 2, 2, 2)
GROUP_AXES = ("yl", "yh", "xl")
OUT_AXES = ("yl", "yh", "xh", "xl")
GROUPS, PARTS, NZ = 8, 2, 8
HEAD = 128
TOK = 32
HEADS = 3
WIDTH = HEADS * HEAD
TAIL = 128
LOG2E = 1.4426950408889634
SCALE2 = HEAD**-0.5 * LOG2E
VMEM_LIMIT = 32 * 1024 * 1024
BF16, F32 = jnp.bfloat16, jnp.float32
IN_VMEM = pl.BlockSpec(memory_space=pltpu.VMEM)
IN_SMEM = pl.BlockSpec(memory_space=pltpu.SMEM)


def ring_z(value):
    pairs = [(2 * z + c, 2 * ((z + 1 - 2 * c) % NZ) + c) for z in range(NZ) for c in range(2)]
    return lax.ppermute(value, ("z", "core"), pairs)


def swap(value, axis):
    return lax.ppermute(value, axis, [(0, 1), (1, 0)])


def options(us, limit=VMEM_LIMIT):
    return dict(
        compiler_params=pltpu.CompilerParams(vmem_limit_bytes=limit),
        cost_estimate=pl.CostEstimate(flops=int(us * 1.0e9), bytes_accessed=int(us * 3.0e6), transcendentals=0),
    )


def mix_kernel(step_ref, q_hbm, ke_hbm, ve_hbm, ks_hbm, vs_hbm, mask_hbm, gate_hbm, out, *refs):
    sources = (mask_hbm, gate_hbm, ke_hbm, ks_hbm, ve_hbm, vs_hbm, q_hbm)
    scratch, gates, sem = refs[:-2], refs[-2], refs[-1]
    copies = [pltpu.make_async_copy(a, b, sem.at[i]) for i, (a, b) in enumerate(zip(sources, scratch))]
    for copy in copies:
        copy.start()
    mask_ref, gate_ref, ke_ref, ks_ref, ve_ref, vs_ref, q_ref = scratch
    copies[0].wait()
    copies[1].wait()
    span = mask_ref.shape[1]
    uly = (lax.axis_index("yh") * 2 + lax.axis_index("xh")) * 2 + lax.axis_index("xl")
    lane = lax.broadcasted_iota(jnp.int32, (TOK, span), 1)
    row = lax.broadcasted_iota(jnp.int32, (TOK, span), 0)
    picked = jnp.where(lane == uly * TOK + row, jnp.broadcast_to(mask_ref[...], (TOK, span)), 0)
    inside = jnp.sum(picked, axis=1, keepdims=True) == 1
    step_lane = lax.broadcasted_iota(jnp.int32, gate_ref.shape, 1)
    at_step = jnp.sum(jnp.where(step_lane == step_ref[0], gate_ref[...], 0.0), axis=1, keepdims=True)
    gates[...] = jnp.broadcast_to(at_step, gates.shape)
    for n, (edit, source) in enumerate(((ke_ref, ks_ref), (ve_ref, vs_ref))):
        copies[2 + 2 * n].wait()
        copies[3 + 2 * n].wait()
        for head in range(GROUPS * HEADS):
            strength = gates[head : head + 1, :]
            cols = slice(head * HEAD, (head + 1) * HEAD)
            e = edit[:, cols].astype(F32)
            s = source[:, cols].astype(F32)
            mixed = jnp.where(inside, e, s + strength * (e - s)).astype(BF16)
            group, h = divmod(head, HEADS)
            out[group, n * TOK : (n + 1) * TOK, h * HEAD : (h + 1) * HEAD] = mixed
    copies[6].wait()
    for group in range(GROUPS):
        out[group, 2 * TOK :, :] = q_ref[:, group * WIDTH : (group + 1) * WIDTH]


def mix(step_index, queries, ke, ve, ks, vs, edit_mask, gate):
    edit_mask = edit_mask.reshape(1, -1)
    gate = gate.T
    big = pltpu.VMEM(queries.shape, BF16)
    return pl.pallas_call(
        mix_kernel,
        out_shape=jax.ShapeDtypeStruct((GROUPS, 3 * TOK, WIDTH), BF16),
        in_specs=[IN_SMEM] + [pl.BlockSpec(memory_space=pltpu.HBM)] * 7,
        out_specs=IN_VMEM,
        scratch_shapes=[pltpu.VMEM(edit_mask.shape, jnp.int32), pltpu.VMEM(gate.shape, F32)]
        + [big] * 5
        + [pltpu.VMEM((gate.shape[0], HEAD), F32)]
        + [pltpu.SemaphoreType.DMA((7,))],
        name="mix",
        **options(2, 60 * 1024 * 1024),
    )(step_index, queries, ke, ve, ks, vs, edit_mask, gate)


def flash_kernel(first, last, blocks, *refs):
    refs = list(refs)
    q_refs, refs = refs[:PARTS], refs[PARTS:]
    kv_refs, refs = refs[:blocks], refs[blocks:]
    if not first:
        acc_in, ml_in, refs = refs[0], refs[1], refs[2:]
    tile = 4 * TOK
    tiles = GROUPS // 4
    logs = [[] for _ in range(PARTS * tiles)]
    for h in range(HEADS):
        cols = slice(h * HEAD, (h + 1) * HEAD)
        pieces = [(r, at) for r in kv_refs for at in range(0, r.shape[0], 2 * TOK)]
        keys = jnp.concatenate([r[at : at + TOK, cols] for r, at in pieces], axis=0)
        values = jnp.concatenate([r[at + TOK : at + 2 * TOK, cols] for r, at in pieces], axis=0)
        for part in range(PARTS * tiles):
            at = slice(part * tile, (part + 1) * tile)
            begin = part % tiles * tile
            q = q_refs[part // tiles][begin : begin + tile, cols]
            s = lax.dot_general(keys, q, (((1,), (1,)), ((), ())), preferred_element_type=F32)
            top = jnp.max(s, axis=0, keepdims=True)
            if not first:
                old = ml_in[8 * h : 8 * h + 1, at]
                top = jnp.maximum(top, old)
            p = jnp.exp2((s - top) * SCALE2)
            total = jnp.sum(p, axis=0, keepdims=True)
            o = lax.dot_general(values, p.astype(BF16), (((0,), (0,)), ((), ())), preferred_element_type=F32)
            if not first:
                alpha = jnp.exp2((old - top) * SCALE2)
                total = total + alpha * ml_in[8 * h + 1 : 8 * h + 2, at]
                o = o + alpha * acc_in[cols, at]
            if last:
                o = (o * (1.0 / total)).T.astype(BF16)
                for e in range(4):
                    refs[0][target(part, e), cols] = o[e * TOK : (e + 1) * TOK, :]
                lse = top * SCALE2 + jnp.log2(total)
                hi = lse.astype(BF16).astype(F32)
                mid = (lse - hi).astype(BF16).astype(F32)
                logs[part].append((hi, mid, lse - hi - mid))
            else:
                refs[0][cols, at] = o
                refs[1][8 * h : 8 * h + 1, at] = top
                refs[1][8 * h + 1 : 8 * h + 2, at] = total
    if last:
        for part in range(PARTS * tiles):
            pad = jnp.zeros((TAIL - 3 * HEADS, tile), F32)
            columns = [log[i] for i in range(3) for log in logs[part]]
            packed = jnp.concatenate(columns + [pad], axis=0).T.astype(BF16)
            for e in range(4):
                refs[0][target(part, e), WIDTH:] = packed[e * TOK : (e + 1) * TOK, :]


def target(part, e):
    source = part % (GROUPS // 4) * 4 + e
    xh = lax.axis_index("xh")
    xh = xh if part < GROUPS // 4 else 1 - xh
    return pl.ds(((source // 2 * 2 + xh) * 2 + source % 2) * TOK, TOK)


def flash(q_parts, kv_blocks, state, last=False):
    queries = PARTS * GROUPS * TOK
    first = state is None
    if last:
        out_shape = jax.ShapeDtypeStruct((queries, WIDTH + TAIL), BF16)
    else:
        out_shape = [
            jax.ShapeDtypeStruct((WIDTH, queries), F32),
            jax.ShapeDtypeStruct((8 * HEADS, queries), F32),
        ]
    n = sum(b.shape[0] // 2 for b in kv_blocks)
    args = list(q_parts) + list(kv_blocks) + list(state or ())
    return pl.pallas_call(
        functools.partial(flash_kernel, first, last, len(kv_blocks)),
        out_shape=out_shape,
        in_specs=[IN_VMEM] * len(args),
        out_specs=IN_VMEM if last else [IN_VMEM, IN_VMEM],
        name="flash",
        **options(1 + n * 0.0023),
    )(*args)


def merge_kernel(in_ref, out_ref):
    lse = in_ref[:, WIDTH:].astype(F32)
    lse = lse[:, :HEADS] + lse[:, HEADS : 2 * HEADS] + lse[:, 2 * HEADS : 3 * HEADS]
    for group in range(GROUPS):
        first = group // 2 * 4 + group % 2
        rows = [slice(r * TOK, (r + 1) * TOK) for r in (first, first + 2)]
        top = jnp.maximum(lse[rows[0]], lse[rows[1]])
        weight = [jnp.exp2(lse[r] - top) for r in rows]
        scale = 1.0 / (weight[0] + weight[1])
        weight = [w * scale for w in weight]
        for h in range(HEADS):
            cols = slice(h * HEAD, (h + 1) * HEAD)
            total = functools.reduce(
                jnp.add, [w[:, h : h + 1] * in_ref[r, cols].astype(F32) for w, r in zip(weight, rows)]
            )
            at = group * WIDTH + h * HEAD
            out_ref[:, at : at + HEAD] = total.astype(BF16)


def merge(parts):
    return pl.pallas_call(
        merge_kernel,
        out_shape=jax.ShapeDtypeStruct((TOK, GROUPS * WIDTH), BF16),
        in_specs=[IN_VMEM],
        out_specs=IN_VMEM,
        name="merge",
        **options(2),
    )(parts)


def on_device(
    queries, keys_edit, values_edit, keys_source, values_source, edit_mask, inject_gate, step_index
):
    mixed = mix(
        step_index, queries, keys_edit, values_edit, keys_source, values_source, edit_mask, inject_gate
    )
    got = lax.all_to_all(mixed, GROUP_AXES, 0, 0, tiled=True)
    near = got[:, : 2 * TOK].reshape(-1, WIDTH)
    query = got[:, 2 * TOK :].reshape(-1, WIDTH)
    far = swap(near, "core")
    q_parts = [query, swap(query, "xh")]
    state = flash(q_parts, [near, far], None)
    for step in range(NZ // 2 - 1):
        near, far = ring_z(near), ring_z(far)
        state = flash(q_parts, [near, swap(near, "core")], state)
        state = flash(q_parts, [far, swap(far, "core")], state)
    near = ring_z(near)
    parts = flash(q_parts, [near, swap(near, "core")], state, last=True)
    parts = lax.all_to_all(parts, OUT_AXES, 0, 0, tiled=True)
    return merge(parts)


def solution(mesh):
    mesh = Mesh(mesh.devices.reshape(SIZES), AXES)
    tokens = P(AXES, None)
    in_specs = (tokens,) * 5 + (P(("yl", "z", "core")), P(), P())
    return jax.shard_map(on_device, mesh=mesh, in_specs=in_specs, out_specs=tokens, check_vma=False)
```

time: 91.6 us -> 83.1 us (0.907)
  blocking collectives: 20.6 us -> 31.2 us
  waiting for transfers between devices: 16.6 us -> 7.15 us
  starting transfers between devices: 34.9 us -> 27.9 us
  other arithmetic: 1.59 us -> 0 us
    all_to_all x1 -> x2, blocking collectives: 20.6 us -> 31.2 us  [the longest x1 15.8 us: on_device(): got = lax.all_to_all(mixed, GROUP_AXES, 0, 0, tiled=True)]
    ppermute x21 -> x16, waiting for transfers between devices: 16.6 us -> 7.15 us  [the longest x7 7.12 us: ring_z(): return lax.ppermute(value, ('z', 'core'), pairs)]
    ppermute x21 -> x16, starting transfers between devices: 34.9 us -> 27.9 us  [the longest x7 16.3 us: ring_z(): return lax.ppermute(value, ('z', 'core'), pairs)]
    pallas_call x2, Pallas kernels: 4.33 us -> 3.36 us  [the longest x1 2.23 us: mix(): pl.pallas_call(mix_kernel, out_shape=jax.ShapeDtypeStruct((GROUPS, 3 * TO...]
    concatenate x2 -> x0, other arithmetic: 0.94 us -> none  [the longest x1 0.92 us: on_device(): near = jnp.concatenate([mixed[0]] + [v[:2 * TOK] for v in got], axis=0)]
  transfers between devices with their start and end apart: 21 -> 16, of which waited for: 8 -> 4; matrix products, arithmetic and copies ran while one was open for 0% -> 0% of each run, Pallas kernels for 11% -> 13%
where the time goes in v3:
time: 83.1 us; the launch traced here: 82.9 us
  blocking collectives  31.2 us (38%)
  starting transfers between devices  27.9 us (34%)
  Pallas kernels  15.9 us (19%)
  waiting for transfers between devices  7.15 us (9%)
    ppermute x7, starting transfers between devices, ring_z(): return lax.ppermute(value, ('z', 'core'), pairs)  16.3 us
    all_to_all x1, blocking collectives, on_device(): got = lax.all_to_all(mixed, GROUP_AXES, 0, 0, tiled=True)  15.8 us
    all_to_all x1, blocking collectives, on_device(): parts = lax.all_to_all(parts, OUT_AXES, 0, 0, tiled=True)  15.4 us
    pallas_call x8, Pallas kernels, flash(): pl.pallas_call(functools.partial(flash_kernel, first, last, len(kv_blocks...  12.5 us
    ppermute x9, starting transfers between devices, swap(): return lax.ppermute(value, axis, [(0, 1), (1, 0)])  11.6 us
    ppermute x7, waiting for transfers between devices, ring_z(): return lax.ppermute(value, ('z', 'core'), pairs)  7.12 us
    pallas_call x1, Pallas kernels, mix(): pl.pallas_call(mix_kernel, out_shape=jax.ShapeDtypeStruct((GROUPS, 3 * TO...  2.23 us
  transfers between devices with their start and end apart: 16, of which 4 were waited for; matrix products, arithmetic and copies ran while one was open for 0% of the time, Pallas kernels for 13%

profile of v3, /device:TPU:1, one launch (start us, length us, event | category | flops | bytes accessed | tf_op | source)
XLA Modules:
  0.0 82.9 jit_solution(1064156623342692527)
XLA Ops:
  0.7 2.2 %mix.1 = bf16[8,96,384]{2,1,0:T(8,128)(2,1)} custom-call(s32[1]{0:T(128)S(6)} %copy.9.step_ref, bf16[32,3072]{1,0:T(8,128)(2,1)} %q_hbm.1, bf16[32,3072]{1,0:T(8,128)(2,1)} %ke_hbm.1, bf16[32,3072]{1,0:T(8,128)(2,1)} %ve_hbm.1, bf16[32,3072]{1,0:T(8,128)(2,1)} %ks_hbm.1, bf16[32,3072]{1,0:T(8,128)(2,1)} %vs_hbm.1, s32[1,256]{1,0:T(1,128)} %bitcast.21, ...), custom_call_target="tpu_custom_call" | custom-call | flops 2000000000 | bytes 6000000 | tf_op jit(solution)/shard_map/mix/pallas_call | solution.py:83
  2.9 15.8 %all_to_all.16 = bf16[8,96,384]{2,1,0:T(8,128)(2,1)S(1)} all-to-all(bf16[8,96,384]{2,1,0:T(8,128)(2,1)} %mix.1), channel_id=1, replica_groups=mesh['yl'=2,'z'=8,'core'=2,'yh'=2,'xh'=2,'xl'=2] {'yl','yh','xl'}, dimensions={0} | all-to-all | bytes 1179648 | tf_op jit(solution)/shard_map/all_to_all | solution.py:213
  18.7 2.2 %collective-permute-start.6 = (bf16[512,384]{1,0:T(8,128)(2,1)S(1)}, bf16[512,384]{1,0:T(8,128)(2,1)S(1)}, u32[]{:S(2)}, u32[]{:S(2)}) collective-permute-start(bf16[512,384]{1,0:T(8,128)(2,1)S(1)} %bitcast.8), channel_id=1, source_target_pairs={{0,8},{8,0},{1,9},{9,1},{2,10},{10,2},{3,11},{11,3},{4,12},{12,4},... | collective-permute-start | bytes 1179656 | tf_op jit(solution)/shard_map/ppermute | solution.py:35
  21.0 5.6 %collective-permute-start.1 = (bf16[512,384]{1,0:T(8,128)(2,1)S(1)}, bf16[512,384]{1,0:T(8,128)(2,1)S(1)}, u32[]{:S(2)}, u32[]{:S(2)}) collective-permute-start(bf16[512,384]{1,0:T(8,128)(2,1)S(1)} %bitcast.9), channel_id=1, source_target_pairs={{0,16},{8,120},{16,32},{24,8},{32,48},{40,24},{48,64},{56,40},{64,... | collective-permute-start | bytes 1179656 | tf_op jit(solution)/shard_map/ppermute | solution.py:31
  26.5 0.0 collective-permute-done.6.refs_3_
  26.5 1.3 %collective-permute-start.7 = (bf16[512,384]{1,0:T(8,128)(2,1)S(1)}, bf16[512,384]{1,0:T(8,128)(2,1)S(1)}, u32[]{:S(2)}, u32[]{:S(2)}) collective-permute-start(bf16[512,384]{1,0:T(8,128)(2,1)S(1)} %collective-permute-done.6.refs_3_), channel_id=1, source_target_pairs={{0,16},{8,120},{16,32},{24,8},{32,48},{40,24},{48,64},{56,40},{64,... | collective-permute-start | bytes 1179656 | tf_op jit(solution)/shard_map/ppermute | solution.py:31
  27.9 3.4 %collective-permute-done.1.refs_2_ = bf16[512,384]{1,0:T(8,128)(2,1)S(1)} collective-permute-done((bf16[512,384]{1,0:T(8,128)(2,1)S(1)}, bf16[512,384]{1,0:T(8,128)(2,1)S(1)}, u32[]{:S(2)}, u32[]{:S(2)}) %collective-permute-start.1) | collective-permute-done | bytes 393248 | tf_op jit(solution)/shard_map/ppermute | solution.py:31
  31.3 3.1 %collective-permute-start.2 = (bf16[512,384]{1,0:T(8,128)(2,1)S(1)}, bf16[512,384]{1,0:T(8,128)(2,1)S(1)}, u32[]{:S(2)}, u32[]{:S(2)}) collective-permute-start(bf16[512,384]{1,0:T(8,128)(2,1)S(1)} %collective-permute-done.1.refs_2_), channel_id=1, source_target_pairs={{0,16},{8,120},{16,32},{24,8},{32,48},{40,24},{48,64},{56,40},{64,... | collective-permute-start | bytes 1179656 | tf_op jit(solution)/shard_map/ppermute | solution.py:31
  34.4 2.5 %collective-permute-start = (bf16[256,384]{1,0:T(8,128)(2,1)S(1)}, bf16[256,384]{1,0:T(8,128)(2,1)S(1)}, u32[]{:S(2)}, u32[]{:S(2)}) collective-permute-start(bf16[256,384]{1,0:T(8,128)(2,1)S(1)} %bitcast.11), channel_id=1, source_target_pairs={{0,2},{2,0},{1,3},{3,1},{4,6},{6,4},{5,7},{7,5},{8,10},{10,8},{9,1... | collective-permute-start | bytes 589832 | tf_op jit(solution)/shard_map/ppermute | solution.py:35
  36.9 0.0 collective-permute-start.15
  36.9 0.0 collective-permute-done.7.refs_2_
  37.0 0.5 collective-permute-start.14
  37.5 1.2 %collective-permute-start.8 = (bf16[512,384]{1,0:T(8,128)(2,1)S(1)}, bf16[512,384]{1,0:T(8,128)(2,1)S(1)}, u32[]{:S(2)}, u32[]{:S(2)}) collective-permute-start(bf16[512,384]{1,0:T(8,128)(2,1)S(1)} %collective-permute-done.7.refs_2_), channel_id=1, source_target_pairs={{0,16},{8,120},{16,32},{24,8},{32,48},{40,24},{48,64},{56,40},{64,... | collective-permute-start | bytes 1179656 | tf_op jit(solution)/shard_map/ppermute | solution.py:31
  38.6 1.1 %collective-permute-done.2.refs_2_ = bf16[512,384]{1,0:T(8,128)(2,1)S(1)} collective-permute-done((bf16[512,384]{1,0:T(8,128)(2,1)S(1)}, bf16[512,384]{1,0:T(8,128)(2,1)S(1)}, u32[]{:S(2)}, u32[]{:S(2)}) %collective-permute-start.2) | collective-permute-done | bytes 393248 | tf_op jit(solution)/shard_map/ppermute | solution.py:31
  39.7 3.2 %collective-permute-start.3 = (bf16[512,384]{1,0:T(8,128)(2,1)S(1)}, bf16[512,384]{1,0:T(8,128)(2,1)S(1)}, u32[]{:S(2)}, u32[]{:S(2)}) collective-permute-start(bf16[512,384]{1,0:T(8,128)(2,1)S(1)} %collective-permute-done.2.refs_2_), channel_id=1, source_target_pairs={{0,16},{8,120},{16,32},{24,8},{32,48},{40,24},{48,64},{56,40},{64,... | collective-permute-start | bytes 1179656 | tf_op jit(solution)/shard_map/ppermute | solution.py:31
  42.9 0.0 collective-permute-done.refs_1_
  42.9 1.5 %flash.8 = (f32[384,512]{1,0:T(8,128)S(1)}, f32[24,512]{1,0:T(8,128)S(1)}) custom-call(bf16[256,384]{1,0:T(8,128)(2,1)S(1)} %bitcast.12, bf16[256,384]{1,0:T(8,128)(2,1)S(1)} %collective-permute-done.refs_1_, bf16[512,384]{1,0:T(8,128)(2,1)S(1)} %bitcast.10, bf16[512,384]{1,0:T(8,128)(2,1)S(1)} %collective-permute-done.6.refs_3_), custom_call_target="tpu_custom_call" | custom-call | flops 2177600000 | bytes 6532800 | tf_op jit(solution)/shard_map/flash/pallas_call | solution.py:167
  44.4 0.1 collective-permute-start.13
  44.5 0.0 collective-permute-done.15.refs_3_
  44.6 1.6 %flash.9 = (f32[384,512]{1,0:T(8,128)S(1)}, f32[24,512]{1,0:T(8,128)S(1)}) custom-call(bf16[256,384]{1,0:T(8,128)(2,1)S(1)} %bitcast.13, bf16[256,384]{1,0:T(8,128)(2,1)S(1)} %collective-permute-done.refs_1_, bf16[512,384]{1,0:T(8,128)(2,1)S(1)} %collective-permute-done.1.refs_2_, bf16[512,384]{1,0:T(8,128)(2,1)S(1)} %collective-permute-done.15.refs_3_, ...), custom_call_target="tpu_custom_call" | custom-call | flops 2177600000 | bytes 6532800 | tf_op jit(solution)/shard_map/flash/pallas_call | solution.py:167
  46.1 0.0 collective-permute-done.8.refs_2_
  46.1 0.6 collective-permute-start.12
  46.7 1.3 %collective-permute-start.9 = (bf16[512,384]{1,0:T(8,128)(2,1)S(1)}, bf16[512,384]{1,0:T(8,128)(2,1)S(1)}, u32[]{:S(2)}, u32[]{:S(2)}) collective-permute-start(bf16[512,384]{1,0:T(8,128)(2,1)S(1)} %collective-permute-done.8.refs_2_), channel_id=1, source_target_pairs={{0,16},{8,120},{16,32},{24,8},{32,48},{40,24},{48,64},{56,40},{64,... | collective-permute-start | bytes 1179656 | tf_op jit(solution)/shard_map/ppermute | solution.py:31
  48.0 0.6 collective-permute-done.3.refs_2_
  48.6 2.1 %collective-permute-start.11 = (bf16[512,384]{1,0:T(8,128)(2,1)S(1)}, bf16[512,384]{1,0:T(8,128)(2,1)S(1)}, u32[]{:S(2)}, u32[]{:S(2)}) collective-permute-start(bf16[512,384]{1,0:T(8,128)(2,1)S(1)} %collective-permute-done.3.refs_2_), channel_id=1, source_target_pairs={{0,8},{8,0},{1,9},{9,1},{2,10},{10,2},{3,11},{11,3},{4,12},{12,4},... | collective-permute-start | bytes 1179656 | tf_op jit(solution)/shard_map/ppermute | solution.py:35
  50.7 0.0 collective-permute-done.14.refs_3_
  50.7 0.6 collective-permute-start.4
  51.3 1.6 %flash.10 = (f32[384,512]{1,0:T(8,128)S(1)}, f32[24,512]{1,0:T(8,128)S(1)}) custom-call(bf16[256,384]{1,0:T(8,128)(2,1)S(1)} %bitcast.14, bf16[256,384]{1,0:T(8,128)(2,1)S(1)} %collective-permute-done.refs_1_, bf16[512,384]{1,0:T(8,128)(2,1)S(1)} %collective-permute-done.7.refs_2_, bf16[512,384]{1,0:T(8,128)(2,1)S(1)} %collective-permute-done.14.refs_3_, ...), custom_call_target="tpu_custom_call" | custom-call | flops 2177600000 | bytes 6532800 | tf_op jit(solution)/shard_map/flash/pallas_call | solution.py:167
  52.8 0.0 collective-permute-done.13.refs_3_
  52.8 1.6 %flash.11 = (f32[384,512]{1,0:T(8,128)S(1)}, f32[24,512]{1,0:T(8,128)S(1)}) custom-call(bf16[256,384]{1,0:T(8,128)(2,1)S(1)} %bitcast.15, bf16[256,384]{1,0:T(8,128)(2,1)S(1)} %collective-permute-done.refs_1_, bf16[512,384]{1,0:T(8,128)(2,1)S(1)} %collective-permute-done.2.refs_2_, bf16[512,384]{1,0:T(8,128)(2,1)S(1)} %collective-permute-done.13.refs_3_, ...), custom_call_target="tpu_custom_call" | custom-call | flops 2177600000 | bytes 6532800 | tf_op jit(solution)/shard_map/flash/pallas_call | solution.py:167
  54.4 0.0 collective-permute-done.9.refs_2_
  54.4 1.4 %collective-permute-start.10 = (bf16[512,384]{1,0:T(8,128)(2,1)S(1)}, bf16[512,384]{1,0:T(8,128)(2,1)S(1)}, u32[]{:S(2)}, u32[]{:S(2)}) collective-permute-start(bf16[512,384]{1,0:T(8,128)(2,1)S(1)} %collective-permute-done.9.refs_2_), channel_id=1, source_target_pairs={{0,8},{8,0},{1,9},{9,1},{2,10},{10,2},{3,11},{11,3},{4,12},{12,4},... | collective-permute-start | bytes 1179656 | tf_op jit(solution)/shard_map/ppermute | solution.py:35
  55.8 2.1 %collective-permute-done.4.refs_2_ = bf16[512,384]{1,0:T(8,128)(2,1)S(1)} collective-permute-done((bf16[512,384]{1,0:T(8,128)(2,1)S(1)}, bf16[512,384]{1,0:T(8,128)(2,1)S(1)}, u32[]{:S(2)}, u32[]{:S(2)}) %collective-permute-start.4) | collective-permute-done | bytes 393248 | tf_op jit(solution)/shard_map/ppermute | solution.py:31
  57.8 2.2 %collective-permute-start.5 = (bf16[512,384]{1,0:T(8,128)(2,1)S(1)}, bf16[512,384]{1,0:T(8,128)(2,1)S(1)}, u32[]{:S(2)}, u32[]{:S(2)}) collective-permute-start(bf16[512,384]{1,0:T(8,128)(2,1)S(1)} %collective-permute-done.4.refs_2_), channel_id=1, source_target_pairs={{0,8},{8,0},{1,9},{9,1},{2,10},{10,2},{3,11},{11,3},{4,12},{12,4},... | collective-permute-start | bytes 1179656 | tf_op jit(solution)/shard_map/ppermute | solution.py:35
  60.0 0.0 collective-permute-done.12.refs_3_
  60.0 1.6 %flash.12 = (f32[384,512]{1,0:T(8,128)S(1)}, f32[24,512]{1,0:T(8,128)S(1)}) custom-call(bf16[256,384]{1,0:T(8,128)(2,1)S(1)} %bitcast.16, bf16[256,384]{1,0:T(8,128)(2,1)S(1)} %collective-permute-done.refs_1_, bf16[512,384]{1,0:T(8,128)(2,1)S(1)} %collective-permute-done.8.refs_2_, bf16[512,384]{1,0:T(8,128)(2,1)S(1)} %collective-permute-done.12.refs_3_, ...), custom_call_target="tpu_custom_call" | custom-call | flops 2177600000 | bytes 6532800 | tf_op jit(solution)/shard_map/flash/pallas_call | solution.py:167
  61.6 0.0 collective-permute-done.11.refs_3_
  61.6 1.6 %flash.13 = (f32[384,512]{1,0:T(8,128)S(1)}, f32[24,512]{1,0:T(8,128)S(1)}) custom-call(bf16[256,384]{1,0:T(8,128)(2,1)S(1)} %bitcast.17, bf16[256,384]{1,0:T(8,128)(2,1)S(1)} %collective-permute-done.refs_1_, bf16[512,384]{1,0:T(8,128)(2,1)S(1)} %collective-permute-done.3.refs_2_, bf16[512,384]{1,0:T(8,128)(2,1)S(1)} %collective-permute-done.11.refs_3_, ...), custom_call_target="tpu_custom_call" | custom-call | flops 2177600000 | bytes 6532800 | tf_op jit(solution)/shard_map/flash/pallas_call | solution.py:167
  63.1 0.0 collective-permute-done.10.refs_3_
  63.1 1.6 %flash.14 = (f32[384,512]{1,0:T(8,128)S(1)}, f32[24,512]{1,0:T(8,128)S(1)}) custom-call(bf16[256,384]{1,0:T(8,128)(2,1)S(1)} %bitcast.18, bf16[256,384]{1,0:T(8,128)(2,1)S(1)} %collective-permute-done.refs_1_, bf16[512,384]{1,0:T(8,128)(2,1)S(1)} %collective-permute-done.9.refs_2_, bf16[512,384]{1,0:T(8,128)(2,1)S(1)} %collective-permute-done.10.refs_3_, ...), custom_call_target="tpu_custom_call" | custom-call | flops 2177600000 | bytes 6532800 | tf_op jit(solution)/shard_map/flash/pallas_call | solution.py:167
  64.7 0.0 collective-permute-done.5.refs_3_
  64.7 1.7 %flash.15 = bf16[512,512]{1,0:T(8,128)(2,1)S(1)} custom-call(bf16[256,384]{1,0:T(8,128)(2,1)S(1)} %bitcast.19, bf16[256,384]{1,0:T(8,128)(2,1)S(1)} %collective-permute-done.refs_1_, bf16[512,384]{1,0:T(8,128)(2,1)S(1)} %collective-permute-done.4.refs_2_, bf16[512,384]{1,0:T(8,128)(2,1)S(1)} %collective-permute-done.5.refs_3_, ...), custom_call_target="tpu_custom_call" | custom-call | flops 2177600000 | bytes 6532800 | tf_op jit(solution)/shard_map/flash/pallas_call | solution.py:167
  66.4 15.4 %all_to_all.17 = bf16[16,32,512]{2,1,0:T(8,128)(2,1)S(1)} all-to-all(bf16[16,32,512]{2,1,0:T(8,128)(2,1)S(1)} %bitcast.6), channel_id=1, replica_groups=mesh['yl'=2,'z'=8,'core'=2,'yh'=2,'xh'=2,'xl'=2] {'yl','yh','xh','xl'}, dimensions={0} | all-to-all | bytes 1048576 | tf_op jit(solution)/shard_map/all_to_all | solution.py:225
  81.8 1.1 %merge.1 = bf16[32,3072]{1,0:T(8,128)(2,1)} custom-call(bf16[512,512]{1,0:T(8,128)(2,1)S(1)} %bitcast.7), custom_call_target="tpu_custom_call" | custom-call | flops 2000000000 | bytes 6000000 | tf_op jit(solution)/shard_map/merge/pallas_call | solution.py:197
  (2 shorter events, 0.1 us)
Async XLA Ops:
  18.7 7.8 %collective-permute-start.6 = (bf16[512,384]{1,0:T(8,128)(2,1)S(1)}, bf16[512,384]{1,0:T(8,128)(2,1)S(1)}, u32[]{:S(2)}, u32[]{:S(2)}) collective-permute-start(bf16[512,384]{1,0:T(8,128)(2,1)S(1)} %bitcast.8), channel_id=1, source_target_pairs={{0,8},{8,0},{1,9},{9,1},{2,10},{10,2},{3,11},{11,3},{4,12},{12,4},... | collective-permute-start | bytes 1179656 | tf_op jit(solution)/shard_map/ppermute | solution.py:35
  21.0 10.3 %collective-permute-start.1 = (bf16[512,384]{1,0:T(8,128)(2,1)S(1)}, bf16[512,384]{1,0:T(8,128)(2,1)S(1)}, u32[]{:S(2)}, u32[]{:S(2)}) collective-permute-start(bf16[512,384]{1,0:T(8,128)(2,1)S(1)} %bitcast.9), channel_id=1, source_target_pairs={{0,16},{8,120},{16,32},{24,8},{32,48},{40,24},{48,64},{56,40},{64,... | collective-permute-start | bytes 1179656 | tf_op jit(solution)/shard_map/ppermute | solution.py:31
  26.5 10.4 %collective-permute-start.7 = (bf16[512,384]{1,0:T(8,128)(2,1)S(1)}, bf16[512,384]{1,0:T(8,128)(2,1)S(1)}, u32[]{:S(2)}, u32[]{:S(2)}) collective-permute-start(bf16[512,384]{1,0:T(8,128)(2,1)S(1)} %collective-permute-done.6.refs_3_), channel_id=1, source_target_pairs={{0,16},{8,120},{16,32},{24,8},{32,48},{40,24},{48,64},{56,40},{64,... | collective-permute-start | bytes 1179656 | tf_op jit(solution)/shard_map/ppermute | solution.py:31
  31.3 8.4 %collective-permute-start.2 = (bf16[512,384]{1,0:T(8,128)(2,1)S(1)}, bf16[512,384]{1,0:T(8,128)(2,1)S(1)}, u32[]{:S(2)}, u32[]{:S(2)}) collective-permute-start(bf16[512,384]{1,0:T(8,128)(2,1)S(1)} %collective-permute-done.1.refs_2_), channel_id=1, source_target_pairs={{0,16},{8,120},{16,32},{24,8},{32,48},{40,24},{48,64},{56,40},{64,... | collective-permute-start | bytes 1179656 | tf_op jit(solution)/shard_map/ppermute | solution.py:31
  34.4 8.5 %collective-permute-start = (bf16[256,384]{1,0:T(8,128)(2,1)S(1)}, bf16[256,384]{1,0:T(8,128)(2,1)S(1)}, u32[]{:S(2)}, u32[]{:S(2)}) collective-permute-start(bf16[256,384]{1,0:T(8,128)(2,1)S(1)} %bitcast.11), channel_id=1, source_target_pairs={{0,2},{2,0},{1,3},{3,1},{4,6},{6,4},{5,7},{7,5},{8,10},{10,8},{9,1... | collective-permute-start | bytes 589832 | tf_op jit(solution)/shard_map/ppermute | solution.py:35
  36.9 7.6 %collective-permute-start.15 = (bf16[512,384]{1,0:T(8,128)(2,1)S(1)}, bf16[512,384]{1,0:T(8,128)(2,1)S(1)}, u32[]{:S(2)}, u32[]{:S(2)}) collective-permute-start(bf16[512,384]{1,0:T(8,128)(2,1)S(1)} %collective-permute-done.1.refs_2_), channel_id=1, source_target_pairs={{0,8},{8,0},{1,9},{9,1},{2,10},{10,2},{3,11},{11,3},{4,12},{12,4},... | collective-permute-start | bytes 1179656 | tf_op jit(solution)/shard_map/ppermute | solution.py:35
  37.0 13.7 %collective-permute-start.14 = (bf16[512,384]{1,0:T(8,128)(2,1)S(1)}, bf16[512,384]{1,0:T(8,128)(2,1)S(1)}, u32[]{:S(2)}, u32[]{:S(2)}) collective-permute-start(bf16[512,384]{1,0:T(8,128)(2,1)S(1)} %collective-permute-done.7.refs_2_), channel_id=1, source_target_pairs={{0,8},{8,0},{1,9},{9,1},{2,10},{10,2},{3,11},{11,3},{4,12},{12,4},... | collective-permute-start | bytes 1179656 | tf_op jit(solution)/shard_map/ppermute | solution.py:35
  37.5 8.7 %collective-permute-start.8 = (bf16[512,384]{1,0:T(8,128)(2,1)S(1)}, bf16[512,384]{1,0:T(8,128)(2,1)S(1)}, u32[]{:S(2)}, u32[]{:S(2)}) collective-permute-start(bf16[512,384]{1,0:T(8,128)(2,1)S(1)} %collective-permute-done.7.refs_2_), channel_id=1, source_target_pairs={{0,16},{8,120},{16,32},{24,8},{32,48},{40,24},{48,64},{56,40},{64,... | collective-permute-start | bytes 1179656 | tf_op jit(solution)/shard_map/ppermute | solution.py:31
  39.7 8.9 %collective-permute-start.3 = (bf16[512,384]{1,0:T(8,128)(2,1)S(1)}, bf16[512,384]{1,0:T(8,128)(2,1)S(1)}, u32[]{:S(2)}, u32[]{:S(2)}) collective-permute-start(bf16[512,384]{1,0:T(8,128)(2,1)S(1)} %collective-permute-done.2.refs_2_), channel_id=1, source_target_pairs={{0,16},{8,120},{16,32},{24,8},{32,48},{40,24},{48,64},{56,40},{64,... | collective-permute-start | bytes 1179656 | tf_op jit(solution)/shard_map/ppermute | solution.py:31
  44.4 8.4 %collective-permute-start.13 = (bf16[512,384]{1,0:T(8,128)(2,1)S(1)}, bf16[512,384]{1,0:T(8,128)(2,1)S(1)}, u32[]{:S(2)}, u32[]{:S(2)}) collective-permute-start(bf16[512,384]{1,0:T(8,128)(2,1)S(1)} %collective-permute-done.2.refs_2_), channel_id=1, source_target_pairs={{0,8},{8,0},{1,9},{9,1},{2,10},{10,2},{3,11},{11,3},{4,12},{12,4},... | collective-permute-start | bytes 1179656 | tf_op jit(solution)/shard_map/ppermute | solution.py:35
  46.1 13.9 %collective-permute-start.12 = (bf16[512,384]{1,0:T(8,128)(2,1)S(1)}, bf16[512,384]{1,0:T(8,128)(2,1)S(1)}, u32[]{:S(2)}, u32[]{:S(2)}) collective-permute-start(bf16[512,384]{1,0:T(8,128)(2,1)S(1)} %collective-permute-done.8.refs_2_), channel_id=1, source_target_pairs={{0,8},{8,0},{1,9},{9,1},{2,10},{10,2},{3,11},{11,3},{4,12},{12,4},... | collective-permute-start | bytes 1179656 | tf_op jit(solution)/shard_map/ppermute | solution.py:35
  46.7 7.7 %collective-permute-start.9 = (bf16[512,384]{1,0:T(8,128)(2,1)S(1)}, bf16[512,384]{1,0:T(8,128)(2,1)S(1)}, u32[]{:S(2)}, u32[]{:S(2)}) collective-permute-start(bf16[512,384]{1,0:T(8,128)(2,1)S(1)} %collective-permute-done.8.refs_2_), channel_id=1, source_target_pairs={{0,16},{8,120},{16,32},{24,8},{32,48},{40,24},{48,64},{56,40},{64,... | collective-permute-start | bytes 1179656 | tf_op jit(solution)/shard_map/ppermute | solution.py:31
  48.6 13.0 %collective-permute-start.11 = (bf16[512,384]{1,0:T(8,128)(2,1)S(1)}, bf16[512,384]{1,0:T(8,128)(2,1)S(1)}, u32[]{:S(2)}, u32[]{:S(2)}) collective-permute-start(bf16[512,384]{1,0:T(8,128)(2,1)S(1)} %collective-permute-done.3.refs_2_), channel_id=1, source_target_pairs={{0,8},{8,0},{1,9},{9,1},{2,10},{10,2},{3,11},{11,3},{4,12},{12,4},... | collective-permute-start | bytes 1179656 | tf_op jit(solution)/shard_map/ppermute | solution.py:35
  50.7 7.2 %collective-permute-start.4 = (bf16[512,384]{1,0:T(8,128)(2,1)S(1)}, bf16[512,384]{1,0:T(8,128)(2,1)S(1)}, u32[]{:S(2)}, u32[]{:S(2)}) collective-permute-start(bf16[512,384]{1,0:T(8,128)(2,1)S(1)} %collective-permute-done.3.refs_2_), channel_id=1, source_target_pairs={{0,16},{8,120},{16,32},{24,8},{32,48},{40,24},{48,64},{56,40},{64,... | collective-permute-start | bytes 1179656 | tf_op jit(solution)/shard_map/ppermute | solution.py:31
  54.4 8.7 %collective-permute-start.10 = (bf16[512,384]{1,0:T(8,128)(2,1)S(1)}, bf16[512,384]{1,0:T(8,128)(2,1)S(1)}, u32[]{:S(2)}, u32[]{:S(2)}) collective-permute-start(bf16[512,384]{1,0:T(8,128)(2,1)S(1)} %collective-permute-done.9.refs_2_), channel_id=1, source_target_pairs={{0,8},{8,0},{1,9},{9,1},{2,10},{10,2},{3,11},{11,3},{4,12},{12,4},... | collective-permute-start | bytes 1179656 | tf_op jit(solution)/shard_map/ppermute | solution.py:35
  57.8 6.9 %collective-permute-start.5 = (bf16[512,384]{1,0:T(8,128)(2,1)S(1)}, bf16[512,384]{1,0:T(8,128)(2,1)S(1)}, u32[]{:S(2)}, u32[]{:S(2)}) collective-permute-start(bf16[512,384]{1,0:T(8,128)(2,1)S(1)} %collective-permute-done.4.refs_2_), channel_id=1, source_target_pairs={{0,8},{8,0},{1,9},{9,1},{2,10},{10,2},{3,11},{11,3},{4,12},{12,4},... | collective-permute-start | bytes 1179656 | tf_op jit(solution)/shard_map/ppermute | solution.py:35

commit v4 on v3

--- a/solution.py
+++ b/solution.py
@@ -10,8 +10,8 @@
 
 AXES = ("yl", "z", "core", "yh", "xh", "xl")
 SIZES = (2, 8, 2, 2, 2, 2)
-GROUP_AXES = ("yl", "yh", "xl")
-OUT_AXES = ("yl", "yh", "xh", "xl")
+GROUP_AXES = ("yl", "yh", "xh")
+OUT_AXES = ("yl", "yh", "xl", "xh")
 GROUPS, PARTS, NZ = 8, 2, 8
 HEAD = 128
 TOK = 32
@@ -147,7 +147,7 @@
 
 def target(part, e):
     source = part % (GROUPS // 4) * 4 + e
-    xh = lax.axis_index("xh")
+    xh = lax.axis_index("xl")
     xh = xh if part < GROUPS // 4 else 1 - xh
     return pl.ds(((source // 2 * 2 + xh) * 2 + source % 2) * TOK, TOK)
 
@@ -174,6 +174,10 @@
     )(*args)
 
 
+def attend(q_parts, block, state, last=False):
+    return flash(q_parts, [block, swap(block, "core")], state, last)
+
+
 def merge_kernel(in_ref, out_ref):
     lse = in_ref[:, WIDTH:].astype(F32)
     lse = lse[:, :HEADS] + lse[:, HEADS : 2 * HEADS] + lse[:, 2 * HEADS : 3 * HEADS]
@@ -214,14 +218,23 @@
     near = got[:, : 2 * TOK].reshape(-1, WIDTH)
     query = got[:, 2 * TOK :].reshape(-1, WIDTH)
     far = swap(near, "core")
-    q_parts = [query, swap(query, "xh")]
+    q_parts = [query, swap(query, "xl")]
+    near1, far1 = ring_z(near), ring_z(far)
+    near1, *q_parts = lax.optimization_barrier([near1, *q_parts])
     state = flash(q_parts, [near, far], None)
-    for step in range(NZ // 2 - 1):
-        near, far = ring_z(near), ring_z(far)
-        state = flash(q_parts, [near, swap(near, "core")], state)
-        state = flash(q_parts, [far, swap(far, "core")], state)
-    near = ring_z(near)
-    parts = flash(q_parts, [near, swap(near, "core")], state, last=True)
+    near2 = ring_z(near1)
+    far1, *state = lax.optimization_barrier([far1, *state])
+    far2 = ring_z(far1)
+    state = attend(q_parts, near1, state)
+    state = attend(q_parts, far1, state)
+    near3, far3 = ring_z(near2), ring_z(far2)
+    state = attend(q_parts, near2, state)
+    state = attend(q_parts, far2, state)
+    near4 = ring_z(near3)
+    state = attend(q_parts, near3, state)
+    far3, *state = lax.optimization_barrier([far3, *state])
+    state = attend(q_parts, far3, state)
+    parts = attend(q_parts, near4, state, last=True)
     parts = lax.all_to_all(parts, OUT_AXES, 0, 0, tiled=True)
     return merge(parts)
 

time: 83.1 us -> 80.1 us (0.964)
  starting transfers between devices: 27.9 us -> 25.8 us
  waiting for transfers between devices: 7.15 us -> 5.77 us
    ppermute x7, waiting for transfers between devices: 7.12 us -> 2.18 us  [ring_z(): return lax.ppermute(value, ('z', 'core'), pairs)]
    ppermute x9, waiting for transfers between devices: 0.02 us -> 3.6 us  [swap(): return lax.ppermute(value, axis, [(0, 1), (1, 0)])]
    all_to_all x1, blocking collectives: 15.8 us -> 18.7 us  [on_device(): got = lax.all_to_all(mixed, GROUP_AXES, 0, 0, tiled=True)]
    ppermute x9, starting transfers between devices: 11.6 us -> 8.81 us  [swap(): return lax.ppermute(value, axis, [(0, 1), (1, 0)])]
    all_to_all x1, blocking collectives: 15.4 us -> 12.9 us  [on_device(): parts = lax.all_to_all(parts, OUT_AXES, 0, 0, tiled=True)]
  transfers between devices with their start and end apart: 16 -> 16, of which waited for: 4 -> 3; matrix products, arithmetic and copies ran while one was open for 0% -> 0% of each run, Pallas kernels for 13% -> 14%
where the time goes in v4:
time: 80.1 us; the launch traced here: 79.9 us
  blocking collectives  31.5 us (39%)
  starting transfers between devices  25.8 us (32%)
  Pallas kernels  15.9 us (20%)
  waiting for transfers between devices  5.77 us (7%)
    all_to_all x1, blocking collectives, on_device(): got = lax.all_to_all(mixed, GROUP_AXES, 0, 0, tiled=True)  18.7 us
    ppermute x7, starting transfers between devices, ring_z(): return lax.ppermute(value, ('z', 'core'), pairs)  17 us
    all_to_all x1, blocking collectives, on_device(): parts = lax.all_to_all(parts, OUT_AXES, 0, 0, tiled=True)  12.9 us
    pallas_call x8, Pallas kernels, flash(): pl.pallas_call(functools.partial(flash_kernel, first, last, len(kv_blocks...  12.5 us
    ppermute x9, starting transfers between devices, swap(): return lax.ppermute(value, axis, [(0, 1), (1, 0)])  8.81 us
    ppermute x9, waiting for transfers between devices, swap(): return lax.ppermute(value, axis, [(0, 1), (1, 0)])  3.6 us
    pallas_call x1, Pallas kernels, mix(): pl.pallas_call(mix_kernel, out_shape=jax.ShapeDtypeStruct((GROUPS, 3 * TO...  2.23 us
    ppermute x7, waiting for transfers between devices, ring_z(): return lax.ppermute(value, ('z', 'core'), pairs)  2.18 us
  transfers between devices with their start and end apart: 16, of which 3 were waited for; matrix products, arithmetic and copies ran while one was open for 0% of the time, Pallas kernels for 14%

profile of v4, /device:TPU:1, one launch (start us, length us, event | category | flops | bytes accessed | tf_op | source)
XLA Modules:
  0.0 79.9 jit_solution(2374002412075068656)
XLA Ops:
  0.7 2.2 %mix.1 = bf16[8,96,384]{2,1,0:T(8,128)(2,1)} custom-call(s32[1]{0:T(128)S(6)} %copy.9.step_ref, bf16[32,3072]{1,0:T(8,128)(2,1)} %q_hbm.1, bf16[32,3072]{1,0:T(8,128)(2,1)} %ke_hbm.1, bf16[32,3072]{1,0:T(8,128)(2,1)} %ve_hbm.1, bf16[32,3072]{1,0:T(8,128)(2,1)} %ks_hbm.1, bf16[32,3072]{1,0:T(8,128)(2,1)} %vs_hbm.1, s32[1,256]{1,0:T(1,128)} %bitcast.21, ...), custom_call_target="tpu_custom_call" | custom-call | flops 2000000000 | bytes 6000000 | tf_op jit(solution)/shard_map/mix/pallas_call | solution.py:83
  2.9 18.7 %all_to_all.16 = bf16[8,96,384]{2,1,0:T(8,128)(2,1)S(1)} all-to-all(bf16[8,96,384]{2,1,0:T(8,128)(2,1)} %mix.1), channel_id=1, replica_groups=mesh['yl'=2,'z'=8,'core'=2,'yh'=2,'xh'=2,'xl'=2] {'yl','yh','xh'}, dimensions={0} | all-to-all | bytes 1179648 | tf_op jit(solution)/shard_map/all_to_all | solution.py:217
  21.6 2.3 %collective-permute-start.6 = (bf16[512,384]{1,0:T(8,128)(2,1)S(1)}, bf16[512,384]{1,0:T(8,128)(2,1)S(1)}, u32[]{:S(2)}, u32[]{:S(2)}) collective-permute-start(bf16[512,384]{1,0:T(8,128)(2,1)S(1)} %bitcast.8), channel_id=1, source_target_pairs={{0,8},{8,0},{1,9},{9,1},{2,10},{10,2},{3,11},{11,3},{4,12},{12,4},... | collective-permute-start | bytes 1179656 | tf_op jit(solution)/shard_map/ppermute | solution.py:35
  24.0 5.6 %collective-permute-start = (bf16[512,384]{1,0:T(8,128)(2,1)S(1)}, bf16[512,384]{1,0:T(8,128)(2,1)S(1)}, u32[]{:S(2)}, u32[]{:S(2)}) collective-permute-start(bf16[512,384]{1,0:T(8,128)(2,1)S(1)} %bitcast.9), channel_id=1, source_target_pairs={{0,16},{8,120},{16,32},{24,8},{32,48},{40,24},{48,64},{56,40},{64,... | collective-permute-start | bytes 1179656 | tf_op jit(solution)/shard_map/ppermute | solution.py:31
  29.6 0.4 collective-permute-start.1
  30.0 0.0 collective-permute-done.6.refs_3_
  30.0 0.9 %collective-permute-start.7 = (bf16[512,384]{1,0:T(8,128)(2,1)S(1)}, bf16[512,384]{1,0:T(8,128)(2,1)S(1)}, u32[]{:S(2)}, u32[]{:S(2)}) collective-permute-start(bf16[512,384]{1,0:T(8,128)(2,1)S(1)} %collective-permute-done.6.refs_3_), channel_id=1, source_target_pairs={{0,16},{8,120},{16,32},{24,8},{32,48},{40,24},{48,64},{56,40},{64,... | collective-permute-start | bytes 1179656 | tf_op jit(solution)/shard_map/ppermute | solution.py:31
  30.9 3.6 %collective-permute-done.1.refs_1_ = bf16[256,384]{1,0:T(8,128)(2,1)S(1)} collective-permute-done((bf16[256,384]{1,0:T(8,128)(2,1)S(1)}, bf16[256,384]{1,0:T(8,128)(2,1)S(1)}, u32[]{:S(2)}, u32[]{:S(2)}) %collective-permute-start.1) | collective-permute-done | bytes 196640 | tf_op jit(solution)/shard_map/ppermute | solution.py:35
  34.5 0.0 collective-permute-done.refs_2_
  34.5 2.9 %collective-permute-start.2 = (bf16[512,384]{1,0:T(8,128)(2,1)S(1)}, bf16[512,384]{1,0:T(8,128)(2,1)S(1)}, u32[]{:S(2)}, u32[]{:S(2)}) collective-permute-start(bf16[512,384]{1,0:T(8,128)(2,1)S(1)} %collective-permute-done.refs_2_), channel_id=1, source_target_pairs={{0,16},{8,120},{16,32},{24,8},{32,48},{40,24},{48,64},{56,40},{64,... | collective-permute-start | bytes 1179656 | tf_op jit(solution)/shard_map/ppermute | solution.py:31
  37.4 0.0 collective-permute-start.14
  37.4 1.5 %flash.8 = (f32[384,512]{1,0:T(8,128)S(1)}, f32[24,512]{1,0:T(8,128)S(1)}) custom-call(bf16[256,384]{1,0:T(8,128)(2,1)S(1)} %bitcast.12, bf16[256,384]{1,0:T(8,128)(2,1)S(1)} %collective-permute-done.1.refs_1_, bf16[512,384]{1,0:T(8,128)(2,1)S(1)} %bitcast.10, bf16[512,384]{1,0:T(8,128)(2,1)S(1)} %collective-permute-done.6.refs_3_), custom_call_target="tpu_custom_call" | custom-call | flops 2177600000 | bytes 6532800 | tf_op jit(solution)/shard_map/flash/pallas_call | solution.py:167
  38.9 0.0 collective-permute-done.7.refs_2_
  38.9 2.7 %collective-permute-start.8 = (bf16[512,384]{1,0:T(8,128)(2,1)S(1)}, bf16[512,384]{1,0:T(8,128)(2,1)S(1)}, u32[]{:S(2)}, u32[]{:S(2)}) collective-permute-start(bf16[512,384]{1,0:T(8,128)(2,1)S(1)} %collective-permute-done.7.refs_2_), channel_id=1, source_target_pairs={{0,16},{8,120},{16,32},{24,8},{32,48},{40,24},{48,64},{56,40},{64,... | collective-permute-start | bytes 1179656 | tf_op jit(solution)/shard_map/ppermute | solution.py:31
  41.6 1.1 %collective-permute-done.2.refs_2_ = bf16[512,384]{1,0:T(8,128)(2,1)S(1)} collective-permute-done((bf16[512,384]{1,0:T(8,128)(2,1)S(1)}, bf16[512,384]{1,0:T(8,128)(2,1)S(1)}, u32[]{:S(2)}, u32[]{:S(2)}) %collective-permute-start.2) | collective-permute-done | bytes 393248 | tf_op jit(solution)/shard_map/ppermute | solution.py:31
  42.7 3.1 %collective-permute-start.3 = (bf16[512,384]{1,0:T(8,128)(2,1)S(1)}, bf16[512,384]{1,0:T(8,128)(2,1)S(1)}, u32[]{:S(2)}, u32[]{:S(2)}) collective-permute-start(bf16[512,384]{1,0:T(8,128)(2,1)S(1)} %collective-permute-done.2.refs_2_), channel_id=1, source_target_pairs={{0,16},{8,120},{16,32},{24,8},{32,48},{40,24},{48,64},{56,40},{64,... | collective-permute-start | bytes 1179656 | tf_op jit(solution)/shard_map/ppermute | solution.py:31
  45.8 0.0 collective-permute-start.13
  45.8 0.5 collective-permute-start.12
  46.3 0.0 collective-permute-done.14.refs_3_
  46.3 1.6 %flash.9 = (f32[384,512]{1,0:T(8,128)S(1)}, f32[24,512]{1,0:T(8,128)S(1)}) custom-call(bf16[256,384]{1,0:T(8,128)(2,1)S(1)} %bitcast.13, bf16[256,384]{1,0:T(8,128)(2,1)S(1)} %collective-permute-done.1.refs_1_, bf16[512,384]{1,0:T(8,128)(2,1)S(1)} %collective-permute-done.refs_2_, bf16[512,384]{1,0:T(8,128)(2,1)S(1)} %collective-permute-done.14.refs_3_, ...), custom_call_target="tpu_custom_call" | custom-call | flops 2177600000 | bytes 6532800 | tf_op jit(solution)/shard_map/flash/pallas_call | solution.py:167
  47.9 0.0 collective-permute-done.8.refs_2_
  47.9 1.0 %collective-permute-start.11 = (bf16[512,384]{1,0:T(8,128)(2,1)S(1)}, bf16[512,384]{1,0:T(8,128)(2,1)S(1)}, u32[]{:S(2)}, u32[]{:S(2)}) collective-permute-start(bf16[512,384]{1,0:T(8,128)(2,1)S(1)} %collective-permute-done.8.refs_2_), channel_id=1, source_target_pairs={{0,8},{8,0},{1,9},{9,1},{2,10},{10,2},{3,11},{11,3},{4,12},{12,4},... | collective-permute-start | bytes 1179656 | tf_op jit(solution)/shard_map/ppermute | solution.py:35
  48.9 1.2 %collective-permute-start.9 = (bf16[512,384]{1,0:T(8,128)(2,1)S(1)}, bf16[512,384]{1,0:T(8,128)(2,1)S(1)}, u32[]{:S(2)}, u32[]{:S(2)}) collective-permute-start(bf16[512,384]{1,0:T(8,128)(2,1)S(1)} %collective-permute-done.8.refs_2_), channel_id=1, source_target_pairs={{0,16},{8,120},{16,32},{24,8},{32,48},{40,24},{48,64},{56,40},{64,... | collective-permute-start | bytes 1179656 | tf_op jit(solution)/shard_map/ppermute | solution.py:31
  50.0 1.1 %collective-permute-done.3.refs_2_ = bf16[512,384]{1,0:T(8,128)(2,1)S(1)} collective-permute-done((bf16[512,384]{1,0:T(8,128)(2,1)S(1)}, bf16[512,384]{1,0:T(8,128)(2,1)S(1)}, u32[]{:S(2)}, u32[]{:S(2)}) %collective-permute-start.3) | collective-permute-done | bytes 393248 | tf_op jit(solution)/shard_map/ppermute | solution.py:31
  51.1 2.5 %collective-permute-start.10 = (bf16[512,384]{1,0:T(8,128)(2,1)S(1)}, bf16[512,384]{1,0:T(8,128)(2,1)S(1)}, u32[]{:S(2)}, u32[]{:S(2)}) collective-permute-start(bf16[512,384]{1,0:T(8,128)(2,1)S(1)} %collective-permute-done.3.refs_2_), channel_id=1, source_target_pairs={{0,8},{8,0},{1,9},{9,1},{2,10},{10,2},{3,11},{11,3},{4,12},{12,4},... | collective-permute-start | bytes 1179656 | tf_op jit(solution)/shard_map/ppermute | solution.py:35
  53.6 0.0 collective-permute-done.13.refs_3_
  53.6 0.6 collective-permute-start.4
  54.3 1.6 %flash.10 = (f32[384,512]{1,0:T(8,128)S(1)}, f32[24,512]{1,0:T(8,128)S(1)}) custom-call(bf16[256,384]{1,0:T(8,128)(2,1)S(1)} %bitcast.14, bf16[256,384]{1,0:T(8,128)(2,1)S(1)} %collective-permute-done.1.refs_1_, bf16[512,384]{1,0:T(8,128)(2,1)S(1)} %collective-permute-done.7.refs_2_, bf16[512,384]{1,0:T(8,128)(2,1)S(1)} %collective-permute-done.13.refs_3_, ...), custom_call_target="tpu_custom_call" | custom-call | flops 2177600000 | bytes 6532800 | tf_op jit(solution)/shard_map/flash/pallas_call | solution.py:167
  55.8 0.0 collective-permute-done.12.refs_3_
  55.8 1.6 %flash.11 = (f32[384,512]{1,0:T(8,128)S(1)}, f32[24,512]{1,0:T(8,128)S(1)}) custom-call(bf16[256,384]{1,0:T(8,128)(2,1)S(1)} %bitcast.15, bf16[256,384]{1,0:T(8,128)(2,1)S(1)} %collective-permute-done.1.refs_1_, bf16[512,384]{1,0:T(8,128)(2,1)S(1)} %collective-permute-done.2.refs_2_, bf16[512,384]{1,0:T(8,128)(2,1)S(1)} %collective-permute-done.12.refs_3_, ...), custom_call_target="tpu_custom_call" | custom-call | flops 2177600000 | bytes 6532800 | tf_op jit(solution)/shard_map/flash/pallas_call | solution.py:167
  57.4 0.0 collective-permute-done.11.refs_3_
  57.4 1.6 %flash.12 = (f32[384,512]{1,0:T(8,128)S(1)}, f32[24,512]{1,0:T(8,128)S(1)}) custom-call(bf16[256,384]{1,0:T(8,128)(2,1)S(1)} %bitcast.16, bf16[256,384]{1,0:T(8,128)(2,1)S(1)} %collective-permute-done.1.refs_1_, bf16[512,384]{1,0:T(8,128)(2,1)S(1)} %collective-permute-done.8.refs_2_, bf16[512,384]{1,0:T(8,128)(2,1)S(1)} %collective-permute-done.11.refs_3_, ...), custom_call_target="tpu_custom_call" | custom-call | flops 2177600000 | bytes 6532800 | tf_op jit(solution)/shard_map/flash/pallas_call | solution.py:167
  59.0 0.0 collective-permute-done.10.refs_3_
  59.0 1.6 %flash.13 = (f32[384,512]{1,0:T(8,128)S(1)}, f32[24,512]{1,0:T(8,128)S(1)}) custom-call(bf16[256,384]{1,0:T(8,128)(2,1)S(1)} %bitcast.17, bf16[256,384]{1,0:T(8,128)(2,1)S(1)} %collective-permute-done.1.refs_1_, bf16[512,384]{1,0:T(8,128)(2,1)S(1)} %collective-permute-done.3.refs_2_, bf16[512,384]{1,0:T(8,128)(2,1)S(1)} %collective-permute-done.10.refs_3_, ...), custom_call_target="tpu_custom_call" | custom-call | flops 2177600000 | bytes 6532800 | tf_op jit(solution)/shard_map/flash/pallas_call | solution.py:167
  60.5 0.0 collective-permute-done.9.refs_2_
  60.6 0.1 collective-permute-start.15
  60.7 0.0 collective-permute-done.4.refs_2_
  60.7 2.0 %collective-permute-start.5 = (bf16[512,384]{1,0:T(8,128)(2,1)S(1)}, bf16[512,384]{1,0:T(8,128)(2,1)S(1)}, u32[]{:S(2)}, u32[]{:S(2)}) collective-permute-start(bf16[512,384]{1,0:T(8,128)(2,1)S(1)} %collective-permute-done.4.refs_2_), channel_id=1, source_target_pairs={{0,8},{8,0},{1,9},{9,1},{2,10},{10,2},{3,11},{11,3},{4,12},{12,4},... | collective-permute-start | bytes 1179656 | tf_op jit(solution)/shard_map/ppermute | solution.py:35
  62.6 0.0 collective-permute-done.15.refs_3_
  62.6 1.6 %flash.14 = (f32[384,512]{1,0:T(8,128)S(1)}, f32[24,512]{1,0:T(8,128)S(1)}) custom-call(bf16[256,384]{1,0:T(8,128)(2,1)S(1)} %bitcast.18, bf16[256,384]{1,0:T(8,128)(2,1)S(1)} %collective-permute-done.1.refs_1_, bf16[512,384]{1,0:T(8,128)(2,1)S(1)} %collective-permute-done.9.refs_2_, bf16[512,384]{1,0:T(8,128)(2,1)S(1)} %collective-permute-done.15.refs_3_, ...), custom_call_target="tpu_custom_call" | custom-call | flops 2177600000 | bytes 6532800 | tf_op jit(solution)/shard_map/flash/pallas_call | solution.py:167
  64.2 0.0 collective-permute-done.5.refs_3_
  64.2 1.7 %flash.15 = bf16[512,512]{1,0:T(8,128)(2,1)S(1)} custom-call(bf16[256,384]{1,0:T(8,128)(2,1)S(1)} %bitcast.19, bf16[256,384]{1,0:T(8,128)(2,1)S(1)} %collective-permute-done.1.refs_1_, bf16[512,384]{1,0:T(8,128)(2,1)S(1)} %collective-permute-done.4.refs_2_, bf16[512,384]{1,0:T(8,128)(2,1)S(1)} %collective-permute-done.5.refs_3_, ...), custom_call_target="tpu_custom_call" | custom-call | flops 2177600000 | bytes 6532800 | tf_op jit(solution)/shard_map/flash/pallas_call | solution.py:167
  65.9 12.9 %all_to_all.17 = bf16[16,32,512]{2,1,0:T(8,128)(2,1)S(1)} all-to-all(bf16[16,32,512]{2,1,0:T(8,128)(2,1)S(1)} %bitcast.6), channel_id=1, replica_groups=mesh['yl'=2,'z'=8,'core'=2,'yh'=2,'xh'=2,'xl'=2] {'yl','yh','xl','xh'}, dimensions={0} | all-to-all | bytes 1048576 | tf_op jit(solution)/shard_map/all_to_all | solution.py:238
  78.8 1.1 %merge.1 = bf16[32,3072]{1,0:T(8,128)(2,1)} custom-call(bf16[512,512]{1,0:T(8,128)(2,1)S(1)} %bitcast.7), custom_call_target="tpu_custom_call" | custom-call | flops 2000000000 | bytes 6000000 | tf_op jit(solution)/shard_map/merge/pallas_call | solution.py:201
  (2 shorter events, 0.1 us)
Async XLA Ops:
  21.6 8.3 %collective-permute-start.6 = (bf16[512,384]{1,0:T(8,128)(2,1)S(1)}, bf16[512,384]{1,0:T(8,128)(2,1)S(1)}, u32[]{:S(2)}, u32[]{:S(2)}) collective-permute-start(bf16[512,384]{1,0:T(8,128)(2,1)S(1)} %bitcast.8), channel_id=1, source_target_pairs={{0,8},{8,0},{1,9},{9,1},{2,10},{10,2},{3,11},{11,3},{4,12},{12,4},... | collective-permute-start | bytes 1179656 | tf_op jit(solution)/shard_map/ppermute | solution.py:35
  24.0 10.5 %collective-permute-start = (bf16[512,384]{1,0:T(8,128)(2,1)S(1)}, bf16[512,384]{1,0:T(8,128)(2,1)S(1)}, u32[]{:S(2)}, u32[]{:S(2)}) collective-permute-start(bf16[512,384]{1,0:T(8,128)(2,1)S(1)} %bitcast.9), channel_id=1, source_target_pairs={{0,16},{8,120},{16,32},{24,8},{32,48},{40,24},{48,64},{56,40},{64,... | collective-permute-start | bytes 1179656 | tf_op jit(solution)/shard_map/ppermute | solution.py:31
  29.6 4.9 %collective-permute-start.1 = (bf16[256,384]{1,0:T(8,128)(2,1)S(1)}, bf16[256,384]{1,0:T(8,128)(2,1)S(1)}, u32[]{:S(2)}, u32[]{:S(2)}) collective-permute-start(bf16[256,384]{1,0:T(8,128)(2,1)S(1)} %bitcast.11), channel_id=1, source_target_pairs={{0,1},{1,0},{2,3},{3,2},{4,5},{5,4},{6,7},{7,6},{8,9},{9,8},{10,11... | collective-permute-start | bytes 589832 | tf_op jit(solution)/shard_map/ppermute | solution.py:35
  30.0 8.9 %collective-permute-start.7 = (bf16[512,384]{1,0:T(8,128)(2,1)S(1)}, bf16[512,384]{1,0:T(8,128)(2,1)S(1)}, u32[]{:S(2)}, u32[]{:S(2)}) collective-permute-start(bf16[512,384]{1,0:T(8,128)(2,1)S(1)} %collective-permute-done.6.refs_3_), channel_id=1, source_target_pairs={{0,16},{8,120},{16,32},{24,8},{32,48},{40,24},{48,64},{56,40},{64,... | collective-permute-start | bytes 1179656 | tf_op jit(solution)/shard_map/ppermute | solution.py:31
  34.5 8.2 %collective-permute-start.2 = (bf16[512,384]{1,0:T(8,128)(2,1)S(1)}, bf16[512,384]{1,0:T(8,128)(2,1)S(1)}, u32[]{:S(2)}, u32[]{:S(2)}) collective-permute-start(bf16[512,384]{1,0:T(8,128)(2,1)S(1)} %collective-permute-done.refs_2_), channel_id=1, source_target_pairs={{0,16},{8,120},{16,32},{24,8},{32,48},{40,24},{48,64},{56,40},{64,... | collective-permute-start | bytes 1179656 | tf_op jit(solution)/shard_map/ppermute | solution.py:31
  37.4 8.9 %collective-permute-start.14 = (bf16[512,384]{1,0:T(8,128)(2,1)S(1)}, bf16[512,384]{1,0:T(8,128)(2,1)S(1)}, u32[]{:S(2)}, u32[]{:S(2)}) collective-permute-start(bf16[512,384]{1,0:T(8,128)(2,1)S(1)} %collective-permute-done.refs_2_), channel_id=1, source_target_pairs={{0,8},{8,0},{1,9},{9,1},{2,10},{10,2},{3,11},{11,3},{4,12},{12,4},... | collective-permute-start | bytes 1179656 | tf_op jit(solution)/shard_map/ppermute | solution.py:35
  38.9 9.0 %collective-permute-start.8 = (bf16[512,384]{1,0:T(8,128)(2,1)S(1)}, bf16[512,384]{1,0:T(8,128)(2,1)S(1)}, u32[]{:S(2)}, u32[]{:S(2)}) collective-permute-start(bf16[512,384]{1,0:T(8,128)(2,1)S(1)} %collective-permute-done.7.refs_2_), channel_id=1, source_target_pairs={{0,16},{8,120},{16,32},{24,8},{32,48},{40,24},{48,64},{56,40},{64,... | collective-permute-start | bytes 1179656 | tf_op jit(solution)/shard_map/ppermute | solution.py:31
  42.7 8.4 %collective-permute-start.3 = (bf16[512,384]{1,0:T(8,128)(2,1)S(1)}, bf16[512,384]{1,0:T(8,128)(2,1)S(1)}, u32[]{:S(2)}, u32[]{:S(2)}) collective-permute-start(bf16[512,384]{1,0:T(8,128)(2,1)S(1)} %collective-permute-done.2.refs_2_), channel_id=1, source_target_pairs={{0,16},{8,120},{16,32},{24,8},{32,48},{40,24},{48,64},{56,40},{64,... | collective-permute-start | bytes 1179656 | tf_op jit(solution)/shard_map/ppermute | solution.py:31
  45.8 7.8 %collective-permute-start.13 = (bf16[512,384]{1,0:T(8,128)(2,1)S(1)}, bf16[512,384]{1,0:T(8,128)(2,1)S(1)}, u32[]{:S(2)}, u32[]{:S(2)}) collective-permute-start(bf16[512,384]{1,0:T(8,128)(2,1)S(1)} %collective-permute-done.7.refs_2_), channel_id=1, source_target_pairs={{0,8},{8,0},{1,9},{9,1},{2,10},{10,2},{3,11},{11,3},{4,12},{12,4},... | collective-permute-start | bytes 1179656 | tf_op jit(solution)/shard_map/ppermute | solution.py:35
  45.8 10.0 %collective-permute-start.12 = (bf16[512,384]{1,0:T(8,128)(2,1)S(1)}, bf16[512,384]{1,0:T(8,128)(2,1)S(1)}, u32[]{:S(2)}, u32[]{:S(2)}) collective-permute-start(bf16[512,384]{1,0:T(8,128)(2,1)S(1)} %collective-permute-done.2.refs_2_), channel_id=1, source_target_pairs={{0,8},{8,0},{1,9},{9,1},{2,10},{10,2},{3,11},{11,3},{4,12},{12,4},... | collective-permute-start | bytes 1179656 | tf_op jit(solution)/shard_map/ppermute | solution.py:35
  47.9 9.5 %collective-permute-start.11 = (bf16[512,384]{1,0:T(8,128)(2,1)S(1)}, bf16[512,384]{1,0:T(8,128)(2,1)S(1)}, u32[]{:S(2)}, u32[]{:S(2)}) collective-permute-start(bf16[512,384]{1,0:T(8,128)(2,1)S(1)} %collective-permute-done.8.refs_2_), channel_id=1, source_target_pairs={{0,8},{8,0},{1,9},{9,1},{2,10},{10,2},{3,11},{11,3},{4,12},{12,4},... | collective-permute-start | bytes 1179656 | tf_op jit(solution)/shard_map/ppermute | solution.py:35
  48.9 11.7 %collective-permute-start.9 = (bf16[512,384]{1,0:T(8,128)(2,1)S(1)}, bf16[512,384]{1,0:T(8,128)(2,1)S(1)}, u32[]{:S(2)}, u32[]{:S(2)}) collective-permute-start(bf16[512,384]{1,0:T(8,128)(2,1)S(1)} %collective-permute-done.8.refs_2_), channel_id=1, source_target_pairs={{0,16},{8,120},{16,32},{24,8},{32,48},{40,24},{48,64},{56,40},{64,... | collective-permute-start | bytes 1179656 | tf_op jit(solution)/shard_map/ppermute | solution.py:31
  51.1 7.9 %collective-permute-start.10 = (bf16[512,384]{1,0:T(8,128)(2,1)S(1)}, bf16[512,384]{1,0:T(8,128)(2,1)S(1)}, u32[]{:S(2)}, u32[]{:S(2)}) collective-permute-start(bf16[512,384]{1,0:T(8,128)(2,1)S(1)} %collective-permute-done.3.refs_2_), channel_id=1, source_target_pairs={{0,8},{8,0},{1,9},{9,1},{2,10},{10,2},{3,11},{11,3},{4,12},{12,4},... | collective-permute-start | bytes 1179656 | tf_op jit(solution)/shard_map/ppermute | solution.py:35
  53.6 7.0 %collective-permute-start.4 = (bf16[512,384]{1,0:T(8,128)(2,1)S(1)}, bf16[512,384]{1,0:T(8,128)(2,1)S(1)}, u32[]{:S(2)}, u32[]{:S(2)}) collective-permute-start(bf16[512,384]{1,0:T(8,128)(2,1)S(1)} %collective-permute-done.3.refs_2_), channel_id=1, source_target_pairs={{0,16},{8,120},{16,32},{24,8},{32,48},{40,24},{48,64},{56,40},{64,... | collective-permute-start | bytes 1179656 | tf_op jit(solution)/shard_map/ppermute | solution.py:31
  60.6 2.1 %collective-permute-start.15 = (bf16[512,384]{1,0:T(8,128)(2,1)S(1)}, bf16[512,384]{1,0:T(8,128)(2,1)S(1)}, u32[]{:S(2)}, u32[]{:S(2)}) collective-permute-start(bf16[512,384]{1,0:T(8,128)(2,1)S(1)} %collective-permute-done.9.refs_2_), channel_id=1, source_target_pairs={{0,8},{8,0},{1,9},{9,1},{2,10},{10,2},{3,11},{11,3},{4,12},{12,4},... | collective-permute-start | bytes 1179656 | tf_op jit(solution)/shard_map/ppermute | solution.py:35
  60.7 3.5 %collective-permute-start.5 = (bf16[512,384]{1,0:T(8,128)(2,1)S(1)}, bf16[512,384]{1,0:T(8,128)(2,1)S(1)}, u32[]{:S(2)}, u32[]{:S(2)}) collective-permute-start(bf16[512,384]{1,0:T(8,128)(2,1)S(1)} %collective-permute-done.4.refs_2_), channel_id=1, source_target_pairs={{0,8},{8,0},{1,9},{9,1},{2,10},{10,2},{3,11},{11,3},{4,12},{12,4},... | collective-permute-start | bytes 1179656 | tf_op jit(solution)/shard_map/ppermute | solution.py:35

commit v5 on v4

--- a/solution.py
+++ b/solution.py
@@ -42,9 +42,10 @@
     )
 
 
-def mix_kernel(step_ref, q_hbm, ke_hbm, ve_hbm, ks_hbm, vs_hbm, mask_hbm, gate_hbm, out, *refs):
+def mix_kernel(step_ref, q_hbm, ke_hbm, ve_hbm, ks_hbm, vs_hbm, mask_hbm, gate_hbm, out_hbm, *refs):
     sources = (mask_hbm, gate_hbm, ke_hbm, ks_hbm, ve_hbm, vs_hbm, q_hbm)
-    scratch, gates, sem = refs[:-2], refs[-2], refs[-1]
+    scratch, gates, out, sem, out_sem = refs[:-4], refs[-4], refs[-3], refs[-2], refs[-1]
+    sends = []
     copies = [pltpu.make_async_copy(a, b, sem.at[i]) for i, (a, b) in enumerate(zip(sources, scratch))]
     for copy in copies:
         copy.start()
@@ -71,9 +72,17 @@
             mixed = jnp.where(inside, e, s + strength * (e - s)).astype(BF16)
             group, h = divmod(head, HEADS)
             out[group, n * TOK : (n + 1) * TOK, h * HEAD : (h + 1) * HEAD] = mixed
+        rows = pl.ds(n * TOK, TOK)
+        sends.append(pltpu.make_async_copy(out.at[:, rows, :], out_hbm.at[:, rows, :], out_sem.at[n]))
+        sends[-1].start()
     copies[6].wait()
     for group in range(GROUPS):
         out[group, 2 * TOK :, :] = q_ref[:, group * WIDTH : (group + 1) * WIDTH]
+    rows = pl.ds(2 * TOK, TOK)
+    sends.append(pltpu.make_async_copy(out.at[:, rows, :], out_hbm.at[:, rows, :], out_sem.at[2]))
+    sends[-1].start()
+    for send in sends:
+        send.wait()
 
 
 def mix(step_index, queries, ke, ve, ks, vs, edit_mask, gate):
@@ -84,11 +93,12 @@
         mix_kernel,
         out_shape=jax.ShapeDtypeStruct((GROUPS, 3 * TOK, WIDTH), BF16),
         in_specs=[IN_SMEM] + [pl.BlockSpec(memory_space=pltpu.HBM)] * 7,
-        out_specs=IN_VMEM,
+        out_specs=pl.BlockSpec(memory_space=pltpu.HBM),
         scratch_shapes=[pltpu.VMEM(edit_mask.shape, jnp.int32), pltpu.VMEM(gate.shape, F32)]
         + [big] * 5
         + [pltpu.VMEM((gate.shape[0], HEAD), F32)]
-        + [pltpu.SemaphoreType.DMA((7,))],
+        + [pltpu.VMEM((GROUPS, 3 * TOK, WIDTH), BF16)]
+        + [pltpu.SemaphoreType.DMA((7,)), pltpu.SemaphoreType.DMA((3,))],
         name="mix",
         **options(2, 60 * 1024 * 1024),
     )(step_index, queries, ke, ve, ks, vs, edit_mask, gate)

time: 80.1 us -> 80.1 us (level)
  no operation moved by 1% of the time
where the time goes in v5:
time: 80.1 us; the launch traced here: 79.8 us
  blocking collectives  31.5 us (39%)
  starting transfers between devices  25.8 us (32%)
  Pallas kernels  15.9 us (20%)
  waiting for transfers between devices  5.77 us (7%)
    all_to_all x1, blocking collectives, on_device(): got = lax.all_to_all(mixed, GROUP_AXES, 0, 0, tiled=True)  18.7 us
    ppermute x7, starting transfers between devices, ring_z(): return lax.ppermute(value, ('z', 'core'), pairs)  17 us
    all_to_all x1, blocking collectives, on_device(): parts = lax.all_to_all(parts, OUT_AXES, 0, 0, tiled=True)  12.8 us
    pallas_call x8, Pallas kernels, flash(): pl.pallas_call(functools.partial(flash_kernel, first, last, len(kv_blocks...  12.5 us
    ppermute x9, starting transfers between devices, swap(): return lax.ppermute(value, axis, [(0, 1), (1, 0)])  8.82 us
    ppermute x9, waiting for transfers between devices, swap(): return lax.ppermute(value, axis, [(0, 1), (1, 0)])  3.6 us
    pallas_call x1, Pallas kernels, mix(): pl.pallas_call(mix_kernel, out_shape=jax.ShapeDtypeStruct((GROUPS, 3 * TO...  2.21 us
    ppermute x7, waiting for transfers between devices, ring_z(): return lax.ppermute(value, ('z', 'core'), pairs)  2.18 us
  transfers between devices with their start and end apart: 16, of which 3 were waited for; matrix products, arithmetic and copies ran while one was open for 0% of the time, Pallas kernels for 14%

profile of v5, /device:TPU:1, one launch (start us, length us, event | category | flops | bytes accessed | tf_op | source)
XLA Modules:
  0.0 79.8 jit_solution(7308713932247207419)
XLA Ops:
  0.7 2.2 %mix.1 = bf16[8,96,384]{2,1,0:T(8,128)(2,1)} custom-call(s32[1]{0:T(128)S(6)} %copy.9.step_ref, bf16[32,3072]{1,0:T(8,128)(2,1)} %q_hbm.1, bf16[32,3072]{1,0:T(8,128)(2,1)} %ke_hbm.1, bf16[32,3072]{1,0:T(8,128)(2,1)} %ve_hbm.1, bf16[32,3072]{1,0:T(8,128)(2,1)} %ks_hbm.1, bf16[32,3072]{1,0:T(8,128)(2,1)} %vs_hbm.1, s32[1,256]{1,0:T(1,128)} %bitcast.21, ...), custom_call_target="tpu_custom_call" | custom-call | flops 2000000000 | bytes 6000000 | tf_op jit(solution)/shard_map/mix/pallas_call | solution.py:92
  2.9 18.7 %all_to_all.16 = bf16[8,96,384]{2,1,0:T(8,128)(2,1)S(1)} all-to-all(bf16[8,96,384]{2,1,0:T(8,128)(2,1)} %mix.1), channel_id=1, replica_groups=mesh['yl'=2,'z'=8,'core'=2,'yh'=2,'xh'=2,'xl'=2] {'yl','yh','xh'}, dimensions={0} | all-to-all | bytes 1179648 | tf_op jit(solution)/shard_map/all_to_all | solution.py:227
  21.6 2.3 %collective-permute-start.6 = (bf16[512,384]{1,0:T(8,128)(2,1)S(1)}, bf16[512,384]{1,0:T(8,128)(2,1)S(1)}, u32[]{:S(2)}, u32[]{:S(2)}) collective-permute-start(bf16[512,384]{1,0:T(8,128)(2,1)S(1)} %bitcast.8), channel_id=1, source_target_pairs={{0,8},{8,0},{1,9},{9,1},{2,10},{10,2},{3,11},{11,3},{4,12},{12,4},... | collective-permute-start | bytes 1179656 | tf_op jit(solution)/shard_map/ppermute | solution.py:35
  23.9 5.6 %collective-permute-start = (bf16[512,384]{1,0:T(8,128)(2,1)S(1)}, bf16[512,384]{1,0:T(8,128)(2,1)S(1)}, u32[]{:S(2)}, u32[]{:S(2)}) collective-permute-start(bf16[512,384]{1,0:T(8,128)(2,1)S(1)} %bitcast.9), channel_id=1, source_target_pairs={{0,16},{8,120},{16,32},{24,8},{32,48},{40,24},{48,64},{56,40},{64,... | collective-permute-start | bytes 1179656 | tf_op jit(solution)/shard_map/ppermute | solution.py:31
  29.5 0.4 collective-permute-start.1
  29.9 0.0 collective-permute-done.6.refs_3_
  29.9 0.9 %collective-permute-start.7 = (bf16[512,384]{1,0:T(8,128)(2,1)S(1)}, bf16[512,384]{1,0:T(8,128)(2,1)S(1)}, u32[]{:S(2)}, u32[]{:S(2)}) collective-permute-start(bf16[512,384]{1,0:T(8,128)(2,1)S(1)} %collective-permute-done.6.refs_3_), channel_id=1, source_target_pairs={{0,16},{8,120},{16,32},{24,8},{32,48},{40,24},{48,64},{56,40},{64,... | collective-permute-start | bytes 1179656 | tf_op jit(solution)/shard_map/ppermute | solution.py:31
  30.9 3.6 %collective-permute-done.1.refs_1_ = bf16[256,384]{1,0:T(8,128)(2,1)S(1)} collective-permute-done((bf16[256,384]{1,0:T(8,128)(2,1)S(1)}, bf16[256,384]{1,0:T(8,128)(2,1)S(1)}, u32[]{:S(2)}, u32[]{:S(2)}) %collective-permute-start.1) | collective-permute-done | bytes 196640 | tf_op jit(solution)/shard_map/ppermute | solution.py:35
  34.4 0.0 collective-permute-done.refs_2_
  34.4 2.9 %collective-permute-start.2 = (bf16[512,384]{1,0:T(8,128)(2,1)S(1)}, bf16[512,384]{1,0:T(8,128)(2,1)S(1)}, u32[]{:S(2)}, u32[]{:S(2)}) collective-permute-start(bf16[512,384]{1,0:T(8,128)(2,1)S(1)} %collective-permute-done.refs_2_), channel_id=1, source_target_pairs={{0,16},{8,120},{16,32},{24,8},{32,48},{40,24},{48,64},{56,40},{64,... | collective-permute-start | bytes 1179656 | tf_op jit(solution)/shard_map/ppermute | solution.py:31
  37.4 0.0 collective-permute-start.14
  37.4 1.5 %flash.8 = (f32[384,512]{1,0:T(8,128)S(1)}, f32[24,512]{1,0:T(8,128)S(1)}) custom-call(bf16[256,384]{1,0:T(8,128)(2,1)S(1)} %bitcast.12, bf16[256,384]{1,0:T(8,128)(2,1)S(1)} %collective-permute-done.1.refs_1_, bf16[512,384]{1,0:T(8,128)(2,1)S(1)} %bitcast.10, bf16[512,384]{1,0:T(8,128)(2,1)S(1)} %collective-permute-done.6.refs_3_), custom_call_target="tpu_custom_call" | custom-call | flops 2177600000 | bytes 6532800 | tf_op jit(solution)/shard_map/flash/pallas_call | solution.py:177
  38.9 0.0 collective-permute-done.7.refs_2_
  38.9 2.7 %collective-permute-start.8 = (bf16[512,384]{1,0:T(8,128)(2,1)S(1)}, bf16[512,384]{1,0:T(8,128)(2,1)S(1)}, u32[]{:S(2)}, u32[]{:S(2)}) collective-permute-start(bf16[512,384]{1,0:T(8,128)(2,1)S(1)} %collective-permute-done.7.refs_2_), channel_id=1, source_target_pairs={{0,16},{8,120},{16,32},{24,8},{32,48},{40,24},{48,64},{56,40},{64,... | collective-permute-start | bytes 1179656 | tf_op jit(solution)/shard_map/ppermute | solution.py:31
  41.6 1.1 %collective-permute-done.2.refs_2_ = bf16[512,384]{1,0:T(8,128)(2,1)S(1)} collective-permute-done((bf16[512,384]{1,0:T(8,128)(2,1)S(1)}, bf16[512,384]{1,0:T(8,128)(2,1)S(1)}, u32[]{:S(2)}, u32[]{:S(2)}) %collective-permute-start.2) | collective-permute-done | bytes 393248 | tf_op jit(solution)/shard_map/ppermute | solution.py:31
  42.7 3.1 %collective-permute-start.3 = (bf16[512,384]{1,0:T(8,128)(2,1)S(1)}, bf16[512,384]{1,0:T(8,128)(2,1)S(1)}, u32[]{:S(2)}, u32[]{:S(2)}) collective-permute-start(bf16[512,384]{1,0:T(8,128)(2,1)S(1)} %collective-permute-done.2.refs_2_), channel_id=1, source_target_pairs={{0,16},{8,120},{16,32},{24,8},{32,48},{40,24},{48,64},{56,40},{64,... | collective-permute-start | bytes 1179656 | tf_op jit(solution)/shard_map/ppermute | solution.py:31
  45.8 0.0 collective-permute-start.13
  45.8 0.5 collective-permute-start.12
  46.3 0.0 collective-permute-done.14.refs_3_
  46.3 1.6 %flash.9 = (f32[384,512]{1,0:T(8,128)S(1)}, f32[24,512]{1,0:T(8,128)S(1)}) custom-call(bf16[256,384]{1,0:T(8,128)(2,1)S(1)} %bitcast.13, bf16[256,384]{1,0:T(8,128)(2,1)S(1)} %collective-permute-done.1.refs_1_, bf16[512,384]{1,0:T(8,128)(2,1)S(1)} %collective-permute-done.refs_2_, bf16[512,384]{1,0:T(8,128)(2,1)S(1)} %collective-permute-done.14.refs_3_, ...), custom_call_target="tpu_custom_call" | custom-call | flops 2177600000 | bytes 6532800 | tf_op jit(solution)/shard_map/flash/pallas_call | solution.py:177
  47.9 0.0 collective-permute-done.8.refs_2_
  47.9 1.0 %collective-permute-start.11 = (bf16[512,384]{1,0:T(8,128)(2,1)S(1)}, bf16[512,384]{1,0:T(8,128)(2,1)S(1)}, u32[]{:S(2)}, u32[]{:S(2)}) collective-permute-start(bf16[512,384]{1,0:T(8,128)(2,1)S(1)} %collective-permute-done.8.refs_2_), channel_id=1, source_target_pairs={{0,8},{8,0},{1,9},{9,1},{2,10},{10,2},{3,11},{11,3},{4,12},{12,4},... | collective-permute-start | bytes 1179656 | tf_op jit(solution)/shard_map/ppermute | solution.py:35
  48.8 1.2 %collective-permute-start.9 = (bf16[512,384]{1,0:T(8,128)(2,1)S(1)}, bf16[512,384]{1,0:T(8,128)(2,1)S(1)}, u32[]{:S(2)}, u32[]{:S(2)}) collective-permute-start(bf16[512,384]{1,0:T(8,128)(2,1)S(1)} %collective-permute-done.8.refs_2_), channel_id=1, source_target_pairs={{0,16},{8,120},{16,32},{24,8},{32,48},{40,24},{48,64},{56,40},{64,... | collective-permute-start | bytes 1179656 | tf_op jit(solution)/shard_map/ppermute | solution.py:31
  50.0 1.1 %collective-permute-done.3.refs_2_ = bf16[512,384]{1,0:T(8,128)(2,1)S(1)} collective-permute-done((bf16[512,384]{1,0:T(8,128)(2,1)S(1)}, bf16[512,384]{1,0:T(8,128)(2,1)S(1)}, u32[]{:S(2)}, u32[]{:S(2)}) %collective-permute-start.3) | collective-permute-done | bytes 393248 | tf_op jit(solution)/shard_map/ppermute | solution.py:31
  51.1 2.5 %collective-permute-start.10 = (bf16[512,384]{1,0:T(8,128)(2,1)S(1)}, bf16[512,384]{1,0:T(8,128)(2,1)S(1)}, u32[]{:S(2)}, u32[]{:S(2)}) collective-permute-start(bf16[512,384]{1,0:T(8,128)(2,1)S(1)} %collective-permute-done.3.refs_2_), channel_id=1, source_target_pairs={{0,8},{8,0},{1,9},{9,1},{2,10},{10,2},{3,11},{11,3},{4,12},{12,4},... | collective-permute-start | bytes 1179656 | tf_op jit(solution)/shard_map/ppermute | solution.py:35
  53.6 0.0 collective-permute-done.13.refs_3_
  53.6 0.6 collective-permute-start.4
  54.2 1.6 %flash.10 = (f32[384,512]{1,0:T(8,128)S(1)}, f32[24,512]{1,0:T(8,128)S(1)}) custom-call(bf16[256,384]{1,0:T(8,128)(2,1)S(1)} %bitcast.14, bf16[256,384]{1,0:T(8,128)(2,1)S(1)} %collective-permute-done.1.refs_1_, bf16[512,384]{1,0:T(8,128)(2,1)S(1)} %collective-permute-done.7.refs_2_, bf16[512,384]{1,0:T(8,128)(2,1)S(1)} %collective-permute-done.13.refs_3_, ...), custom_call_target="tpu_custom_call" | custom-call | flops 2177600000 | bytes 6532800 | tf_op jit(solution)/shard_map/flash/pallas_call | solution.py:177
  55.8 0.0 collective-permute-done.12.refs_3_
  55.8 1.6 %flash.11 = (f32[384,512]{1,0:T(8,128)S(1)}, f32[24,512]{1,0:T(8,128)S(1)}) custom-call(bf16[256,384]{1,0:T(8,128)(2,1)S(1)} %bitcast.15, bf16[256,384]{1,0:T(8,128)(2,1)S(1)} %collective-permute-done.1.refs_1_, bf16[512,384]{1,0:T(8,128)(2,1)S(1)} %collective-permute-done.2.refs_2_, bf16[512,384]{1,0:T(8,128)(2,1)S(1)} %collective-permute-done.12.refs_3_, ...), custom_call_target="tpu_custom_call" | custom-call | flops 2177600000 | bytes 6532800 | tf_op jit(solution)/shard_map/flash/pallas_call | solution.py:177
  57.4 0.0 collective-permute-done.11.refs_3_
  57.4 1.6 %flash.12 = (f32[384,512]{1,0:T(8,128)S(1)}, f32[24,512]{1,0:T(8,128)S(1)}) custom-call(bf16[256,384]{1,0:T(8,128)(2,1)S(1)} %bitcast.16, bf16[256,384]{1,0:T(8,128)(2,1)S(1)} %collective-permute-done.1.refs_1_, bf16[512,384]{1,0:T(8,128)(2,1)S(1)} %collective-permute-done.8.refs_2_, bf16[512,384]{1,0:T(8,128)(2,1)S(1)} %collective-permute-done.11.refs_3_, ...), custom_call_target="tpu_custom_call" | custom-call | flops 2177600000 | bytes 6532800 | tf_op jit(solution)/shard_map/flash/pallas_call | solution.py:177
  58.9 0.0 collective-permute-done.10.refs_3_
  59.0 1.6 %flash.13 = (f32[384,512]{1,0:T(8,128)S(1)}, f32[24,512]{1,0:T(8,128)S(1)}) custom-call(bf16[256,384]{1,0:T(8,128)(2,1)S(1)} %bitcast.17, bf16[256,384]{1,0:T(8,128)(2,1)S(1)} %collective-permute-done.1.refs_1_, bf16[512,384]{1,0:T(8,128)(2,1)S(1)} %collective-permute-done.3.refs_2_, bf16[512,384]{1,0:T(8,128)(2,1)S(1)} %collective-permute-done.10.refs_3_, ...), custom_call_target="tpu_custom_call" | custom-call | flops 2177600000 | bytes 6532800 | tf_op jit(solution)/shard_map/flash/pallas_call | solution.py:177
  60.5 0.0 collective-permute-done.9.refs_2_
  60.5 0.1 collective-permute-start.15
  60.6 0.0 collective-permute-done.4.refs_2_
  60.6 2.0 %collective-permute-start.5 = (bf16[512,384]{1,0:T(8,128)(2,1)S(1)}, bf16[512,384]{1,0:T(8,128)(2,1)S(1)}, u32[]{:S(2)}, u32[]{:S(2)}) collective-permute-start(bf16[512,384]{1,0:T(8,128)(2,1)S(1)} %collective-permute-done.4.refs_2_), channel_id=1, source_target_pairs={{0,8},{8,0},{1,9},{9,1},{2,10},{10,2},{3,11},{11,3},{4,12},{12,4},... | collective-permute-start | bytes 1179656 | tf_op jit(solution)/shard_map/ppermute | solution.py:35
  62.6 0.0 collective-permute-done.15.refs_3_
  62.6 1.6 %flash.14 = (f32[384,512]{1,0:T(8,128)S(1)}, f32[24,512]{1,0:T(8,128)S(1)}) custom-call(bf16[256,384]{1,0:T(8,128)(2,1)S(1)} %bitcast.18, bf16[256,384]{1,0:T(8,128)(2,1)S(1)} %collective-permute-done.1.refs_1_, bf16[512,384]{1,0:T(8,128)(2,1)S(1)} %collective-permute-done.9.refs_2_, bf16[512,384]{1,0:T(8,128)(2,1)S(1)} %collective-permute-done.15.refs_3_, ...), custom_call_target="tpu_custom_call" | custom-call | flops 2177600000 | bytes 6532800 | tf_op jit(solution)/shard_map/flash/pallas_call | solution.py:177
  64.2 0.0 collective-permute-done.5.refs_3_
  64.2 1.7 %flash.15 = bf16[512,512]{1,0:T(8,128)(2,1)S(1)} custom-call(bf16[256,384]{1,0:T(8,128)(2,1)S(1)} %bitcast.19, bf16[256,384]{1,0:T(8,128)(2,1)S(1)} %collective-permute-done.1.refs_1_, bf16[512,384]{1,0:T(8,128)(2,1)S(1)} %collective-permute-done.4.refs_2_, bf16[512,384]{1,0:T(8,128)(2,1)S(1)} %collective-permute-done.5.refs_3_, ...), custom_call_target="tpu_custom_call" | custom-call | flops 2177600000 | bytes 6532800 | tf_op jit(solution)/shard_map/flash/pallas_call | solution.py:177
  65.9 12.8 %all_to_all.17 = bf16[16,32,512]{2,1,0:T(8,128)(2,1)S(1)} all-to-all(bf16[16,32,512]{2,1,0:T(8,128)(2,1)S(1)} %bitcast.6), channel_id=1, replica_groups=mesh['yl'=2,'z'=8,'core'=2,'yh'=2,'xh'=2,'xl'=2] {'yl','yh','xl','xh'}, dimensions={0} | all-to-all | bytes 1048576 | tf_op jit(solution)/shard_map/all_to_all | solution.py:248
  78.7 1.1 %merge.1 = bf16[32,3072]{1,0:T(8,128)(2,1)} custom-call(bf16[512,512]{1,0:T(8,128)(2,1)S(1)} %bitcast.7), custom_call_target="tpu_custom_call" | custom-call | flops 2000000000 | bytes 6000000 | tf_op jit(solution)/shard_map/merge/pallas_call | solution.py:211
  (2 shorter events, 0.1 us)
Async XLA Ops:
  21.6 8.3 %collective-permute-start.6 = (bf16[512,384]{1,0:T(8,128)(2,1)S(1)}, bf16[512,384]{1,0:T(8,128)(2,1)S(1)}, u32[]{:S(2)}, u32[]{:S(2)}) collective-permute-start(bf16[512,384]{1,0:T(8,128)(2,1)S(1)} %bitcast.8), channel_id=1, source_target_pairs={{0,8},{8,0},{1,9},{9,1},{2,10},{10,2},{3,11},{11,3},{4,12},{12,4},... | collective-permute-start | bytes 1179656 | tf_op jit(solution)/shard_map/ppermute | solution.py:35
  23.9 10.5 %collective-permute-start = (bf16[512,384]{1,0:T(8,128)(2,1)S(1)}, bf16[512,384]{1,0:T(8,128)(2,1)S(1)}, u32[]{:S(2)}, u32[]{:S(2)}) collective-permute-start(bf16[512,384]{1,0:T(8,128)(2,1)S(1)} %bitcast.9), channel_id=1, source_target_pairs={{0,16},{8,120},{16,32},{24,8},{32,48},{40,24},{48,64},{56,40},{64,... | collective-permute-start | bytes 1179656 | tf_op jit(solution)/shard_map/ppermute | solution.py:31
  29.5 4.9 %collective-permute-start.1 = (bf16[256,384]{1,0:T(8,128)(2,1)S(1)}, bf16[256,384]{1,0:T(8,128)(2,1)S(1)}, u32[]{:S(2)}, u32[]{:S(2)}) collective-permute-start(bf16[256,384]{1,0:T(8,128)(2,1)S(1)} %bitcast.11), channel_id=1, source_target_pairs={{0,1},{1,0},{2,3},{3,2},{4,5},{5,4},{6,7},{7,6},{8,9},{9,8},{10,11... | collective-permute-start | bytes 589832 | tf_op jit(solution)/shard_map/ppermute | solution.py:35
  29.9 8.9 %collective-permute-start.7 = (bf16[512,384]{1,0:T(8,128)(2,1)S(1)}, bf16[512,384]{1,0:T(8,128)(2,1)S(1)}, u32[]{:S(2)}, u32[]{:S(2)}) collective-permute-start(bf16[512,384]{1,0:T(8,128)(2,1)S(1)} %collective-permute-done.6.refs_3_), channel_id=1, source_target_pairs={{0,16},{8,120},{16,32},{24,8},{32,48},{40,24},{48,64},{56,40},{64,... | collective-permute-start | bytes 1179656 | tf_op jit(solution)/shard_map/ppermute | solution.py:31
  34.4 8.2 %collective-permute-start.2 = (bf16[512,384]{1,0:T(8,128)(2,1)S(1)}, bf16[512,384]{1,0:T(8,128)(2,1)S(1)}, u32[]{:S(2)}, u32[]{:S(2)}) collective-permute-start(bf16[512,384]{1,0:T(8,128)(2,1)S(1)} %collective-permute-done.refs_2_), channel_id=1, source_target_pairs={{0,16},{8,120},{16,32},{24,8},{32,48},{40,24},{48,64},{56,40},{64,... | collective-permute-start | bytes 1179656 | tf_op jit(solution)/shard_map/ppermute | solution.py:31
  37.4 8.9 %collective-permute-start.14 = (bf16[512,384]{1,0:T(8,128)(2,1)S(1)}, bf16[512,384]{1,0:T(8,128)(2,1)S(1)}, u32[]{:S(2)}, u32[]{:S(2)}) collective-permute-start(bf16[512,384]{1,0:T(8,128)(2,1)S(1)} %collective-permute-done.refs_2_), channel_id=1, source_target_pairs={{0,8},{8,0},{1,9},{9,1},{2,10},{10,2},{3,11},{11,3},{4,12},{12,4},... | collective-permute-start | bytes 1179656 | tf_op jit(solution)/shard_map/ppermute | solution.py:35
  38.9 9.0 %collective-permute-start.8 = (bf16[512,384]{1,0:T(8,128)(2,1)S(1)}, bf16[512,384]{1,0:T(8,128)(2,1)S(1)}, u32[]{:S(2)}, u32[]{:S(2)}) collective-permute-start(bf16[512,384]{1,0:T(8,128)(2,1)S(1)} %collective-permute-done.7.refs_2_), channel_id=1, source_target_pairs={{0,16},{8,120},{16,32},{24,8},{32,48},{40,24},{48,64},{56,40},{64,... | collective-permute-start | bytes 1179656 | tf_op jit(solution)/shard_map/ppermute | solution.py:31
  42.7 8.4 %collective-permute-start.3 = (bf16[512,384]{1,0:T(8,128)(2,1)S(1)}, bf16[512,384]{1,0:T(8,128)(2,1)S(1)}, u32[]{:S(2)}, u32[]{:S(2)}) collective-permute-start(bf16[512,384]{1,0:T(8,128)(2,1)S(1)} %collective-permute-done.2.refs_2_), channel_id=1, source_target_pairs={{0,16},{8,120},{16,32},{24,8},{32,48},{40,24},{48,64},{56,40},{64,... | collective-permute-start | bytes 1179656 | tf_op jit(solution)/shard_map/ppermute | solution.py:31
  45.8 7.8 %collective-permute-start.13 = (bf16[512,384]{1,0:T(8,128)(2,1)S(1)}, bf16[512,384]{1,0:T(8,128)(2,1)S(1)}, u32[]{:S(2)}, u32[]{:S(2)}) collective-permute-start(bf16[512,384]{1,0:T(8,128)(2,1)S(1)} %collective-permute-done.7.refs_2_), channel_id=1, source_target_pairs={{0,8},{8,0},{1,9},{9,1},{2,10},{10,2},{3,11},{11,3},{4,12},{12,4},... | collective-permute-start | bytes 1179656 | tf_op jit(solution)/shard_map/ppermute | solution.py:35
  45.8 10.0 %collective-permute-start.12 = (bf16[512,384]{1,0:T(8,128)(2,1)S(1)}, bf16[512,384]{1,0:T(8,128)(2,1)S(1)}, u32[]{:S(2)}, u32[]{:S(2)}) collective-permute-start(bf16[512,384]{1,0:T(8,128)(2,1)S(1)} %collective-permute-done.2.refs_2_), channel_id=1, source_target_pairs={{0,8},{8,0},{1,9},{9,1},{2,10},{10,2},{3,11},{11,3},{4,12},{12,4},... | collective-permute-start | bytes 1179656 | tf_op jit(solution)/shard_map/ppermute | solution.py:35
  47.9 9.5 %collective-permute-start.11 = (bf16[512,384]{1,0:T(8,128)(2,1)S(1)}, bf16[512,384]{1,0:T(8,128)(2,1)S(1)}, u32[]{:S(2)}, u32[]{:S(2)}) collective-permute-start(bf16[512,384]{1,0:T(8,128)(2,1)S(1)} %collective-permute-done.8.refs_2_), channel_id=1, source_target_pairs={{0,8},{8,0},{1,9},{9,1},{2,10},{10,2},{3,11},{11,3},{4,12},{12,4},... | collective-permute-start | bytes 1179656 | tf_op jit(solution)/shard_map/ppermute | solution.py:35
  48.8 11.7 %collective-permute-start.9 = (bf16[512,384]{1,0:T(8,128)(2,1)S(1)}, bf16[512,384]{1,0:T(8,128)(2,1)S(1)}, u32[]{:S(2)}, u32[]{:S(2)}) collective-permute-start(bf16[512,384]{1,0:T(8,128)(2,1)S(1)} %collective-permute-done.8.refs_2_), channel_id=1, source_target_pairs={{0,16},{8,120},{16,32},{24,8},{32,48},{40,24},{48,64},{56,40},{64,... | collective-permute-start | bytes 1179656 | tf_op jit(solution)/shard_map/ppermute | solution.py:31
  51.1 7.9 %collective-permute-start.10 = (bf16[512,384]{1,0:T(8,128)(2,1)S(1)}, bf16[512,384]{1,0:T(8,128)(2,1)S(1)}, u32[]{:S(2)}, u32[]{:S(2)}) collective-permute-start(bf16[512,384]{1,0:T(8,128)(2,1)S(1)} %collective-permute-done.3.refs_2_), channel_id=1, source_target_pairs={{0,8},{8,0},{1,9},{9,1},{2,10},{10,2},{3,11},{11,3},{4,12},{12,4},... | collective-permute-start | bytes 1179656 | tf_op jit(solution)/shard_map/ppermute | solution.py:35
  53.6 7.0 %collective-permute-start.4 = (bf16[512,384]{1,0:T(8,128)(2,1)S(1)}, bf16[512,384]{1,0:T(8,128)(2,1)S(1)}, u32[]{:S(2)}, u32[]{:S(2)}) collective-permute-start(bf16[512,384]{1,0:T(8,128)(2,1)S(1)} %collective-permute-done.3.refs_2_), channel_id=1, source_target_pairs={{0,16},{8,120},{16,32},{24,8},{32,48},{40,24},{48,64},{56,40},{64,... | collective-permute-start | bytes 1179656 | tf_op jit(solution)/shard_map/ppermute | solution.py:31
  60.5 2.1 %collective-permute-start.15 = (bf16[512,384]{1,0:T(8,128)(2,1)S(1)}, bf16[512,384]{1,0:T(8,128)(2,1)S(1)}, u32[]{:S(2)}, u32[]{:S(2)}) collective-permute-start(bf16[512,384]{1,0:T(8,128)(2,1)S(1)} %collective-permute-done.9.refs_2_), channel_id=1, source_target_pairs={{0,8},{8,0},{1,9},{9,1},{2,10},{10,2},{3,11},{11,3},{4,12},{12,4},... | collective-permute-start | bytes 1179656 | tf_op jit(solution)/shard_map/ppermute | solution.py:35
  60.6 3.5 %collective-permute-start.5 = (bf16[512,384]{1,0:T(8,128)(2,1)S(1)}, bf16[512,384]{1,0:T(8,128)(2,1)S(1)}, u32[]{:S(2)}, u32[]{:S(2)}) collective-permute-start(bf16[512,384]{1,0:T(8,128)(2,1)S(1)} %collective-permute-done.4.refs_2_), channel_id=1, source_target_pairs={{0,8},{8,0},{1,9},{9,1},{2,10},{10,2},{3,11},{11,3},{4,12},{12,4},... | collective-permute-start | bytes 1179656 | tf_op jit(solution)/shard_map/ppermute | solution.py:35
